TPU v7x, 256 devices: a whole 4x4x8 slice. The times are simulated.
256 devices in a mesh: pts: 64 (over y, z, core), head: 4 (over x).
Axes of the slice: x: 4, y: 4, z: 8, core: 2. Of those that a mesh axis runs over, the one named last changes fastest.
Arguments:
- mesh_vertex_state: bfloat16 [524288, 256], P('pts'), may hold values from -6 to 6
- upstream_derivative: bfloat16 [524288, 256], P('pts'), may hold values from -6 to 6
- aggregate_mapping_matrix: bfloat16 [256, 256], P(None, 'head'), may hold values from -0.375 to 0.375
- partition_mapping_matrix: bfloat16 [256, 256], P(None, 'head'), may hold values from -0.375 to 0.375
- partition_score_matrix: bfloat16 [8, 32, 64], P('head'), may hold values from -1 to 1
- softmax_sharpness: float32 [8], P('head'), may hold values from 0.3 to 1
- query_key_value_maps: float32 [8, 3, 32, 32], P('head'), may hold values from -2 to 2
- final_mixing_matrix: bfloat16 [256, 256], P('head'), may hold values from -0.375 to 0.375
Outputs:
- input_grad: bfloat16 [524288, 256], P('pts', 'head')
- fx_weight_grad: float32 [256, 256], P(None, 'head')
- mid_weight_grad: float32 [256, 256], P(None, 'head')
- slice_weight_grad: float32 [8, 32, 64], P('head')
- attn_weight_grad: float32 [8, 3, 32, 32], P('head')
- out_weight_grad: float32 [256, 256], P('head')
All inputs are finite; a program needn't handle non-finite values.
Results may differ from a plain program's by a relative error of at most 0.015.
Values may be sent and summed in bfloat16 or wider, within the bound.
No kernel may reach another device: no remote copies, remote signals or barrier semaphores. Data moves between devices by JAX's collectives and lax.ppermute only.
A program may use at most 128 MiB of HBM per device.

v0:
```python
import math

import jax
import jax.numpy as jnp
from jax import lax
from jax.sharding import PartitionSpec as P

HIGH = lax.Precision.HIGHEST


def fein(form, left, right):
    return jnp.einsum(form, left, right, precision=HIGH, preferred_element_type=jnp.float32)


def batched_product(left, right):
    return jnp.dot(left, right, preferred_element_type=jnp.float32)


def block_diag(blocks, eyes):
    count, first, second = blocks.shape
    return fein("hab,hg->hagb", blocks, eyes).reshape(count * first, count * second)


def diag_blocks(full, eyes):
    count = eyes.shape[0]
    first = full.shape[0] // count
    second = full.shape[1] // count
    return fein("hagb,hg->hab", full.reshape(count, first, count, second), eyes)


def local_pass(
    pts_rows,
    cot_rows,
    both_proj,
    partition_score_matrix,
    softmax_sharpness,
    query_key_value_maps,
    final_mixing_matrix,
    scale,
    reduce_fn,
):
    local_heads, head_size, number_of_partitions = partition_score_matrix.shape
    inner = local_heads * head_size
    slice_cols = local_heads * number_of_partitions
    root = 1.0 / math.sqrt(head_size)
    eyes = jnp.eye(local_heads, dtype=jnp.float32)
    partition_segment = block_diag(partition_score_matrix.astype(jnp.float32), eyes).astype(
        jnp.bfloat16
    )
    group = jnp.einsum(
        "hg,mn->hmgn", eyes, jnp.ones((number_of_partitions, number_of_partitions), jnp.float32)
    ).reshape(slice_cols, slice_cols)
    sharpness_per_subspace = jnp.repeat(softmax_sharpness, number_of_partitions)
    projected = batched_product(pts_rows, both_proj).astype(jnp.bfloat16)
    feat = projected[:, :inner]
    partition_inputs = projected[:, inner:]
    partition_score = (
        batched_product(partition_inputs, partition_segment) / sharpness_per_subspace[None, :]
    )
    expo = jnp.exp(partition_score)
    parameter_tensors = expo / fein("pm,mn->pn", expo, group)
    weights_b = parameter_tensors.astype(jnp.bfloat16)
    pool_part = diag_blocks(batched_product(weights_b.T, feat), eyes)
    norm_part = jnp.sum(parameter_tensors, axis=0).reshape(local_heads, number_of_partitions)
    grad_desliced = batched_product(cot_rows, final_mixing_matrix.T).astype(jnp.bfloat16)
    grad_out_part = diag_blocks(batched_product(weights_b.T, grad_desliced), eyes)
    pool, norm, grad_slice_out = reduce_fn(pool_part, norm_part, grad_out_part)
    token = pool / norm[:, :, None]
    w_query = query_key_value_maps[:, 0]
    w_key = query_key_value_maps[:, 1]
    w_value = query_key_value_maps[:, 2]
    query = fein("hme,hef->hmf", token, w_query)
    keys_t = fein("hme,hef->hmf", token, w_key)
    values_t = fein("hme,hef->hmf", token, w_value)
    expo_s = jnp.exp(fein("hme,hne->hmn", query, keys_t) * root)
    prob = expo_s / jnp.sum(expo_s, axis=2, keepdims=True)
    slice_out = fein("hmn,hne->hme", prob, values_t)
    slice_out_b = slice_out.astype(jnp.bfloat16)
    out_block = block_diag(slice_out_b.astype(jnp.float32), eyes).astype(jnp.bfloat16)
    desliced = batched_product(weights_b, out_block).astype(jnp.bfloat16)
    out_local = scale * batched_product(desliced.T, cot_rows)
    grad_w1 = batched_product(grad_desliced, out_block.T)
    grad_prob = fein("hme,hne->hmn", grad_slice_out, values_t)
    grad_value = fein("hmn,hme->hne", prob, grad_slice_out)
    grad_score = prob * (grad_prob - jnp.sum(prob * grad_prob, axis=2, keepdims=True)) * root
    grad_query = fein("hmn,hne->hme", grad_score, keys_t)
    grad_key = fein("hmn,hme->hne", grad_score, query)
    attn_grad = jnp.stack(
        [
            fein("hme,hmf->hef", token, grad_query),
            fein("hme,hmf->hef", token, grad_key),
            fein("hme,hmf->hef", token, grad_value),
        ],
        axis=1,
    )
    grad_token = (
        fein("hmf,hef->hme", grad_query, w_query)
        + fein("hmf,hef->hme", grad_key, w_key)
        + fein("hmf,hef->hme", grad_value, w_value)
    )
    grad_pool = (grad_token / norm[:, :, None]).astype(jnp.bfloat16)
    pool_block = block_diag(grad_pool.astype(jnp.float32), eyes).astype(jnp.bfloat16)
    grad_norm = (-jnp.sum(grad_token * token, axis=2) / norm).reshape(slice_cols)
    parameter_derivative = grad_w1 + batched_product(feat, pool_block.T) + grad_norm[None, :]
    score_derivative = (
        parameter_tensors
        * (
            parameter_derivative
            - fein("pm,mn->pn", parameter_tensors * parameter_derivative, group)
        )
        / sharpness_per_subspace[None, :]
    )
    score_derivative = score_derivative.astype(jnp.bfloat16)
    grad_mid = batched_product(score_derivative, partition_segment.T).astype(jnp.bfloat16)
    grad_feat = batched_product(weights_b, pool_block).astype(jnp.bfloat16)
    slice_local = scale * diag_blocks(batched_product(partition_inputs.T, score_derivative), eyes)
    grad_both = jnp.concatenate([grad_feat, grad_mid], axis=1)
    proj_local = batched_product(pts_rows.T, grad_both)
    return (
        out_local,
        proj_local[:, :inner],
        scale * proj_local[:, inner:],
        slice_local,
        attn_grad,
        grad_both,
    )


def per_device(
    mesh_vertex_state,
    upstream_derivative,
    aggregate_mapping_matrix,
    partition_mapping_matrix,
    partition_score_matrix,
    softmax_sharpness,
    query_key_value_maps,
    final_mixing_matrix,
):
    rows = mesh_vertex_state.shape[0]
    scale = 1.0 / math.sqrt(rows * lax.axis_size("pts"))
    both_proj = jnp.concatenate([aggregate_mapping_matrix, partition_mapping_matrix], axis=1)

    def reduce_slices(pool_part, norm_part, grad_out_part):
        pool, norm = lax.psum((pool_part, norm_part), "pts")
        summed = lax.psum(grad_out_part, "pts")
        return (pool, norm, summed)

    out_local, fx_local, mid_local, slice_local, attn_grad, grad_both = local_pass(
        mesh_vertex_state,
        upstream_derivative,
        both_proj,
        partition_score_matrix,
        softmax_sharpness,
        query_key_value_maps,
        final_mixing_matrix,
        scale,
        reduce_slices,
    )
    out_grad = lax.psum(out_local, "pts")
    fx_grad, mid_grad, slice_grad = lax.psum((fx_local, mid_local, slice_local), "pts")
    partial_sum = batched_product(grad_both, both_proj.T)
    input_grad = lax.psum_scatter(
        partial_sum.astype(jnp.bfloat16), "head", scatter_dimension=1, tiled=True
    )
    return (input_grad, fx_grad, mid_grad, slice_grad, attn_grad, out_grad)


def solution(mesh):
    in_specs = (
        P("pts", None),
        P("pts", None),
        P(None, "head"),
        P(None, "head"),
        P("head", None, None),
        P("head"),
        P("head", None, None, None),
        P("head", None),
    )
    out_specs = (
        P("pts", "head"),
        P(None, "head"),
        P(None, "head"),
        P("head", None, None),
        P("head", None, None, None),
        P("head", None),
    )
    return jax.shard_map(
        per_device, mesh=mesh, in_specs=in_specs, out_specs=out_specs, check_vma=False
    )
```

profile of v0, /device:TPU:1, one launch (start us, length us, event | category | flops | bytes accessed | tf_op | source)
XLA Modules:
  0.0 571.8 jit_solution(12324847988146747681)
XLA Ops:
  8.2 0.7 broadcast_in_dim.2
  9.0 0.7 convert.24
  9.9 0.8 constant_dynamic-update-slice_fusion.1
  10.9 0.8 constant_dynamic-update-slice_fusion
  11.6 3.7 fusion.2
  15.3 0.9 fusion.3
  16.2 0.5 copy-done.2
  16.7 4.9 fusion.49
  21.7 1.7 fusion.14
  23.6 3.6 convolution_convert_fusion.5
  27.1 0.5 fusion.54
  27.9 249.9 %all-reduce = (f32[2,64,32]{1,2,0:T(8,128)S(1)}, f32[2,64]{1,0:T(2,128)S(1)}, f32[2,64,32]{1,2,0:T(8,128)S(1)}) all-reduce(f32[2,64,32]{1,2,0:T(8,128)S(1)} %copy.62, f32[2,64]{1,0:T(2,128)S(1)} %reshape.42, f32[2,64,32]{1,2,0:T(8,128)S(1)} %copy.68), channel_id=1, replica_groups=mesh['pts'=64,'head'=4] {'pts'}, use_global_device_ids=true, to_apply=%region_0.0 | all-reduce | flops 8320 | bytes 66560 | tf_op jit(solution)/shard_map/psum | solution.py:144
  277.8 1.0 fusion.26
  278.8 1.0 fusion.23
  279.9 1.0 fusion.30
  280.9 0.3 fusion.50
  281.2 0.3 fusion.10
  281.6 0.2 fusion.40
  281.8 0.2 fusion.41
  282.0 0.2 fusion.51
  282.2 0.2 fusion.12
  282.5 0.9 fusion.28
  283.4 0.9 convolution_add_fusion.2
  284.3 1.0 multiply_reduce_fusion.3
  285.5 4.2 fusion.11
  289.7 2.7 fusion.52
  292.6 0.8 convolution_convert_fusion.4
  293.5 1.3 copy-done.1
  294.8 2.2 fusion.1
  297.0 0.3 copy-done.7
  297.3 3.8 fusion.5
  301.1 0.8 convolution_convert_fusion.3
  302.0 1.0 copy-done.3
  302.9 0.7 copy-done.4
  303.7 0.8 fusion.9
  304.4 0.7 slice_multiply_fusion
  305.2 4.4 convolution_convert_fusion
  309.8 0.6 copy-done.6
  310.4 0.2 convolution_bitcast_fusion
  310.6 0.2 convolution_bitcast_fusion.2
  310.7 0.2 convolution_bitcast_fusion.1
  311.0 0.6 copy.56
  311.6 1.7 fusion.16
  313.4 0.2 fusion.53
  313.7 246.2 %psum.54 = f32[2,32,64]{2,1,0:T(8,128)} all-reduce(f32[2,32,64]{2,1,0:T(8,128)S(1)} %broadcast_multiply_fusion), channel_id=1, replica_groups=mesh['pts'=64,'head'=4] {'pts'}, use_global_device_ids=true, to_apply=%region_10.0 | all-reduce | flops 4096 | bytes 32768 | tf_op jit(solution)/shard_map/psum | solution.py:160
  559.9 1.5 copy.86
  561.4 1.5 copy.87
  562.8 1.5 copy.88
  (42 shorter events, 2.0 us)
Async XLA Ops:
  8.0 15.6 %copy-start = (bf16[64,256]{1,0:T(8,128)(2,1)S(1)}, bf16[64,256]{1,0:T(8,128)(2,1)}, u32[]{:S(2)}) copy-start(bf16[64,256]{1,0:T(8,128)(2,1)} %param.15) | copy-start | bytes 98308
  8.0 551.9 %all-reduce.4.cloned.1.call-start = ((), (), s32[]{:S(2)}) async-start(), calls=%async_computation.2 | async-start | bytes 393216 | tf_op jit(solution)/shard_map/psum | solution.py:160
  15.3 1.4 copy-start.2
  277.8 3.0 copy-start.5
  292.6 2.2 copy-start.1
  294.8 2.5 copy-start.7
  301.1 2.6 copy-start.4
  302.0 1.0 copy-start.3
  305.1 254.8 %reduce-scatter.2.cloned.1.call-start = ((), (), s32[]{:S(2)}) async-start(), calls=%async_computation.1 | async-start | bytes 5242880 | tf_op jit(solution)/shard_map/reduce_scatter | solution.py:162
  309.6 0.8 copy-start.6
Sparse Core Ops, SparseCore 0:
  305.3 177.5 all-reduce.3
Sparse Core Ops, SparseCore 1:
  309.7 47.9 reduce-scatter.1
where the time goes:
time: 577 us; the launch traced here: 572 us
  blocking collectives  496 us (86%)
  matrix products  44.7 us (8%)
  between operations  15.8 us (3%)
  local copies, waits for them, and re-layouts  13.1 us (2%)
    psum x1, blocking collectives, reduce_slices(): pool, norm = lax.psum((pool_part, norm_part), 'pts')  250 us
    psum x1, blocking collectives, per_device(): lax.psum((fx_local, mid_local, slice_local), 'pts')  246 us
    dot_general x13, matrix products, batched_product(): return jnp.dot(left, right, preferred_element_type=jnp.float32)  28 us
    dot_general x18, matrix products, fein(): jnp.einsum(form, left, right, precision=HIGH, preferred_element_type=jnp....  16.7 us
  transfers between devices with their start and end apart: 2, of which 0 were waited for; matrix products, arithmetic and copies ran while one was open for 1% of the time, Pallas kernels for 0%

commit v1 on v0

v1 whole, which is shorter than its diff:
```python
import math

import jax
import jax.numpy as jnp
import numpy as np
from jax import lax
from jax.experimental import pallas as pl
from jax.experimental.pallas import tpu as pltpu
from jax.sharding import Mesh
from jax.sharding import PartitionSpec as P

HIGH = lax.Precision.HIGHEST
F32 = jnp.float32
BF16 = jnp.bfloat16
LOG2E = 1.4426950408889634
NN = (((1,), (0,)), ((), ()))
NT = (((1,), (1,)), ((), ()))
TN = (((0,), (0,)), ((), ()))
PTS = ("y", "z", "core")


def bdot(left, right, dims=NN):
    return lax.dot_general(left, right, dims, preferred_element_type=F32)


def fdot(left, right, dims=NN):
    return lax.dot_general(left, right, dims, precision=HIGH, preferred_element_type=F32)


def slice_weights(logits):
    rows, cols = logits.shape
    expo = jnp.exp2(logits).reshape(rows // 64, 64, cols)
    weights = expo * (1.0 / jnp.sum(expo, axis=1, keepdims=True))
    return weights.reshape(rows, cols)


def pool_kernel(sharp, x_ref, u_ref, wmid, ws, wfx, wout, pay_ref, ab_ref, mq_ref, mq, acc, nacc):
    step = pl.program_id(0)

    @pl.when(step == 0)
    def _():
        for h in range(2):
            full = bdot(ws[h], wmid[32 * h : 32 * h + 32, :], TN) * (LOG2E / sharp[h])
            high = full.astype(BF16)
            mq[64 * h : 64 * h + 64, :] = high
            mq[128 + 64 * h : 192 + 64 * h, :] = (full - high.astype(F32)).astype(BF16)
        acc[...] = jnp.zeros_like(acc)
        nacc[...] = jnp.zeros_like(nacc)

    rows = x_ref.shape[0]
    sub = 512
    for part in range(rows // sub):
        xs = x_ref[part * sub : part * sub + sub, :]
        us = u_ref[part * sub : part * sub + sub, :]
        both = bdot(mq[...], xs, NT)
        weights = slice_weights(both[:128] + both[128:])
        total = weights[:, :128]
        for tile in range(1, sub // 128):
            total = total + weights[:, 128 * tile : 128 * tile + 128]
        nacc[...] += total
        weights_b = weights.astype(BF16)
        acc[:, :256] += bdot(weights_b, xs)
        acc[:, 256:] += bdot(weights_b, us)

    @pl.when(step == pl.num_programs(0) - 1)
    def _():
        ab_ref[...] = acc[...]
        mq_ref[...] = mq[...]
        pool = fdot(wfx[...].astype(F32), acc[:, :256], NT)
        grad_out = fdot(wout[...].astype(F32), acc[:, 256:], NT)
        first = lax.broadcasted_iota(jnp.int32, (32, 128), 1) < 64
        pay_ref[0:32, :] = jnp.where(first, pool[:32], pool[32:])
        pay_ref[32:64, :] = jnp.where(first, grad_out[:32], grad_out[32:])
        norm = fdot(jnp.ones((16, 128), F32), nacc[...], NT)
        top = lax.broadcasted_iota(jnp.int32, (16, 128), 0) == 0
        pay_ref[64:80, :] = jnp.where(top, norm, 0.0)


def token_part(pay, h, sharp, qkv, ws, wmid, wfx, wout):
    lanes = slice(64 * h, 64 * h + 64)
    root = 1.0 / math.sqrt(32.0)
    norm = pay[64:65, lanes]
    token = pay[0:32, lanes] / norm
    grad_so = pay[32:64, lanes]
    maps = qkv[h]
    proj = fdot(maps, token)
    query, key, value = proj[:32], proj[32:64], proj[64:]
    expo = jnp.exp(fdot(key, query, TN) * root)
    prob = expo / jnp.sum(expo, axis=0, keepdims=True)
    so = fdot(value, prob)
    grad_prob = fdot(value, grad_so, TN)
    grad_value = fdot(grad_so, prob, NT)
    grad_score = prob * (grad_prob - jnp.sum(prob * grad_prob, axis=0, keepdims=True)) * root
    grad_query = fdot(key, grad_score)
    grad_key = fdot(query, grad_score, NT)
    grads = jnp.concatenate([grad_query, grad_key, grad_value], axis=0)
    attn = fdot(token, grads, NT)
    grad_token = fdot(maps, grads, TN)
    grad_pool = (grad_token / norm).astype(BF16)
    grad_norm = -fdot(grad_token * token / norm, jnp.ones((32, 128), F32), TN)
    return so.astype(BF16), grad_pool, grad_norm, attn


def centre(block):
    return block - jnp.mean(block, axis=0, keepdims=True)


def grad_kernel(
    scale, sharp, me, pay, qkv, ws, wmid, wfx, wout, ab, mq, x_ref, u_ref,
    out0, out1, out2, out3, grads_ref, attn_ref,
    mx, mu, gn, wc, wcr, sob, gpb, gacc,
):
    step = pl.program_id(0)

    @pl.when(step == 0)
    def _():
        mx[0:256, :] = mq[...]
        for h in range(2):
            feat = slice(32 * h, 32 * h + 32)
            rows = slice(64 * h, 64 * h + 64)
            so, grad_pool, grad_norm, attn = token_part(pay, h, sharp, qkv, ws, wmid, wfx, wout)
            sob[feat, :] = so
            gpb[feat, :] = grad_pool
            for j in range(3):
                attn_ref[h, j] = attn[:, 32 * j : 32 * j + 32]
            inv = 1.0 / sharp[h]
            mu[rows, :] = (centre(bdot(so, wout[feat, :], TN)) * inv).astype(BF16)
            mx[256 + 64 * h : 320 + 64 * h, :] = (
                centre(bdot(grad_pool, wfx[feat, :], TN)) * inv
            ).astype(BF16)
            gn[rows, :] = grad_norm * inv
            wc[:, 64 * h : 64 * h + 64] = bdot(wmid[feat, :], ws[h], TN).astype(BF16)
            wc[:, 128 + 64 * h : 192 + 64 * h] = bdot(wfx[feat, :], grad_pool, TN).astype(BF16)
        for k in range(4):
            group = lax.rem(me[0] + k, 4)
            wcr[64 * k : 64 * k + 64, :] = wc[pl.ds(pl.multiple_of(group * 64, 64), 64), :]
        gacc[...] = jnp.zeros_like(gacc)

    rows = x_ref.shape[0]
    sub = 512
    for part in range(rows // sub):
        here = slice(part * sub, part * sub + sub)
        xs = x_ref[here, :]
        us = u_ref[here, :]
        both = bdot(mx[...], xs, NT)
        weights = slice_weights(both[:128] + both[128:256])
        grad_w = both[256:] + bdot(mu[...], us, NT) + gn[:, :1]
        prod = (weights * grad_w).reshape(2, 64, sub)
        mean = jnp.sum(prod, axis=1, keepdims=True)
        grad_logit = (prod - weights.reshape(2, 64, sub) * mean).reshape(128, sub).astype(BF16)
        gacc[...] += bdot(grad_logit, xs)
        pair = jnp.concatenate([grad_logit, weights.astype(BF16)], axis=0)
        out = bdot(wcr[...], pair).astype(BF16)
        for k, ref in enumerate((out0, out1, out2, out3)):
            ref[:, here] = out[64 * k : 64 * k + 64]

    @pl.when(step == pl.num_programs(0) - 1)
    def _():
        for h in range(2):
            feat = slice(32 * h, 32 * h + 32)
            rows = slice(64 * h, 64 * h + 64)
            grads_ref[feat, :] = fdot(gpb[feat, :].astype(F32), ab[rows, :256])
            grads_ref[64 + 32 * h : 96 + 32 * h, :] = scale * fdot(ws[h].astype(F32), gacc[rows, :])
            grads_ref[128 + 32 * h : 160 + 32 * h, :] = scale * fdot(
                sob[feat, :].astype(F32), ab[rows, 256:]
            )
        score = scale * fdot(wmid[...].astype(F32), gacc[...], NT)
        first = lax.broadcasted_iota(jnp.int32, (32, 128), 1) < 64
        score = jnp.where(first, score[:32], score[32:])
        grads_ref[192:208, :128] = score[:16]
        grads_ref[192:208, 128:] = score[16:]


def whole(shape):
    return pl.BlockSpec(shape, lambda i: (0,) * len(shape))


SMEM = pl.BlockSpec(memory_space=pltpu.SMEM)


def first_pass(sharp, x, u, wmid, ws, wfx, wout, block=1024):
    points = x.shape[0]
    rows = pl.BlockSpec((block, 256), lambda i: (i, 0))
    return pl.pallas_call(
        pool_kernel,
        grid=(points // block,),
        in_specs=[SMEM, rows, rows, whole((64, 256)), whole((2, 32, 64)), whole((64, 256)), whole((64, 256))],
        out_specs=[whole((80, 128)), whole((128, 512)), whole((256, 256))],
        out_shape=[
            jax.ShapeDtypeStruct((80, 128), F32),
            jax.ShapeDtypeStruct((128, 512), F32),
            jax.ShapeDtypeStruct((256, 256), BF16),
        ],
        scratch_shapes=[
            pltpu.VMEM((256, 256), BF16),
            pltpu.VMEM((128, 512), F32),
            pltpu.VMEM((128, 128), F32),
        ],
        compiler_params=pltpu.CompilerParams(vmem_limit_bytes=32 * 1024 * 1024),
        name="pool_pass",
    )(sharp, x, u, wmid, ws, wfx, wout)


def second_pass(scale, sharp, me, pay, qkv, ws, wmid, wfx, wout, ab, mq, x, u, block=1024):
    points = x.shape[0]
    rows = pl.BlockSpec((block, 256), lambda i: (i, 0))
    cols = pl.BlockSpec((64, block), lambda i: (0, i))

    def kernel(*refs):
        grad_kernel(scale, *refs)

    return pl.pallas_call(
        kernel,
        grid=(points // block,),
        in_specs=[
            SMEM, SMEM, whole((80, 128)), whole((2, 96, 32)), whole((2, 32, 64)), whole((64, 256)),
            whole((64, 256)), whole((64, 256)), whole((128, 512)), whole((256, 256)), rows, rows,
        ],
        out_specs=[cols] * 4 + [whole((208, 256)), whole((2, 3, 32, 32))],
        out_shape=[jax.ShapeDtypeStruct((64, points), BF16)] * 4
        + [
            jax.ShapeDtypeStruct((208, 256), F32),
            jax.ShapeDtypeStruct((2, 3, 32, 32), F32),
        ],
        scratch_shapes=[
            pltpu.VMEM((384, 256), BF16),
            pltpu.VMEM((128, 256), BF16),
            pltpu.VMEM((128, 128), F32),
            pltpu.VMEM((256, 256), BF16),
            pltpu.VMEM((256, 256), BF16),
            pltpu.VMEM((64, 64), BF16),
            pltpu.VMEM((64, 64), BF16),
            pltpu.VMEM((128, 256), F32),
        ],
        compiler_params=pltpu.CompilerParams(vmem_limit_bytes=32 * 1024 * 1024),
        name="grad_pass",
    )(sharp, me, pay, qkv, ws, wmid, wfx, wout, ab, mq, x, u)


def core_swap(value):
    return lax.ppermute(value, "core", [(0, 1), (1, 0)])


def core_scatter(value):
    core = lax.axis_index("core")
    half = value.shape[0] // 2
    mine = lax.dynamic_slice_in_dim(value, core * half, half)
    other = lax.dynamic_slice_in_dim(value, (1 - core) * half, half)
    return mine + core_swap(other)


def core_gather(value):
    core = lax.axis_index("core")
    other = core_swap(value)
    return jnp.concatenate(
        [jnp.where(core == 0, value, other), jnp.where(core == 0, other, value)], axis=0
    )


def y_sum(value, size, kind=F32):
    parts = [
        lax.ppermute(value, "y", [(i, i ^ k) for i in range(size)]).astype(kind)
        for k in range(1, size)
    ]
    return (value.astype(kind) + parts[0]) + (parts[1] + parts[2])


def z_sum(value, size, kind=F32):
    sent = jnp.broadcast_to(value[None], (size,) + value.shape)
    return jnp.sum(lax.all_to_all(sent, "z", 0, 0).astype(kind), axis=0)


def sum_points(value, sizes):
    half = core_scatter(value)
    half = y_sum(half, sizes["y"])
    half = z_sum(half, sizes["z"])
    return core_gather(half)


def sum_points_16(value, sizes):
    half = core_scatter(value).astype(BF16)
    half = y_sum(half, sizes["y"]).astype(BF16)
    half = z_sum(half, sizes["z"])
    return core_gather(half)


def solution(mesh):
    sizes = {"y": 4, "z": 8, "core": 2, "head": 4}
    fine = Mesh(np.asarray(mesh.devices).reshape(tuple(sizes.values())), tuple(sizes))

    def per_device(x, u, wfx, wmid, ws, sharp, qkv, wout):
        points = x.shape[0]
        scale = 1.0 / math.sqrt(points * 64)
        wfx_t = wfx.T
        wmid_t = wmid.T
        maps = jnp.swapaxes(qkv, 2, 3).reshape(2, 96, 32)
        pay, ab, mq = first_pass(sharp, x, u, wmid_t, ws, wfx_t, wout)
        pay = sum_points(pay, sizes)
        me = lax.axis_index("head").astype(jnp.int32).reshape(1)
        out0, out1, out2, out3, grads, attn = second_pass(
            scale, sharp, me, pay, maps, ws, wmid_t, wfx_t, wout, ab, mq, x, u
        )
        received = [
            lax.ppermute(part, "head", [(i, (i + k) % 4) for i in range(4)])
            for k, part in ((1, out1), (2, out2), (3, out3))
        ]
        grads = sum_points_16(grads, sizes)
        total = out0.astype(F32)
        for part in received:
            total = total + part.astype(F32)
        score = jnp.concatenate([grads[192:, :128], grads[192:, 128:]], axis=0)
        slice_grad = score.reshape(32, 2, 64).transpose(1, 0, 2)
        return (
            total.astype(BF16).T,
            grads[0:64].T,
            grads[64:128].T,
            slice_grad,
            attn,
            grads[128:192],
        )

    in_specs = (
        P(PTS, None),
        P(PTS, None),
        P(None, "head"),
        P(None, "head"),
        P("head", None, None),
        P("head"),
        P("head", None, None, None),
        P("head", None),
    )
    out_specs = (
        P(PTS, "head"),
        P(None, "head"),
        P(None, "head"),
        P("head", None, None),
        P("head", None, None, None),
        P("head", None),
    )
    return jax.shard_map(
        per_device, mesh=fine, in_specs=in_specs, out_specs=out_specs, check_vma=False
    )
```

time: 577 us -> 133 us (0.23)
  blocking collectives: 496 us -> 16.1 us
  waiting for transfers between devices: 0.04 us -> 51.7 us
  matrix products: 44.7 us -> 0 us
  starting transfers between devices: 0.08 us -> 23.3 us
  Pallas kernels: 0 us -> 20.7 us
  between operations: 15.8 us -> 0.83 us
    psum x2 -> x0, blocking collectives: 496 us -> none  [the longest x1 250 us: reduce_slices(): pool, norm = lax.psum((pool_part, norm_part), 'pts')]
    dot_general x31 -> x0, matrix products: 44.7 us -> none  [the longest x13 28 us: batched_product(): return jnp.dot(left, right, preferred_element_type=jnp.float32)]
    ppermute x0 -> x13, waiting for transfers between devices: none -> 42.2 us  [the longest x3 33.1 us: per_device(): lax.ppermute(part, 'head', [(i, (i + k) % 4) for i in range(4)])]
    pallas_call x0 -> x2, Pallas kernels: none -> 20.7 us  [the longest x1 12.9 us: second_pass(): pl.pallas_call(kernel, grid=(points // block,), in_specs=[SMEM, SMEM, who...]
    ppermute x0 -> x13, starting transfers between devices: none -> 19.8 us  [the longest x4 10.2 us: core_swap(): return lax.ppermute(value, 'core', [(0, 1), (1, 0)])]
    all_to_all x0 -> x1, blocking collectives: none -> 16.1 us  [z_sum(): return jnp.sum(lax.all_to_all(sent, 'z', 0, 0).astype(kind), axis=0)]
    all_to_all x0 -> x1, waiting for transfers between devices: none -> 9.47 us  [z_sum(): return jnp.sum(lax.all_to_all(sent, 'z', 0, 0).astype(kind), axis=0)]
    unnamed x21 -> x34, local copies, waits for them, and re-layouts: 10.3 us -> 14.4 us
  transfers between devices with their start and end apart: 2 -> 14, of which waited for: 0 -> 12; matrix products, arithmetic and copies ran while one was open for 1% -> 1% of each run, Pallas kernels for 0% -> 0%
where the time goes in v1:
time: 133 us
  waiting for transfers between devices  51.7 us (39%)
  starting transfers between devices  23.3 us (18%)
  Pallas kernels  20.7 us (16%)
  blocking collectives  16.1 us (12%)
  local copies, waits for them, and re-layouts  16 us (12%)
  other arithmetic  4.18 us (3%)
    ppermute x3, waiting for transfers between devices, per_device(): lax.ppermute(part, 'head', [(i, (i + k) % 4) for i in range(4)])  33.1 us
    all_to_all x1, blocking collectives, z_sum(): return jnp.sum(lax.all_to_all(sent, 'z', 0, 0).astype(kind), axis=0)  16.1 us
    unnamed x34, local copies, waits for them, and re-layouts  14.4 us
    pallas_call x1, Pallas kernels, second_pass(): pl.pallas_call(kernel, grid=(points // block,), in_specs=[SMEM, SMEM, who...  12.9 us
    ppermute x4, starting transfers between devices, core_swap(): return lax.ppermute(value, 'core', [(0, 1), (1, 0)])  10.2 us
    all_to_all x1, waiting for transfers between devices, z_sum(): return jnp.sum(lax.all_to_all(sent, 'z', 0, 0).astype(kind), axis=0)  9.47 us
    pallas_call x1, Pallas kernels, first_pass(): pl.pallas_call(pool_kernel, grid=(points // block,), in_specs=[SMEM, rows...  7.85 us
    ppermute x6, starting transfers between devices, y_sum(): lax.ppermute(value, 'y', [(i, i ^ k) for i in range(size)]).astype(kind)  5.99 us
  transfers between devices with their start and end apart: 14, of which 12 were waited for; matrix products, arithmetic and copies ran while one was open for 1% of the time, Pallas kernels for 0%

profile of v1, /device:TPU:1, one launch (start us, length us, event | category | flops | bytes accessed | tf_op | source)
XLA Modules:
  0.0 132.8 jit_solution(8380139553407285671)
XLA Ops:
  0.6 0.0 copy-start
  0.7 2.2 %copy-done = bf16[8192,256]{1,0:T(8,128)(2,1)S(1)} copy-done((bf16[8192,256]{1,0:T(8,128)(2,1)S(1)}, bf16[8192,256]{1,0:T(8,128)(2,1)}, u32[]{:S(2)}) %copy-start) | copy-done | bytes 4194328
  2.8 2.2 %copy-done.2 = bf16[8192,256]{1,0:T(8,128)(2,1)S(1)} copy-done((bf16[8192,256]{1,0:T(8,128)(2,1)S(1)}, bf16[8192,256]{1,0:T(8,128)(2,1)}, u32[]{:S(2)}) %copy-start.2) | copy-done | bytes 4194328
  5.0 0.8 copy-done.4
  5.8 0.8 copy-done.6
  6.5 0.8 copy-done.8
  7.3 0.7 copy-done.10
  8.0 0.7 copy-done.12
  8.7 7.8 %pool_pass.1 = (f32[80,128]{1,0:T(8,128)S(1)}, f32[128,512]{1,0:T(8,128)S(1)}, bf16[256,256]{1,0:T(8,128)(2,1)S(1)}) custom-call(f32[2]{0:T(128)S(1)} %copy-done.12, bf16[8192,256]{1,0:T(8,128)(2,1)S(1)} %copy-done, bf16[8192,256]{1,0:T(8,128)(2,1)S(1)} %copy-done.2, bf16[64,256]{1,0:T(8,128)(2,1)S(1)} %bitcast.15, bf16[2,32,64]{2,1,0:T(8,128)(2,1)S(1)} %copy-done.10, ...), custom_call_target="tpu_custom_call" | custom-call | tf_op jit(solution)/shard_map/pool_pass/pallas_call | solution.py:184
  16.6 3.3 %collective-permute-start = (f32[40,128]{1,0:T(8,128)S(1)}, f32[40,128]{1,0:T(8,128)S(1)}, u32[]{:S(2)}, u32[]{:S(2)}) collective-permute-start(f32[40,128]{1,0:T(8,128)S(1)} %constant_dynamic-slice_fusion.1), channel_id=1, source_target_pairs={{0,4},{4,0},{1,5},{5,1},{2,6},{6,2},{3,7},{7,3},{8,12},{12,8},{9,1... | collective-permute-start | bytes 61448 | tf_op jit(solution)/shard_map/ppermute | solution.py:241
  19.9 0.8 collective-permute-done
  20.8 1.2 collective-permute-start.2
  21.9 0.8 collective-permute-start.3
  22.7 0.7 collective-permute-start.1
  23.4 1.5 %collective-permute-done.2 = f32[40,128]{1,0:T(8,128)S(1)} collective-permute-done((f32[40,128]{1,0:T(8,128)S(1)}, f32[40,128]{1,0:T(8,128)S(1)}, u32[]{:S(2)}, u32[]{:S(2)}) %collective-permute-start.2) | collective-permute-done | bytes 20512 | tf_op jit(solution)/shard_map/ppermute | solution.py:262
  24.9 1.1 collective-permute-done.3
  26.0 16.1 %all_to_all.10 = f32[8,40,128]{2,1,0:T(8,128)S(1)} all-to-all(f32[8,40,128]{2,1,0:T(8,128)S(1)} %broadcast_in_dim.4), channel_id=1, replica_groups=mesh['y'=4,'z'=8,'core'=2,'head'=4] {'z'}, dimensions={0} | all-to-all | bytes 327680 | tf_op jit(solution)/shard_map/all_to_all | solution.py:270
  42.2 3.2 %collective-permute-start.4 = (f32[40,128]{1,0:T(8,128)S(1)}, f32[40,128]{1,0:T(8,128)S(1)}, u32[]{:S(2)}, u32[]{:S(2)}) collective-permute-start(f32[40,128]{1,0:T(8,128)S(1)} %reduce_sum.18), channel_id=1, source_target_pairs={{0,4},{4,0},{1,5},{5,1},{2,6},{6,2},{3,7},{7,3},{8,12},{12,8},{9,1... | collective-permute-start | bytes 61448 | tf_op jit(solution)/shard_map/ppermute | solution.py:241
  45.4 0.1 copy.16
  45.5 0.7 collective-permute-done.4
  46.3 0.0 copy-start.1
  46.3 2.2 %copy-done.1 = bf16[8192,256]{1,0:T(8,128)(2,1)S(1)} copy-done((bf16[8192,256]{1,0:T(8,128)(2,1)S(1)}, bf16[8192,256]{1,0:T(8,128)(2,1)}, u32[]{:S(2)}) %copy-start.1) | copy-done | bytes 4194328
  48.5 2.2 %copy-done.3 = bf16[8192,256]{1,0:T(8,128)(2,1)S(1)} copy-done((bf16[8192,256]{1,0:T(8,128)(2,1)S(1)}, bf16[8192,256]{1,0:T(8,128)(2,1)}, u32[]{:S(2)}) %copy-start.3) | copy-done | bytes 4194328
  50.7 12.9 %grad_pass.1 = (bf16[64,8192]{1,0:T(8,128)(2,1)S(1)}, bf16[64,8192]{1,0:T(8,128)(2,1)S(1)}, bf16[64,8192]{1,0:T(8,128)(2,1)S(1)}, bf16[64,8192]{1,0:T(8,128)(2,1...) custom-call(f32[2]{0:T(128)S(1)} %copy-done.13, s32[1]{0:T(128)} %bitcast.refs_1_, ...), custom_call_target="tpu_custom_call" | custom-call | tf_op jit(solution)/shard_map/grad_pass/pallas_call | solution.py:212
  63.5 1.0 copy-done.14
  64.5 1.0 copy-done.15
  65.5 0.4 collective-permute-start.8
  65.9 1.0 collective-permute-done.8
  66.9 1.8 %collective-permute-start.11 = (bf16[104,256]{1,0:T(8,128)(2,1)S(1)}, bf16[104,256]{1,0:T(8,128)(2,1)S(1)}, u32[]{:S(2)}, u32[]{:S(2)}) collective-permute-start(bf16[104,256]{1,0:T(8,128)(2,1)S(1)} %add_convert_fusion.2), channel_id=1, source_target_pairs={{0,192},{64,128},{128,64},{192,0},{1,193},{65,129},{129,65},{193,1... | collective-permute-start | bytes 159752 | tf_op jit(solution)/shard_map/ppermute | solution.py:262
  68.7 1.5 %collective-permute-start.9 = (bf16[104,256]{1,0:T(8,128)(2,1)S(1)}, bf16[104,256]{1,0:T(8,128)(2,1)S(1)}, u32[]{:S(2)}, u32[]{:S(2)}) collective-permute-start(bf16[104,256]{1,0:T(8,128)(2,1)S(1)} %add_convert_fusion.2), channel_id=1, source_target_pairs={{0,64},{64,0},{128,192},{192,128},{1,65},{65,1},{129,193},{193,129... | collective-permute-start | bytes 159752 | tf_op jit(solution)/shard_map/ppermute | solution.py:262
  70.3 0.9 collective-permute-done.11
  71.2 2.0 %collective-permute-done.10 = bf16[104,256]{1,0:T(8,128)(2,1)S(1)} collective-permute-done((bf16[104,256]{1,0:T(8,128)(2,1)S(1)}, bf16[104,256]{1,0:T(8,128)(2,1)S(1)}, u32[]{:S(2)}, u32[]{:S(2)}) %collective-permute-start.10) | collective-permute-done | bytes 53280 | tf_op jit(solution)/shard_map/ppermute | solution.py:262
  73.3 0.8 broadcast_in_dim.5
  74.1 3.5 %all-to-all-start.1 = ((bf16[8,104,256]{2,1,0:T(8,128)(2,1)}), bf16[8,104,256]{2,1,0:T(8,128)(2,1)S(1)}, u32[]{:S(2)}, u32[]{:S(2)}) async-start(bf16[8,104,256]{2,1,0:T(8,128)(2,1)} %broadcast_in_dim.5), calls=%async_computation.1 | async-start | bytes 851968 | tf_op jit(solution)/shard_map/all_to_all | solution.py:270
  77.5 2.5 %collective-permute-start.7 = (bf16[64,8192]{1,0:T(8,128)(2,1)}, bf16[64,8192]{1,0:T(8,128)(2,1)}, u32[]{:S(2)}, u32[]{:S(2)}) collective-permute-start(bf16[64,8192]{1,0:T(8,128)(2,1)} %copy-done.15), channel_id=1, source_target_pairs={{0,3},{1,0},{2,1},{3,2},{4,7},{5,4},{6,5},{7,6},{8,11},{9,8},{10,9... | collective-permute-start | bytes 3145736 | tf_op jit(solution)/shard_map/ppermute | solution.py:304
  80.1 0.5 collective-permute-start.6
  80.6 0.6 collective-permute-start.5
  81.2 9.5 %all-to-all-done.1 = bf16[8,104,256]{2,1,0:T(8,128)(2,1)S(1)} async-done(((bf16[8,104,256]{2,1,0:T(8,128)(2,1)}), bf16[8,104,256]{2,1,0:T(8,128)(2,1)S(1)}, u32[]{:S(2)}, u32[]{:S(2)}) %all-to-all-start.1) | async-done | bytes 426016 | tf_op jit(solution)/shard_map/all_to_all | solution.py:270
  90.6 0.1 convert_reduce_fusion
  90.7 3.2 %collective-permute-start.12 = (f32[104,256]{1,0:T(8,128)S(1)}, f32[104,256]{1,0:T(8,128)S(1)}, u32[]{:S(2)}, u32[]{:S(2)}) collective-permute-start(f32[104,256]{1,0:T(8,128)S(1)} %convert_reduce_fusion), channel_id=1, source_target_pairs={{0,4},{4,0},{1,5},{5,1},{2,6},{6,2},{3,7},{7,3},{8,12},{12,8},{9,1... | collective-permute-start | bytes 319496 | tf_op jit(solution)/shard_map/ppermute | solution.py:241
  93.9 1.0 collective-permute-done.12
  94.9 0.1 reshape.25
  95.0 0.6 copy.19
  95.6 0.7 fusion.2
  96.3 5.5 %collective-permute-done.7 = bf16[64,8192]{1,0:T(8,128)(2,1)} collective-permute-done((bf16[64,8192]{1,0:T(8,128)(2,1)}, bf16[64,8192]{1,0:T(8,128)(2,1)}, u32[]{:S(2)}, u32[]{:S(2)}) %collective-permute-start.7) | collective-permute-done | bytes 1048608 | tf_op jit(solution)/shard_map/ppermute | solution.py:304
  101.8 2.7 %collective-permute-done.6 = bf16[64,8192]{1,0:T(8,128)(2,1)} collective-permute-done((bf16[64,8192]{1,0:T(8,128)(2,1)}, bf16[64,8192]{1,0:T(8,128)(2,1)}, u32[]{:S(2)}, u32[]{:S(2)}) %collective-permute-start.6) | collective-permute-done | bytes 1048608 | tf_op jit(solution)/shard_map/ppermute | solution.py:304
  104.5 24.9 %collective-permute-done.5 = bf16[64,8192]{1,0:T(8,128)(2,1)} collective-permute-done((bf16[64,8192]{1,0:T(8,128)(2,1)S(1)}, bf16[64,8192]{1,0:T(8,128)(2,1)}, u32[]{:S(2)}, u32[]{:S(2)}) %collective-permute-start.5) | collective-permute-done | bytes 1048608 | tf_op jit(solution)/shard_map/ppermute | solution.py:304
  129.4 3.3 %fusion = bf16[8192,64]{0,1:T(8,128)(2,1)} fusion(bf16[64,8192]{1,0:T(8,128)(2,1)} %collective-permute-done.7, bf16[64,8192]{1,0:T(8,128)(2,1)} %collective-permute-done.6, bf16[64,8192]{1,0:T(8,128)(2,1)} %collective-permute-done.5, bf16[64,8192]{1,0:T(8,128)(2,1)S(1)} %get-tuple-element.18), kind=kLoop, calls=%fused_computation.1 | loop fusion | flops 4194304 | bytes 5242880 | tf_op jit(solution)/shard_map/transpose | solution.py:314
  (37 shorter events, 0.2 us)
Async XLA Ops:
  0.6 2.2 %copy-start = (bf16[8192,256]{1,0:T(8,128)(2,1)S(1)}, bf16[8192,256]{1,0:T(8,128)(2,1)}, u32[]{:S(2)}) copy-start(bf16[8192,256]{1,0:T(8,128)(2,1)} %refs_10_.1) | copy-start | bytes 12582916
  2.8 2.2 %copy-start.2 = (bf16[8192,256]{1,0:T(8,128)(2,1)S(1)}, bf16[8192,256]{1,0:T(8,128)(2,1)}, u32[]{:S(2)}) copy-start(bf16[8192,256]{1,0:T(8,128)(2,1)} %refs_11_.1) | copy-start | bytes 12582916
  5.0 0.8 copy-start.4
  5.8 0.8 copy-start.6
  6.5 0.8 copy-start.8
  7.3 0.7 copy-start.10
  8.0 0.7 copy-start.12
  8.7 36.7 %copy-start.16 = (f32[2,3,32,32]{3,2,1,0:T(8,128)S(1)}, f32[2,3,32,32]{3,2,1,0:T(8,128)}, u32[]{:S(2)}) copy-start(f32[2,3,32,32]{3,2,1,0:T(8,128)} %param.14) | copy-start | bytes 73732
  8.7 37.6 %copy-start.5 = (bf16[256,64]{0,1:T(8,128)(2,1)S(1)}, bf16[256,64]{0,1:T(8,128)(2,1)}, u32[]{:S(2)}) copy-start(bf16[256,64]{0,1:T(8,128)(2,1)} %param.11) | copy-start | bytes 98308
  8.7 37.6 %copy-start.7 = (bf16[256,64]{0,1:T(8,128)(2,1)S(1)}, bf16[256,64]{0,1:T(8,128)(2,1)}, u32[]{:S(2)}) copy-start(bf16[256,64]{0,1:T(8,128)(2,1)} %param.10) | copy-start | bytes 98308
  8.7 37.6 %copy-start.9 = (bf16[64,256]{1,0:T(8,128)(2,1)S(1)}, bf16[64,256]{1,0:T(8,128)(2,1)}, u32[]{:S(2)}) copy-start(bf16[64,256]{1,0:T(8,128)(2,1)} %refs_7_.1) | copy-start | bytes 98308
  8.7 37.6 %copy-start.11 = (bf16[2,32,64]{2,1,0:T(8,128)(2,1)S(1)}, bf16[2,32,64]{2,1,0:T(8,128)(2,1)}, u32[]{:S(2)}) copy-start(bf16[2,32,64]{2,1,0:T(8,128)(2,1)} %refs_4_.1) | copy-start | bytes 24580
  8.7 37.6 %copy-start.13 = (f32[2]{0:T(128)S(1)}, f32[2]{0:T(128)}, u32[]{:S(2)}) copy-start(f32[2]{0:T(128)} %refs_0_.1) | copy-start | bytes 28
  16.6 4.2 %collective-permute-start = (f32[40,128]{1,0:T(8,128)S(1)}, f32[40,128]{1,0:T(8,128)S(1)}, u32[]{:S(2)}, u32[]{:S(2)}) collective-permute-start(f32[40,128]{1,0:T(8,128)S(1)} %constant_dynamic-slice_fusion.1), channel_id=1, source_target_pairs={{0,4},{4,0},{1,5},{5,1},{2,6},{6,2},{3,7},{7,3},{8,12},{12,8},{9,1... | collective-permute-start | bytes 61448 | tf_op jit(solution)/shard_map/ppermute | solution.py:241
  20.8 4.1 %collective-permute-start.2 = (f32[40,128]{1,0:T(8,128)S(1)}, f32[40,128]{1,0:T(8,128)S(1)}, u32[]{:S(2)}, u32[]{:S(2)}) collective-permute-start(f32[40,128]{1,0:T(8,128)S(1)} %dynamic-slice_add_fusion), channel_id=1, source_target_pairs={{0,128},{64,192},{128,0},{192,64},{1,129},{65,193},{129,1},{193,65... | collective-permute-start | bytes 61448 | tf_op jit(solution)/shard_map/ppermute | solution.py:262
  21.9 4.1 %collective-permute-start.3 = (f32[40,128]{1,0:T(8,128)S(1)}, f32[40,128]{1,0:T(8,128)S(1)}, u32[]{:S(2)}, u32[]{:S(2)}) collective-permute-start(f32[40,128]{1,0:T(8,128)S(1)} %dynamic-slice_add_fusion), channel_id=1, source_target_pairs={{0,192},{64,128},{128,64},{192,0},{1,193},{65,129},{129,65},{193,1... | collective-permute-start | bytes 61448 | tf_op jit(solution)/shard_map/ppermute | solution.py:262
  22.7 3.3 %collective-permute-start.1 = (f32[40,128]{1,0:T(8,128)S(1)}, f32[40,128]{1,0:T(8,128)S(1)}, u32[]{:S(2)}, u32[]{:S(2)}) collective-permute-start(f32[40,128]{1,0:T(8,128)S(1)} %dynamic-slice_add_fusion), channel_id=1, source_target_pairs={{0,64},{64,0},{128,192},{192,128},{1,65},{65,1},{129,193},{193,129... | collective-permute-start | bytes 61448 | tf_op jit(solution)/shard_map/ppermute | solution.py:262
  42.2 4.1 %collective-permute-start.4 = (f32[40,128]{1,0:T(8,128)S(1)}, f32[40,128]{1,0:T(8,128)S(1)}, u32[]{:S(2)}, u32[]{:S(2)}) collective-permute-start(f32[40,128]{1,0:T(8,128)S(1)} %reduce_sum.18), channel_id=1, source_target_pairs={{0,4},{4,0},{1,5},{5,1},{2,6},{6,2},{3,7},{7,3},{8,12},{12,8},{9,1... | collective-permute-start | bytes 61448 | tf_op jit(solution)/shard_map/ppermute | solution.py:241
  46.3 2.2 %copy-start.1 = (bf16[8192,256]{1,0:T(8,128)(2,1)S(1)}, bf16[8192,256]{1,0:T(8,128)(2,1)}, u32[]{:S(2)}) copy-start(bf16[8192,256]{1,0:T(8,128)(2,1)} %refs_10_.1) | copy-start | bytes 12582916
  48.5 2.2 %copy-start.3 = (bf16[8192,256]{1,0:T(8,128)(2,1)S(1)}, bf16[8192,256]{1,0:T(8,128)(2,1)}, u32[]{:S(2)}) copy-start(bf16[8192,256]{1,0:T(8,128)(2,1)} %refs_11_.1) | copy-start | bytes 12582916
  63.5 1.0 copy-start.14
  64.5 1.0 copy-start.15
  65.5 1.4 %collective-permute-start.8 = (f32[104,256]{1,0:T(8,128)S(1)}, f32[104,256]{1,0:T(8,128)S(1)}, u32[]{:S(2)}, u32[]{:S(2)}) collective-permute-start(f32[104,256]{1,0:T(8,128)S(1)} %constant_dynamic-slice_fusion), channel_id=1, source_target_pairs={{0,4},{4,0},{1,5},{5,1},{2,6},{6,2},{3,7},{7,3},{8,12},{12,8},{9,1... | collective-permute-start | bytes 319496 | tf_op jit(solution)/shard_map/ppermute | solution.py:241
  66.9 4.3 %collective-permute-start.11 = (bf16[104,256]{1,0:T(8,128)(2,1)S(1)}, bf16[104,256]{1,0:T(8,128)(2,1)S(1)}, u32[]{:S(2)}, u32[]{:S(2)}) collective-permute-start(bf16[104,256]{1,0:T(8,128)(2,1)S(1)} %add_convert_fusion.2), channel_id=1, source_target_pairs={{0,192},{64,128},{128,64},{192,0},{1,193},{65,129},{129,65},{193,1... | collective-permute-start | bytes 159752 | tf_op jit(solution)/shard_map/ppermute | solution.py:262
  68.7 4.5 %collective-permute-start.10 = (bf16[104,256]{1,0:T(8,128)(2,1)S(1)}, bf16[104,256]{1,0:T(8,128)(2,1)S(1)}, u32[]{:S(2)}, u32[]{:S(2)}) collective-permute-start(bf16[104,256]{1,0:T(8,128)(2,1)S(1)} %add_convert_fusion.2), channel_id=1, source_target_pairs={{0,128},{64,192},{128,0},{192,64},{1,129},{65,193},{129,1},{193,65... | collective-permute-start | bytes 159752 | tf_op jit(solution)/shard_map/ppermute | solution.py:262
  68.7 4.5 %collective-permute-start.9 = (bf16[104,256]{1,0:T(8,128)(2,1)S(1)}, bf16[104,256]{1,0:T(8,128)(2,1)S(1)}, u32[]{:S(2)}, u32[]{:S(2)}) collective-permute-start(bf16[104,256]{1,0:T(8,128)(2,1)S(1)} %add_convert_fusion.2), channel_id=1, source_target_pairs={{0,64},{64,0},{128,192},{192,128},{1,65},{65,1},{129,193},{193,129... | collective-permute-start | bytes 159752 | tf_op jit(solution)/shard_map/ppermute | solution.py:262
  74.1 16.6 %all-to-all-start.1 = ((bf16[8,104,256]{2,1,0:T(8,128)(2,1)}), bf16[8,104,256]{2,1,0:T(8,128)(2,1)S(1)}, u32[]{:S(2)}, u32[]{:S(2)}) async-start(bf16[8,104,256]{2,1,0:T(8,128)(2,1)} %broadcast_in_dim.5), calls=%async_computation.1 | async-start | bytes 851968 | tf_op jit(solution)/shard_map/all_to_all | solution.py:270
  77.5 24.3 %collective-permute-start.7 = (bf16[64,8192]{1,0:T(8,128)(2,1)}, bf16[64,8192]{1,0:T(8,128)(2,1)}, u32[]{:S(2)}, u32[]{:S(2)}) collective-permute-start(bf16[64,8192]{1,0:T(8,128)(2,1)} %copy-done.15), channel_id=1, source_target_pairs={{0,3},{1,0},{2,1},{3,2},{4,7},{5,4},{6,5},{7,6},{8,11},{9,8},{10,9... | collective-permute-start | bytes 3145736 | tf_op jit(solution)/shard_map/ppermute | solution.py:304
  80.1 24.4 %collective-permute-start.6 = (bf16[64,8192]{1,0:T(8,128)(2,1)}, bf16[64,8192]{1,0:T(8,128)(2,1)}, u32[]{:S(2)}, u32[]{:S(2)}) collective-permute-start(bf16[64,8192]{1,0:T(8,128)(2,1)} %copy-done.14), channel_id=1, source_target_pairs={{0,2},{1,3},{2,0},{3,1},{4,6},{5,7},{6,4},{7,5},{8,10},{9,11},{10,... | collective-permute-start | bytes 3145736 | tf_op jit(solution)/shard_map/ppermute | solution.py:304
  80.6 48.8 %collective-permute-start.5 = (bf16[64,8192]{1,0:T(8,128)(2,1)S(1)}, bf16[64,8192]{1,0:T(8,128)(2,1)}, u32[]{:S(2)}, u32[]{:S(2)}) collective-permute-start(bf16[64,8192]{1,0:T(8,128)(2,1)S(1)} %get-tuple-element.19), channel_id=1, source_target_pairs={{0,1},{1,2},{2,3},{3,0},{4,5},{5,6},{6,7},{7,4},{8,9},{9,10},{10,1... | collective-permute-start | bytes 3145736 | tf_op jit(solution)/shard_map/ppermute | solution.py:304
  90.7 4.2 %collective-permute-start.12 = (f32[104,256]{1,0:T(8,128)S(1)}, f32[104,256]{1,0:T(8,128)S(1)}, u32[]{:S(2)}, u32[]{:S(2)}) collective-permute-start(f32[104,256]{1,0:T(8,128)S(1)} %convert_reduce_fusion), channel_id=1, source_target_pairs={{0,4},{4,0},{1,5},{5,1},{2,6},{6,2},{3,7},{7,3},{8,12},{12,8},{9,1... | collective-permute-start | bytes 319496 | tf_op jit(solution)/shard_map/ppermute | solution.py:241

commit v2 on v0

v2 whole, which is shorter than its diff:
```python
import math
import jax
import jax.numpy as jnp
import numpy as np
from jax import lax
from jax.experimental import pallas as pl
from jax.experimental.pallas import tpu as pltpu
from jax.sharding import Mesh
from jax.sharding import PartitionSpec as P

HIGH = lax.Precision.HIGHEST
F32 = jnp.float32
BF16 = jnp.bfloat16
LOG2E = 1.4426950408889634
PTS = ("y", "z", "core")
NN = (((1,), (0,)), ((), ()))
NT = (((1,), (1,)), ((), ()))
TN = (((0,), (0,)), ((), ()))
LIMIT = 24 * 1024 * 1024


def bdot(left, right, dims=NN):
    return lax.dot_general(left, right, dims, preferred_element_type=F32)


def fdot(left, right, dims=NN):
    return lax.dot_general(left, right, dims, precision=HIGH, preferred_element_type=F32)


def slice_weights(logits):
    rows, cols = logits.shape
    expo = jnp.exp2(logits).reshape(rows // 64, 64, cols)
    weights = expo * (1.0 / jnp.sum(expo, axis=1, keepdims=True))
    return weights.reshape(rows, cols)


def start_rows(pairs, sems, cuts):
    waits = []
    for k, (lo, hi) in enumerate(cuts):
        copies = [
            pltpu.make_async_copy(src.at[lo:hi, :], dst.at[lo:hi, :], sems.at[j, k])
            for j, (src, dst) in enumerate(pairs)
        ]
        for copy in copies:
            copy.start()
        waits.append(copies)
    return waits


def pool_kernel(
    cuts, sub, me, sharp, x_hbm, u_hbm, wmid, ws, wfx, wout,
    mine_ref, rest_ref, ab_ref, mq, x, u, pay, nacc, sems,
):
    waits = start_rows(((x_hbm, x), (u_hbm, u)), sems, cuts)
    for h in range(2):
        full = bdot(ws[h], wmid[32 * h : 32 * h + 32, :], TN) * (LOG2E / sharp[h])
        high = full.astype(BF16)
        mq[64 * h : 64 * h + 64, :] = high
        mq[128 + 64 * h : 192 + 64 * h, :] = (full - high.astype(F32)).astype(BF16)
    ab_ref[...] = jnp.zeros_like(ab_ref)
    nacc[...] = jnp.zeros_like(nacc)
    for (first, last), copies in zip(cuts, waits):
        for copy in copies:
            copy.wait()
        for lo in range(first, last, sub):
            xs = x[lo : lo + sub, :]
            both = bdot(mq[...], xs, NT)
            weights = slice_weights(both[:128] + both[128:])
            total = weights[:, :128]
            for tile in range(1, sub // 128):
                total = total + weights[:, 128 * tile : 128 * tile + 128]
            nacc[...] += total
            weights_b = weights.astype(BF16)
            ab_ref[:, :256] += bdot(weights_b, xs)
            ab_ref[:, 256:] += bdot(weights_b, u[lo : lo + sub, :])
    pool = fdot(wfx[...].astype(F32), ab_ref[:, :256], NT)
    grad_out = fdot(wout[...].astype(F32), ab_ref[:, 256:], NT)
    first = lax.broadcasted_iota(jnp.int32, (32, 128), 1) < 64
    pay[0:32, :] = jnp.where(first, pool[:32], pool[32:])
    pay[32:64, :] = jnp.where(first, grad_out[:32], grad_out[32:])
    norm = fdot(jnp.ones((16, 128), F32), nacc[...], NT)
    top = lax.broadcasted_iota(jnp.int32, (16, 128), 0) == 0
    pay[64:80, :] = jnp.where(top, norm, 0.0)
    split_rows(me[1], pay, mine_ref, rest_ref)


def split_rows(core, value, mine, rest):
    half = mine.shape[0]
    mine[...] = value[pl.ds(pl.multiple_of(core * half, 8), half), :]
    rest[...] = value[pl.ds(pl.multiple_of((1 - core) * half, 8), half), :]


def token_part(pay, h, qkv):
    lanes = slice(64 * h, 64 * h + 64)
    root = 1.0 / math.sqrt(32.0)
    norm = pay[64:65, lanes]
    token = pay[0:32, lanes] / norm
    grad_so = pay[32:64, lanes]
    maps = jnp.concatenate([qkv[h, 0], qkv[h, 1], qkv[h, 2]], axis=1)
    proj = fdot(maps, token, TN)
    query, key, value = proj[:32], proj[32:64], proj[64:]
    expo = jnp.exp(fdot(key, query, TN) * root)
    prob = expo / jnp.sum(expo, axis=0, keepdims=True)
    so = fdot(value, prob)
    grad_prob = fdot(value, grad_so, TN)
    grad_value = fdot(grad_so, prob, NT)
    grad_score = prob * (grad_prob - jnp.sum(prob * grad_prob, axis=0, keepdims=True)) * root
    grad_query = fdot(key, grad_score)
    grad_key = fdot(query, grad_score, NT)
    grads = jnp.concatenate([grad_query, grad_key, grad_value], axis=0)
    attn = fdot(token, grads, NT)
    grad_token = fdot(maps, grads)
    grad_pool = (grad_token / norm).astype(BF16)
    grad_norm = -jnp.sum(grad_token * token, axis=0, keepdims=True) / norm
    return so.astype(BF16), grad_pool, grad_norm, attn


def centre(block):
    rows, cols = block.shape
    heads = block.reshape(rows // 64, 64, cols)
    return (heads - jnp.mean(heads, axis=1, keepdims=True)).reshape(rows, cols)


def split3(value):
    high = value.astype(BF16)
    rest = value - high.astype(F32)
    mid = rest.astype(BF16)
    return high, mid, (rest - mid.astype(F32)).astype(BF16)


def token_kernel(
    me, sharp, half, other, qkv, ws, wmid, wfx, wout, pack, attn_ref, mu_ref, mx_ref, gn_ref, pay,
):
    rows = half.shape[0]
    pay[pl.ds(pl.multiple_of(me[1] * rows, 8), rows), :] = half[...]
    pay[pl.ds(pl.multiple_of((1 - me[1]) * rows, 8), rows), :] = other[...]
    pack[0:80, :] = jnp.zeros((80, 256), BF16)
    pack[80:144, :] = wfx[...]
    pack[144:208, :] = wmid[...]
    pack[208:272, :] = wout[...]
    pack[272:336, :] = jnp.zeros((64, 256), BF16)
    for h in range(2):
        feat = slice(32 * h, 32 * h + 32)
        so, grad_pool, grad_norm, attn = token_part(pay, h, qkv)
        for j in range(3):
            attn_ref[h, j] = attn[:, 32 * j : 32 * j + 32]
        pack[feat, 64 * h : 64 * h + 64] = so
        pack[feat, 128 + 64 * h : 192 + 64 * h] = grad_pool
        pack[272 + 32 * h : 304 + 32 * h, 64 * h : 64 * h + 64] = ws[h]
        inv = 1.0 / (jnp.zeros((1, 64), F32) + sharp[h])
        parts = split3(grad_norm) + split3(inv)
        rows = [p for p in parts] + [jnp.zeros((10, 64), BF16)]
        pack[64:80, 64 * h : 64 * h + 64] = jnp.concatenate(rows, axis=0)
    mu, mx, _, gn = unpack_maps(pack, wfx[...], wout[...])
    mu_ref[...] = mu
    mx_ref[...] = mx
    gn_ref[...] = gn


def unpack_maps(pack, wfx, wout):
    pick = lax.broadcasted_iota(jnp.int32, (16, 256), 0)
    lane = lax.broadcasted_iota(jnp.int32, (16, 256), 1)
    first = jnp.where(lane < 128, 0, 3)
    chosen = jnp.where((pick >= first) & (pick < first + 3), 1.0, 0.0).astype(BF16)
    cols = bdot(pack[64:80, 0:128], chosen, TN)
    inv = cols[:, 128:]
    gn = cols[:, :128] * inv
    mu = centre(bdot(pack[0:64, 0:128], wout, TN)) * inv[:, :1]
    mx = centre(bdot(pack[0:64, 128:256], wfx, TN)) * inv[:, :1]
    return mu.astype(BF16), mx.astype(BF16), inv, gn


def logit_grad(weights, grad_w):
    rows, cols = weights.shape
    prod = (weights * grad_w).reshape(rows // 64, 64, cols)
    mean = jnp.sum(prod, axis=1, keepdims=True)
    grad = prod - weights.reshape(rows // 64, 64, cols) * mean
    return grad.reshape(rows, cols).astype(BF16)


def weight_kernel(
    scale, sub, unroll, me, wmid, ws, pack, ab, mq, mu, mx, gn, x, u, mine, rest, grads_ref, maps, gacc,
):
    points=x.shape[0]
    maps[0:256, :] = mq[...]
    maps[256:384, :] = mx[...]
    gacc[...] = jnp.zeros_like(gacc)
    def one(lo):
        here=pl.ds(lo,sub)
        xs = x[here, :]
        both = bdot(maps[...], xs, NT)
        weights = slice_weights(both[:128] + both[128:256])
        grad_w = both[256:] + bdot(mu[...], u[here, :], NT) + gn[:, :1]
        gacc[...] += bdot(logit_grad(weights, grad_w), xs)
    n=points//sub
    def body(i,_):
        for j in range(unroll): one(pl.multiple_of((i*unroll+j)*sub,sub))
        return 0
    if unroll==n: body(0,0)
    else: lax.fori_loop(0,n//unroll,body,0)
    so = pack[0:64, 0:128].astype(F32)
    grad_pool = pack[0:64, 128:256].astype(F32)
    grads_ref[0:64, :] = fdot(grad_pool, ab[:, :256])
    for h in range(2):
        grads_ref[64 + 32 * h : 96 + 32 * h, :] = scale * fdot(
            ws[h].astype(F32), gacc[64 * h : 64 * h + 64, :]
        )
    grads_ref[128:192, :] = scale * fdot(so, ab[:, 256:])
    score = scale * fdot(wmid[...].astype(F32), gacc[...], NT)
    first = lax.broadcasted_iota(jnp.int32, (32, 128), 1) < 64
    score = jnp.where(first, score[:32], score[32:])
    grads_ref[192:208, :128] = score[:16]
    grads_ref[192:208, 128:] = score[16:]
    split_rows(me[1], grads_ref, mine, rest)

def input_kernel(
    sub, unroll, me, p0, p1, p2, p3, x, u, out0, out1, out2, out3,
    qx, mu, gn, wc, wcr,
):
    points = out0.shape[1]
    for g, pack in enumerate((p0, p1, p2, p3)):
        rows = slice(128 * g, 128 * g + 128)
        wfx = pack[80:144, :]
        wmid = pack[144:208, :]
        score_map = pack[272:336, 0:128]
        mu_g, mx_g, inv, gn_g = unpack_maps(pack, wfx, pack[208:272, :])
        full = bdot(score_map, wmid, TN) * (LOG2E * inv[:, :1])
        high = full.astype(BF16)
        qx[rows, :] = high
        qx[512 + 128 * g : 640 + 128 * g, :] = (full - high.astype(F32)).astype(BF16)
        qx[1024 + 128 * g : 1152 + 128 * g, :] = mx_g
        mu[rows, :] = mu_g
        gn[rows, :] = gn_g
        wc[:, rows] = bdot(wmid, score_map, TN).astype(BF16)
        wc[:, 512 + 128 * g : 640 + 128 * g] = bdot(wfx, pack[0:64, 128:256], TN).astype(BF16)
    for k in range(4):
        group = lax.rem(me[0] + k, 4)
        wcr[64 * k : 64 * k + 64, :] = wc[pl.ds(pl.multiple_of(group * 64, 64), 64), :]
    def one(lo):
        here = pl.ds(pl.multiple_of(me[0] * points + lo, sub), sub)
        both = bdot(qx[...], x[here, :], NT)
        weights = slice_weights(both[:512] + both[512:1024])
        grad_w = both[1024:] + bdot(mu[...], u[here, :], NT) + gn[:, :1]
        pair = jnp.concatenate([logit_grad(weights, grad_w), weights.astype(BF16)], axis=0)
        out = bdot(wcr[...], pair).astype(BF16)
        for k, ref in enumerate((out0, out1, out2, out3)):
            ref[:, pl.ds(lo,sub)] = out[64 * k : 64 * k + 64]
    n=points//sub
    def body(i,_):
        for j in range(unroll): one(pl.multiple_of((i*unroll+j)*sub,sub))
        return 0
    if unroll==n: body(0,0)
    else: lax.fori_loop(0,n//unroll,body,0)

SMEM = pl.BlockSpec(memory_space=pltpu.SMEM)
VM = pl.BlockSpec(memory_space=pltpu.VMEM)
HB = pl.BlockSpec(memory_space=pltpu.HBM)
PARAMS = pltpu.CompilerParams(vmem_limit_bytes=LIMIT)


def cost(flops):
    return pl.CostEstimate(flops=flops, bytes_accessed=1 << 23, transcendentals=0)


def first_pass(me, sharp, x, u, wmid, ws, wfx, wout, chunks=4, sub=256):
    points = x.shape[0]
    size = points // chunks
    cuts = [(size * i, size * i + size) for i in range(chunks)]

    def kernel(*refs):
        pool_kernel(cuts, sub, *refs)

    return pl.pallas_call(
        kernel,
        in_specs=[SMEM, SMEM, HB, HB, VM, VM, VM, VM],
        out_specs=[VM] * 6,
        out_shape=[
            jax.ShapeDtypeStruct((40, 128), F32),
            jax.ShapeDtypeStruct((40, 128), F32),
            jax.ShapeDtypeStruct((128, 512), F32),
            jax.ShapeDtypeStruct((256, 256), BF16),
            jax.ShapeDtypeStruct(x.shape, BF16),
            jax.ShapeDtypeStruct(u.shape, BF16),
        ],
        scratch_shapes=[
            pltpu.VMEM((80, 128), F32),
            pltpu.VMEM((128, 128), F32),
            pltpu.SemaphoreType.DMA((2, len(cuts))),
        ],
        compiler_params=PARAMS,
        cost_estimate=cost(1 << 33),
        name="pool_pass",
    )(me, sharp, x, u, wmid, ws, wfx, wout)


def token_pass(me, sharp, half, other, qkv, ws, wmid, wfx, wout):
    return pl.pallas_call(
        token_kernel,
        in_specs=[SMEM, SMEM] + [VM] * 7,
        out_specs=[VM] * 5,
        out_shape=[
            jax.ShapeDtypeStruct((336, 256), BF16),
            jax.ShapeDtypeStruct((2, 3, 32, 32), F32),
            jax.ShapeDtypeStruct((128, 256), BF16),
            jax.ShapeDtypeStruct((128, 256), BF16),
            jax.ShapeDtypeStruct((128, 128), F32),
        ],
        scratch_shapes=[pltpu.VMEM((80, 128), F32)],
        compiler_params=PARAMS,
        name="token_pass",
    )(me, sharp, half, other, qkv, ws, wmid, wfx, wout)


def weight_pass(me, scale, wmid, ws, pack, ab, mq, mu, mx, gn, x, u, sub=512, unroll=8):
    def kernel(*refs):
        weight_kernel(scale, sub, unroll, *refs)

    return pl.pallas_call(
        kernel,
        in_specs=[SMEM] + [VM] * 10,
        out_specs=[VM] * 2,
        out_shape=[jax.ShapeDtypeStruct((104, 256), F32)] * 2,
        scratch_shapes=[
            pltpu.VMEM((208, 256), F32),
            pltpu.VMEM((384, 256), BF16),
            pltpu.VMEM((128, 256), F32),
        ],
        compiler_params=PARAMS,
        cost_estimate=cost(1 << 33),
        name="weight_pass",
    )(me, wmid, ws, pack, ab, mq, mu, mx, gn, x, u)


def input_pass(me, packs, x, u, sub=512, unroll=4):
    points = x.shape[0] // 4

    def kernel(*refs):
        input_kernel(sub, unroll, *refs)

    return pl.pallas_call(
        kernel,
        in_specs=[SMEM] + [VM] * 6,
        out_specs=[VM] * 4,
        out_shape=[jax.ShapeDtypeStruct((64, points), BF16)] * 4,
        scratch_shapes=[
            pltpu.VMEM((1536, 256), BF16),
            pltpu.VMEM((512, 256), BF16),
            pltpu.VMEM((512, 128), F32),
            pltpu.VMEM((256, 1024), BF16),
            pltpu.VMEM((256, 1024), BF16),
        ],
        compiler_params=PARAMS,
        cost_estimate=cost(1 << 33),
        name="input_pass",
    )(me, *packs, x, u)


def final_kernel(me, half, other, part0, part1, part2, part3, fx, mid, out, score, grad, grads, sems):
    copies = []
    for k, part in enumerate((part0, part1, part2, part3)):
        group = lax.rem(me[0] + 4 - k, 4)
        size = part.shape[1]
        place = grad.at[:, pl.ds(pl.multiple_of(group * size, size), size)]
        copies.append(pltpu.make_async_copy(part, place, sems.at[k]))
        copies[-1].start()
    rows = half.shape[0]
    grads[pl.ds(pl.multiple_of(me[1] * rows, 8), rows), :] = half[...]
    grads[pl.ds(pl.multiple_of((1 - me[1]) * rows, 8), rows), :] = other[...]
    fx[...] = grads[0:64, :]
    mid[...] = grads[64:128, :]
    out[...] = grads[128:192, :]
    for h in range(2):
        for j in range(2):
            score[h, 16 * j : 16 * j + 16, :] = grads[
                192:208, 128 * j + 64 * h : 128 * j + 64 * h + 64
            ]
    for copy in copies:
        copy.wait()


def final_pass(me, half, other, parts):
    size = parts[0].shape[1]
    flat = jax.ShapeDtypeStruct((64, 256), F32)
    return pl.pallas_call(
        final_kernel,
        in_specs=[SMEM] + [VM] * 6,
        out_specs=[VM] * 4 + [HB],
        out_shape=[flat, flat, flat]
        + [
            jax.ShapeDtypeStruct((2, 32, 64), F32),
            jax.ShapeDtypeStruct((64, 4 * size), BF16),
        ],
        scratch_shapes=[pltpu.VMEM((208, 256), F32), pltpu.SemaphoreType.DMA((4,))],
        compiler_params=PARAMS,
        name="final_pass",
    )(me, half, other, *parts)


def core_swap(value):
    return lax.ppermute(value, "core", [(0, 1), (1, 0)])


def y_sum(value):
    parts = [
        lax.ppermute(value, "y", [(i, i ^ k) for i in range(4)]).astype(F32) for k in range(1, 4)
    ]
    return (value.astype(F32) + parts[0]) + (parts[1] + parts[2])


def z_sum(value):
    sent = jnp.broadcast_to(value[None], (8,) + value.shape)
    got = lax.all_to_all(sent, "z", 0, 0).astype(F32)
    total = got[0]
    for part in range(1, 8):
        total = total + got[part]
    return total


def shifted(value, k):
    return lax.ppermute(value, "head", [(i, (i + k) % 4) for i in range(4)])


def per_device(x, u, wfx, wmid, ws, sharp, qkv, wout):
    points = x.shape[0]
    scale = 1.0 / math.sqrt(points * 64)
    me = jnp.stack([lax.axis_index("head"), lax.axis_index("core")]).astype(jnp.int32)
    wfx = wfx.T
    wmid = wmid.T
    held = [
        pltpu.with_memory_space_constraint(v, pltpu.HBM) for v in (sharp, x, u, wmid, ws, wfx, wout)
    ]
    mine, rest, ab, mq, x, u = first_pass(me, *held)
    half = z_sum(y_sum(mine + core_swap(rest)))
    pack, attn, mu, mx, gn = token_pass(
        me, sharp, half, core_swap(half), qkv, ws, wmid, wfx, wout
    )
    packs = [pack] + [shifted(pack, k) for k in (1, 2, 3)]
    mine, rest = weight_pass(me, scale, wmid, ws, pack, ab, mq, mu, mx, gn, x, u)
    mine, rest, packs = lax.optimization_barrier((mine, rest, packs))
    half = y_sum((mine + core_swap(rest)).astype(BF16)).astype(BF16)
    parts = input_pass(me, packs, x, u)
    half, parts = lax.optimization_barrier((half, parts))
    parts = [parts[0]] + [shifted(parts[k], k) for k in (1, 2, 3)]
    half = z_sum(half)
    fx, mid, out, score, grad = final_pass(me, half, core_swap(half), parts)
    return grad.T, fx.T, mid.T, score, attn, out


def solution(mesh):
    fine = Mesh(np.asarray(mesh.devices).reshape(4, 8, 2, 4), PTS + ("head",))
    in_specs = (
        P(PTS, None),
        P(PTS, None),
        P(None, "head"),
        P(None, "head"),
        P("head", None, None),
        P("head"),
        P("head", None, None, None),
        P("head", None),
    )
    out_specs = (
        P(PTS, "head"),
        P(None, "head"),
        P(None, "head"),
        P("head", None, None),
        P("head", None, None, None),
        P("head", None),
    )
    return jax.shard_map(
        per_device, mesh=fine, in_specs=in_specs, out_specs=out_specs, check_vma=False
    )
```

time: 577 us -> 87.1 us (0.15)
  blocking collectives: 496 us -> 16.1 us
  matrix products: 44.7 us -> 0 us
  starting transfers between devices: 0.08 us -> 28.7 us
  Pallas kernels: 0 us -> 23.2 us
  waiting for transfers between devices: 0.04 us -> 16.8 us
  between operations: 15.8 us -> 0.96 us
  local copies, waits for them, and re-layouts: 13.1 us -> 0.83 us
    psum x2 -> x0, blocking collectives: 496 us -> none  [the longest x1 250 us: reduce_slices(): pool, norm = lax.psum((pool_part, norm_part), 'pts')]
    dot_general x31 -> x0, matrix products: 44.7 us -> none  [the longest x13 28 us: batched_product(): return jnp.dot(left, right, preferred_element_type=jnp.float32)]
    ppermute x0 -> x16, starting transfers between devices: none -> 25.2 us  [the longest x4 9.92 us: core_swap(): return lax.ppermute(value, 'core', [(0, 1), (1, 0)])]
    pallas_call x0 -> x5, Pallas kernels: none -> 23.2 us  [the longest x1 6.57 us: first_pass(): pl.pallas_call(kernel, in_specs=[SMEM, SMEM, HB, HB, VM, VM, VM, VM], out...]
    all_to_all x0 -> x1, blocking collectives: none -> 16.1 us  [z_sum(): got = lax.all_to_all(sent, 'z', 0, 0).astype(F32)]
    unnamed x21 -> x12, local copies, waits for them, and re-layouts: 10.3 us -> 0.03 us
    all_to_all x0 -> x1, waiting for transfers between devices: none -> 9.64 us  [z_sum(): got = lax.all_to_all(sent, 'z', 0, 0).astype(F32)]
    ppermute x0 -> x16, waiting for transfers between devices: none -> 7.12 us  [the longest x4 3.59 us: core_swap(): return lax.ppermute(value, 'core', [(0, 1), (1, 0)])]
  transfers between devices with their start and end apart: 2 -> 17, of which waited for: 0 -> 8; matrix products, arithmetic and copies ran while one was open for 1% -> 0% of each run, Pallas kernels for 0% -> 13%
where the time goes in v2:
time: 87.1 us; the launch traced here: 86.8 us
  starting transfers between devices  28.7 us (33%)
  Pallas kernels  23.2 us (27%)
  waiting for transfers between devices  16.8 us (19%)
  blocking collectives  16.1 us (18%)
  between operations  0.96 us (1%)
    all_to_all x1, blocking collectives, z_sum(): got = lax.all_to_all(sent, 'z', 0, 0).astype(F32)  16.1 us
    ppermute x4, starting transfers between devices, core_swap(): return lax.ppermute(value, 'core', [(0, 1), (1, 0)])  9.92 us
    all_to_all x1, waiting for transfers between devices, z_sum(): got = lax.all_to_all(sent, 'z', 0, 0).astype(F32)  9.64 us
    ppermute x6, starting transfers between devices, shifted(): return lax.ppermute(value, 'head', [(i, (i + k) % 4) for i in range(4)])  9.33 us
    pallas_call x1, Pallas kernels, first_pass(): pl.pallas_call(kernel, in_specs=[SMEM, SMEM, HB, HB, VM, VM, VM, VM], out...  6.57 us
    ppermute x6, starting transfers between devices, y_sum(): lax.ppermute(value, 'y', [(i, i ^ k) for i in range(4)]).astype(F32)  5.99 us
    pallas_call x1, Pallas kernels, weight_pass(): pl.pallas_call(kernel, in_specs=[SMEM] + [VM] * 10, out_specs=[VM] * 2, o...  5.73 us
    pallas_call x1, Pallas kernels, input_pass(): pl.pallas_call(kernel, in_specs=[SMEM] + [VM] * 6, out_specs=[VM] * 4, ou...  5.21 us
  transfers between devices with their start and end apart: 17, of which 8 were waited for; matrix products, arithmetic and copies ran while one was open for 0% of the time, Pallas kernels for 13%

profile of v2, /device:TPU:1, one launch (start us, length us, event | category | flops | bytes accessed | tf_op | source)
XLA Modules:
  0.0 86.8 jit_solution(7202973001192418256)
XLA Ops:
  0.6 0.1 pad_add_fusion.refs_0_.me
  0.7 0.0 copy-start.4
  0.7 0.0 copy-start.5
  0.7 6.6 %pool_pass.1 = (f32[40,128]{1,0:T(8,128)S(1)}, f32[40,128]{1,0:T(8,128)S(1)}, f32[128,512]{1,0:T(8,128)S(1)}, bf16[256,256]{1,0:T(8,128)(2,1)S(1)}, bf16[8192,25...) custom-call(s32[2]{0:T(128)S(1)} %pad_add_fusion.refs_0_.me, f32[2]{0:T(128)} %sharp.1, bf16[8192,256]{1,0:T(8,128)(2,1)} %refs_2_.2, ...), custom_call_target="tpu_custom_call" | custom-call | flops 8589934592 | bytes 8388608 | tf_op jit(solution)/shard_map/pool_pass/pallas_call | solution.py:273
  7.3 3.3 %collective-permute-start = (f32[40,128]{1,0:T(8,128)S(1)}, f32[40,128]{1,0:T(8,128)S(1)}, u32[]{:S(2)}, u32[]{:S(2)}) collective-permute-start(f32[40,128]{1,0:T(8,128)S(1)} %get-tuple-element.40), channel_id=1, source_target_pairs={{0,4},{4,0},{1,5},{5,1},{2,6},{6,2},{3,7},{7,3},{8,12},{12,8},{9,1... | collective-permute-start | bytes 61448 | tf_op jit(solution)/shard_map/ppermute | solution.py:400
  10.7 0.8 collective-permute-done
  11.5 1.2 %collective-permute-start.2 = (f32[40,128]{1,0:T(8,128)S(1)}, f32[40,128]{1,0:T(8,128)S(1)}, u32[]{:S(2)}, u32[]{:S(2)}) collective-permute-start(f32[40,128]{1,0:T(8,128)S(1)} %add.78), channel_id=1, source_target_pairs={{0,128},{64,192},{128,0},{192,64},{1,129},{65,193},{129,1},{193,65... | collective-permute-start | bytes 61448 | tf_op jit(solution)/shard_map/ppermute | solution.py:405
  12.7 0.8 collective-permute-start.3
  13.5 0.7 collective-permute-start.1
  14.2 1.5 %collective-permute-done.2 = f32[40,128]{1,0:T(8,128)S(1)} collective-permute-done((f32[40,128]{1,0:T(8,128)S(1)}, f32[40,128]{1,0:T(8,128)S(1)}, u32[]{:S(2)}, u32[]{:S(2)}) %collective-permute-start.2) | collective-permute-done | bytes 20512 | tf_op jit(solution)/shard_map/ppermute | solution.py:405
  15.6 1.1 %collective-permute-done.3 = f32[40,128]{1,0:T(8,128)S(1)} collective-permute-done((f32[40,128]{1,0:T(8,128)S(1)}, f32[40,128]{1,0:T(8,128)S(1)}, u32[]{:S(2)}, u32[]{:S(2)}) %collective-permute-start.3) | collective-permute-done | bytes 20512 | tf_op jit(solution)/shard_map/ppermute | solution.py:405
  16.7 0.0 collective-permute-done.1
  16.8 16.1 %all_to_all.10 = f32[8,40,128]{2,1,0:T(8,128)S(1)} all-to-all(f32[8,40,128]{2,1,0:T(8,128)S(1)} %broadcast_in_dim.4), channel_id=1, replica_groups=mesh['y'=4,'z'=8,'core'=2,'head'=4] {'z'}, dimensions={0} | all-to-all | bytes 327680 | tf_op jit(solution)/shard_map/all_to_all | solution.py:412
  32.9 3.2 %collective-permute-start.4 = (f32[40,128]{1,0:T(8,128)S(1)}, f32[40,128]{1,0:T(8,128)S(1)}, u32[]{:S(2)}, u32[]{:S(2)}) collective-permute-start(f32[40,128]{1,0:T(8,128)S(1)} %fusion.1.half), channel_id=1, source_target_pairs={{0,4},{4,0},{1,5},{5,1},{2,6},{6,2},{3,7},{7,3},{8,12},{12,8},{9,1... | collective-permute-start | bytes 61448 | tf_op jit(solution)/shard_map/ppermute | solution.py:400
  36.1 0.8 collective-permute-done.4.other
  37.0 0.0 copy-done
  37.0 0.0 copy-done.4
  37.0 3.4 %token_pass.1 = (bf16[336,256]{1,0:T(8,128)(2,1)S(1)}, f32[2,3,32,32]{3,2,1,0:T(8,128)}, bf16[128,256]{1,0:T(8,128)(2,1)S(1)}, bf16[128,256]{1,0:T(8,128)(2,1)S(1)}, f32[128,128]{1,0:T(8,128)S(1)}) custom-call(s32[2]{0:T(128)S(1)} %pad_add_fusion.refs_0_.me, f32[2]{0:T(128)S(1)} %copy-done.5, f32[40,128]{1,0:T(8,128)S(1)} %fusion.1.half, ...), custom_call_target="tpu_custom_call" | custom-call | tf_op jit(solution)/shard_map/token_pass/pallas_call | solution.py:297
  40.5 1.2 %collective-permute-start.5 = (bf16[336,256]{1,0:T(8,128)(2,1)S(1)}, bf16[336,256]{1,0:T(8,128)(2,1)S(1)}, u32[]{:S(2)}, u32[]{:S(2)}) collective-permute-start(bf16[336,256]{1,0:T(8,128)(2,1)S(1)} %get-tuple-element.53.refs_3_.refs_1_), channel_id=1, source_target_pairs={{0,1},{1,2},{2,3},{3,0},{4,5},{5,6},{6,7},{7,4},{8,9},{9,10},{10,1... | collective-permute-start | bytes 516104 | tf_op jit(solution)/shard_map/ppermute | solution.py:420
  41.7 2.5 %collective-permute-start.6 = (bf16[336,256]{1,0:T(8,128)(2,1)S(1)}, bf16[336,256]{1,0:T(8,128)(2,1)S(1)}, u32[]{:S(2)}, u32[]{:S(2)}) collective-permute-start(bf16[336,256]{1,0:T(8,128)(2,1)S(1)} %get-tuple-element.53.refs_3_.refs_1_), channel_id=1, source_target_pairs={{0,2},{1,3},{2,0},{3,1},{4,6},{5,7},{6,4},{7,5},{8,10},{9,11},{10,... | collective-permute-start | bytes 516104 | tf_op jit(solution)/shard_map/ppermute | solution.py:420
  44.1 1.1 %collective-permute-start.7 = (bf16[336,256]{1,0:T(8,128)(2,1)S(1)}, bf16[336,256]{1,0:T(8,128)(2,1)S(1)}, u32[]{:S(2)}, u32[]{:S(2)}) collective-permute-start(bf16[336,256]{1,0:T(8,128)(2,1)S(1)} %get-tuple-element.53.refs_3_.refs_1_), channel_id=1, source_target_pairs={{0,3},{1,0},{2,1},{3,2},{4,7},{5,4},{6,5},{7,6},{8,11},{9,8},{10,9... | collective-permute-start | bytes 516104 | tf_op jit(solution)/shard_map/ppermute | solution.py:420
  45.3 5.7 %weight_pass.1 = (f32[104,256]{1,0:T(8,128)S(1)}, f32[104,256]{1,0:T(8,128)S(1)}) custom-call(s32[2]{0:T(128)S(1)} %pad_add_fusion.refs_0_.me, bf16[64,256]{1,0:T(8,128)(2,1)S(1)} %bitcast.15, bf16[2,32,64]{2,1,0:T(8,128)(2,1)S(1)} %copy-done.4, bf16[336,256]{1,0:T(8,128)(2,1)S(1)} %get-tuple-element.53.refs_3_.refs_1_, ...), custom_call_target="tpu_custom_call" | custom-call | flops 8589934592 | bytes 8388608 | tf_op jit(solution)/shard_map/weight_pass/pallas_call | solution.py:318
  51.0 0.0 collective-permute-done.5.refs_2_
  51.0 0.9 %collective-permute-done.6.refs_3_ = bf16[336,256]{1,0:T(8,128)(2,1)S(1)} collective-permute-done((bf16[336,256]{1,0:T(8,128)(2,1)S(1)}, bf16[336,256]{1,0:T(8,128)(2,1)S(1)}, u32[]{:S(2)}, u32[]{:S(2)}) %collective-permute-start.6) | collective-permute-done | bytes 172064 | tf_op jit(solution)/shard_map/ppermute | solution.py:420
  52.0 0.0 collective-permute-done.7.refs_4_
  52.0 1.2 %collective-permute-start.8 = (f32[104,256]{1,0:T(8,128)S(1)}, f32[104,256]{1,0:T(8,128)S(1)}, u32[]{:S(2)}, u32[]{:S(2)}) collective-permute-start(f32[104,256]{1,0:T(8,128)S(1)} %get-tuple-element.52), channel_id=1, source_target_pairs={{0,4},{4,0},{1,5},{5,1},{2,6},{6,2},{3,7},{7,3},{8,12},{12,8},{9,1... | collective-permute-start | bytes 319496 | tf_op jit(solution)/shard_map/ppermute | solution.py:400
  53.1 1.0 %collective-permute-done.8 = f32[104,256]{1,0:T(8,128)S(1)} collective-permute-done((f32[104,256]{1,0:T(8,128)S(1)}, f32[104,256]{1,0:T(8,128)S(1)}, u32[]{:S(2)}, u32[]{:S(2)}) %collective-permute-start.8) | collective-permute-done | bytes 106528 | tf_op jit(solution)/shard_map/ppermute | solution.py:400
  54.1 1.8 %collective-permute-start.11 = (bf16[104,256]{1,0:T(8,128)(2,1)S(1)}, bf16[104,256]{1,0:T(8,128)(2,1)S(1)}, u32[]{:S(2)}, u32[]{:S(2)}) collective-permute-start(bf16[104,256]{1,0:T(8,128)(2,1)S(1)} %add_convert_fusion.1), channel_id=1, source_target_pairs={{0,192},{64,128},{128,64},{192,0},{1,193},{65,129},{129,65},{193,1... | collective-permute-start | bytes 159752 | tf_op jit(solution)/shard_map/ppermute | solution.py:405
  55.9 0.0 collective-permute-start.10
  55.9 1.5 %collective-permute-start.9 = (bf16[104,256]{1,0:T(8,128)(2,1)S(1)}, bf16[104,256]{1,0:T(8,128)(2,1)S(1)}, u32[]{:S(2)}, u32[]{:S(2)}) collective-permute-start(bf16[104,256]{1,0:T(8,128)(2,1)S(1)} %add_convert_fusion.1), channel_id=1, source_target_pairs={{0,64},{64,0},{128,192},{192,128},{1,65},{65,1},{129,193},{193,129... | collective-permute-start | bytes 159752 | tf_op jit(solution)/shard_map/ppermute | solution.py:405
  57.5 5.2 %input_pass.1 = (bf16[64,2048]{1,0:T(8,128)(2,1)S(1)}, bf16[64,2048]{1,0:T(8,128)(2,1)S(1)}, bf16[64,2048]{1,0:T(8,128)(2,1)S(1)}, bf16[64,2048]{1,0:T(8,128)(2,1)S(1)}) custom-call(s32[2]{0:T(128)S(1)} %pad_add_fusion.refs_0_.me, bf16[336,256]{1,0:T(8,128)(2,1)S(1)} %get-tuple-element.53.refs_3_.refs_1_, ...), custom_call_target="tpu_custom_call" | custom-call | flops 8589934592 | bytes 8388608 | tf_op jit(solution)/shard_map/input_pass/pallas_call | solution.py:340
  62.7 0.0 collective-permute-done.11
  62.7 0.0 collective-permute-done.10
  62.7 0.0 collective-permute-done.9
  62.7 0.8 broadcast_in_dim.5
  63.5 3.5 %all-to-all-start.1 = ((bf16[8,104,256]{2,1,0:T(8,128)(2,1)}), bf16[8,104,256]{2,1,0:T(8,128)(2,1)S(1)}, u32[]{:S(2)}, u32[]{:S(2)}) async-start(bf16[8,104,256]{2,1,0:T(8,128)(2,1)} %broadcast_in_dim.5), calls=%async_computation.1 | async-start | bytes 851968 | tf_op jit(solution)/shard_map/all_to_all | solution.py:412
  67.0 1.1 %collective-permute-start.13 = (bf16[64,2048]{1,0:T(8,128)(2,1)S(1)}, bf16[64,2048]{1,0:T(8,128)(2,1)S(1)}, u32[]{:S(2)}, u32[]{:S(2)}) collective-permute-start(bf16[64,2048]{1,0:T(8,128)(2,1)S(1)} %get-tuple-element.63), channel_id=1, source_target_pairs={{0,1},{1,2},{2,3},{3,0},{4,5},{5,6},{6,7},{7,4},{8,9},{9,10},{10,1... | collective-permute-start | bytes 786440 | tf_op jit(solution)/shard_map/ppermute | solution.py:420
  68.1 2.1 %collective-permute-start.14 = (bf16[64,2048]{1,0:T(8,128)(2,1)S(1)}, bf16[64,2048]{1,0:T(8,128)(2,1)S(1)}, u32[]{:S(2)}, u32[]{:S(2)}) collective-permute-start(bf16[64,2048]{1,0:T(8,128)(2,1)S(1)} %get-tuple-element.64), channel_id=1, source_target_pairs={{0,2},{1,3},{2,0},{3,1},{4,6},{5,7},{6,4},{7,5},{8,10},{9,11},{10,... | collective-permute-start | bytes 786440 | tf_op jit(solution)/shard_map/ppermute | solution.py:420
  70.2 1.3 %collective-permute-start.15 = (bf16[64,2048]{1,0:T(8,128)(2,1)S(1)}, bf16[64,2048]{1,0:T(8,128)(2,1)S(1)}, u32[]{:S(2)}, u32[]{:S(2)}) collective-permute-start(bf16[64,2048]{1,0:T(8,128)(2,1)S(1)} %get-tuple-element.65), channel_id=1, source_target_pairs={{0,3},{1,0},{2,1},{3,2},{4,7},{5,4},{6,5},{7,6},{8,11},{9,8},{10,9... | collective-permute-start | bytes 786440 | tf_op jit(solution)/shard_map/ppermute | solution.py:420
  71.5 9.6 %all-to-all-done.1 = bf16[8,104,256]{2,1,0:T(8,128)(2,1)S(1)} async-done(((bf16[8,104,256]{2,1,0:T(8,128)(2,1)}), bf16[8,104,256]{2,1,0:T(8,128)(2,1)S(1)}, u32[]{:S(2)}, u32[]{:S(2)}) %all-to-all-start.1) | async-done | bytes 426016 | tf_op jit(solution)/shard_map/all_to_all | solution.py:412
  81.2 0.1 convert_element_type.27
  81.2 0.1 fusion.half
  81.3 2.2 %collective-permute-start.12 = (f32[104,256]{1,0:T(8,128)S(1)}, f32[104,256]{1,0:T(8,128)S(1)}, u32[]{:S(2)}, u32[]{:S(2)}) collective-permute-start(f32[104,256]{1,0:T(8,128)S(1)} %fusion.half), channel_id=1, source_target_pairs={{0,4},{4,0},{1,5},{5,1},{2,6},{6,2},{3,7},{7,3},{8,12},{12,8},{9,1... | collective-permute-start | bytes 319496 | tf_op jit(solution)/shard_map/ppermute | solution.py:400
  83.5 0.0 collective-permute-done.13.part1
  83.5 0.0 collective-permute-done.14.part2
  83.5 0.0 collective-permute-done.15.part3
  83.5 0.9 %collective-permute-done.12.other = f32[104,256]{1,0:T(8,128)S(1)} collective-permute-done((f32[104,256]{1,0:T(8,128)S(1)}, f32[104,256]{1,0:T(8,128)S(1)}, u32[]{:S(2)}, u32[]{:S(2)}) %collective-permute-start.12) | collective-permute-done | bytes 106528 | tf_op jit(solution)/shard_map/ppermute | solution.py:400
  84.4 2.2 %final_pass.1 = (f32[64,256]{1,0:T(8,128)}, f32[64,256]{1,0:T(8,128)}, f32[64,256]{1,0:T(8,128)}, f32[2,32,64]{2,1,0:T(8,128)}, bf16[64,8192]{1,0:T(8,128)(2,1)}) custom-call(s32[2]{0:T(128)S(1)} %pad_add_fusion.refs_0_.me, f32[104,256]{1,0:T(8,128)S(1)} %fusion.half, f32[104,256]{1,0:T(8,128)S(1)} %collective-permute-done.12.other, ...), custom_call_target="tpu_custom_call" | custom-call | tf_op jit(solution)/shard_map/final_pass/pallas_call | solution.py:384
  (14 shorter events, 0.1 us)
Async XLA Ops:
  0.7 36.3 %copy-start = (f32[2,3,32,32]{3,2,1,0:T(8,128)S(1)}, f32[2,3,32,32]{3,2,1,0:T(8,128)}, u32[]{:S(2)}) copy-start(f32[2,3,32,32]{3,2,1,0:T(8,128)} %qkv.1) | copy-start | bytes 73732
  0.7 36.3 %copy-start.1 = (bf16[256,64]{0,1:T(8,128)(2,1)S(1)}, bf16[256,64]{0,1:T(8,128)(2,1)}, u32[]{:S(2)}) copy-start(bf16[256,64]{0,1:T(8,128)(2,1)} %param.10) | copy-start | bytes 98308
  0.7 36.3 %copy-start.2 = (bf16[64,256]{1,0:T(8,128)(2,1)S(1)}, bf16[64,256]{1,0:T(8,128)(2,1)}, u32[]{:S(2)}) copy-start(bf16[64,256]{1,0:T(8,128)(2,1)} %wout.1) | copy-start | bytes 98308
  0.7 36.3 %copy-start.3 = (bf16[256,64]{0,1:T(8,128)(2,1)S(1)}, bf16[256,64]{0,1:T(8,128)(2,1)}, u32[]{:S(2)}) copy-start(bf16[256,64]{0,1:T(8,128)(2,1)} %param.11) | copy-start | bytes 98308
  0.7 36.3 %copy-start.4 = (bf16[2,32,64]{2,1,0:T(8,128)(2,1)S(1)}, bf16[2,32,64]{2,1,0:T(8,128)(2,1)}, u32[]{:S(2)}) copy-start(bf16[2,32,64]{2,1,0:T(8,128)(2,1)} %refs_2_.3) | copy-start | bytes 24580
  0.7 36.3 %copy-start.5 = (f32[2]{0:T(128)S(1)}, f32[2]{0:T(128)}, u32[]{:S(2)}) copy-start(f32[2]{0:T(128)} %sharp.1) | copy-start | bytes 28
  7.3 4.2 %collective-permute-start = (f32[40,128]{1,0:T(8,128)S(1)}, f32[40,128]{1,0:T(8,128)S(1)}, u32[]{:S(2)}, u32[]{:S(2)}) collective-permute-start(f32[40,128]{1,0:T(8,128)S(1)} %get-tuple-element.40), channel_id=1, source_target_pairs={{0,4},{4,0},{1,5},{5,1},{2,6},{6,2},{3,7},{7,3},{8,12},{12,8},{9,1... | collective-permute-start | bytes 61448 | tf_op jit(solution)/shard_map/ppermute | solution.py:400
  11.5 4.1 %collective-permute-start.2 = (f32[40,128]{1,0:T(8,128)S(1)}, f32[40,128]{1,0:T(8,128)S(1)}, u32[]{:S(2)}, u32[]{:S(2)}) collective-permute-start(f32[40,128]{1,0:T(8,128)S(1)} %add.78), channel_id=1, source_target_pairs={{0,128},{64,192},{128,0},{192,64},{1,129},{65,193},{129,1},{193,65... | collective-permute-start | bytes 61448 | tf_op jit(solution)/shard_map/ppermute | solution.py:405
  12.7 4.1 %collective-permute-start.3 = (f32[40,128]{1,0:T(8,128)S(1)}, f32[40,128]{1,0:T(8,128)S(1)}, u32[]{:S(2)}, u32[]{:S(2)}) collective-permute-start(f32[40,128]{1,0:T(8,128)S(1)} %add.78), channel_id=1, source_target_pairs={{0,192},{64,128},{128,64},{192,0},{1,193},{65,129},{129,65},{193,1... | collective-permute-start | bytes 61448 | tf_op jit(solution)/shard_map/ppermute | solution.py:405
  13.5 3.3 %collective-permute-start.1 = (f32[40,128]{1,0:T(8,128)S(1)}, f32[40,128]{1,0:T(8,128)S(1)}, u32[]{:S(2)}, u32[]{:S(2)}) collective-permute-start(f32[40,128]{1,0:T(8,128)S(1)} %add.78), channel_id=1, source_target_pairs={{0,64},{64,0},{128,192},{192,128},{1,65},{65,1},{129,193},{193,129... | collective-permute-start | bytes 61448 | tf_op jit(solution)/shard_map/ppermute | solution.py:405
  32.9 4.1 %collective-permute-start.4 = (f32[40,128]{1,0:T(8,128)S(1)}, f32[40,128]{1,0:T(8,128)S(1)}, u32[]{:S(2)}, u32[]{:S(2)}) collective-permute-start(f32[40,128]{1,0:T(8,128)S(1)} %fusion.1.half), channel_id=1, source_target_pairs={{0,4},{4,0},{1,5},{5,1},{2,6},{6,2},{3,7},{7,3},{8,12},{12,8},{9,1... | collective-permute-start | bytes 61448 | tf_op jit(solution)/shard_map/ppermute | solution.py:400
  40.5 10.6 %collective-permute-start.5 = (bf16[336,256]{1,0:T(8,128)(2,1)S(1)}, bf16[336,256]{1,0:T(8,128)(2,1)S(1)}, u32[]{:S(2)}, u32[]{:S(2)}) collective-permute-start(bf16[336,256]{1,0:T(8,128)(2,1)S(1)} %get-tuple-element.53.refs_3_.refs_1_), channel_id=1, source_target_pairs={{0,1},{1,2},{2,3},{3,0},{4,5},{5,6},{6,7},{7,4},{8,9},{9,10},{10,1... | collective-permute-start | bytes 516104 | tf_op jit(solution)/shard_map/ppermute | solution.py:420
  41.7 10.3 %collective-permute-start.6 = (bf16[336,256]{1,0:T(8,128)(2,1)S(1)}, bf16[336,256]{1,0:T(8,128)(2,1)S(1)}, u32[]{:S(2)}, u32[]{:S(2)}) collective-permute-start(bf16[336,256]{1,0:T(8,128)(2,1)S(1)} %get-tuple-element.53.refs_3_.refs_1_), channel_id=1, source_target_pairs={{0,2},{1,3},{2,0},{3,1},{4,6},{5,7},{6,4},{7,5},{8,10},{9,11},{10,... | collective-permute-start | bytes 516104 | tf_op jit(solution)/shard_map/ppermute | solution.py:420
  44.1 7.8 %collective-permute-start.7 = (bf16[336,256]{1,0:T(8,128)(2,1)S(1)}, bf16[336,256]{1,0:T(8,128)(2,1)S(1)}, u32[]{:S(2)}, u32[]{:S(2)}) collective-permute-start(bf16[336,256]{1,0:T(8,128)(2,1)S(1)} %get-tuple-element.53.refs_3_.refs_1_), channel_id=1, source_target_pairs={{0,3},{1,0},{2,1},{3,2},{4,7},{5,4},{6,5},{7,6},{8,11},{9,8},{10,9... | collective-permute-start | bytes 516104 | tf_op jit(solution)/shard_map/ppermute | solution.py:420
  52.0 2.1 %collective-permute-start.8 = (f32[104,256]{1,0:T(8,128)S(1)}, f32[104,256]{1,0:T(8,128)S(1)}, u32[]{:S(2)}, u32[]{:S(2)}) collective-permute-start(f32[104,256]{1,0:T(8,128)S(1)} %get-tuple-element.52), channel_id=1, source_target_pairs={{0,4},{4,0},{1,5},{5,1},{2,6},{6,2},{3,7},{7,3},{8,12},{12,8},{9,1... | collective-permute-start | bytes 319496 | tf_op jit(solution)/shard_map/ppermute | solution.py:400
  54.1 8.6 %collective-permute-start.11 = (bf16[104,256]{1,0:T(8,128)(2,1)S(1)}, bf16[104,256]{1,0:T(8,128)(2,1)S(1)}, u32[]{:S(2)}, u32[]{:S(2)}) collective-permute-start(bf16[104,256]{1,0:T(8,128)(2,1)S(1)} %add_convert_fusion.1), channel_id=1, source_target_pairs={{0,192},{64,128},{128,64},{192,0},{1,193},{65,129},{129,65},{193,1... | collective-permute-start | bytes 159752 | tf_op jit(solution)/shard_map/ppermute | solution.py:405
  55.9 6.7 %collective-permute-start.10 = (bf16[104,256]{1,0:T(8,128)(2,1)S(1)}, bf16[104,256]{1,0:T(8,128)(2,1)S(1)}, u32[]{:S(2)}, u32[]{:S(2)}) collective-permute-start(bf16[104,256]{1,0:T(8,128)(2,1)S(1)} %add_convert_fusion.1), channel_id=1, source_target_pairs={{0,128},{64,192},{128,0},{192,64},{1,129},{65,193},{129,1},{193,65... | collective-permute-start | bytes 159752 | tf_op jit(solution)/shard_map/ppermute | solution.py:405
  55.9 6.8 %collective-permute-start.9 = (bf16[104,256]{1,0:T(8,128)(2,1)S(1)}, bf16[104,256]{1,0:T(8,128)(2,1)S(1)}, u32[]{:S(2)}, u32[]{:S(2)}) collective-permute-start(bf16[104,256]{1,0:T(8,128)(2,1)S(1)} %add_convert_fusion.1), channel_id=1, source_target_pairs={{0,64},{64,0},{128,192},{192,128},{1,65},{65,1},{129,193},{193,129... | collective-permute-start | bytes 159752 | tf_op jit(solution)/shard_map/ppermute | solution.py:405
  63.5 17.6 %all-to-all-start.1 = ((bf16[8,104,256]{2,1,0:T(8,128)(2,1)}), bf16[8,104,256]{2,1,0:T(8,128)(2,1)S(1)}, u32[]{:S(2)}, u32[]{:S(2)}) async-start(bf16[8,104,256]{2,1,0:T(8,128)(2,1)} %broadcast_in_dim.5), calls=%async_computation.1 | async-start | bytes 851968 | tf_op jit(solution)/shard_map/all_to_all | solution.py:412
  67.0 16.5 %collective-permute-start.13 = (bf16[64,2048]{1,0:T(8,128)(2,1)S(1)}, bf16[64,2048]{1,0:T(8,128)(2,1)S(1)}, u32[]{:S(2)}, u32[]{:S(2)}) collective-permute-start(bf16[64,2048]{1,0:T(8,128)(2,1)S(1)} %get-tuple-element.63), channel_id=1, source_target_pairs={{0,1},{1,2},{2,3},{3,0},{4,5},{5,6},{6,7},{7,4},{8,9},{9,10},{10,1... | collective-permute-start | bytes 786440 | tf_op jit(solution)/shard_map/ppermute | solution.py:420
  68.1 15.3 %collective-permute-start.14 = (bf16[64,2048]{1,0:T(8,128)(2,1)S(1)}, bf16[64,2048]{1,0:T(8,128)(2,1)S(1)}, u32[]{:S(2)}, u32[]{:S(2)}) collective-permute-start(bf16[64,2048]{1,0:T(8,128)(2,1)S(1)} %get-tuple-element.64), channel_id=1, source_target_pairs={{0,2},{1,3},{2,0},{3,1},{4,6},{5,7},{6,4},{7,5},{8,10},{9,11},{10,... | collective-permute-start | bytes 786440 | tf_op jit(solution)/shard_map/ppermute | solution.py:420
  70.2 13.2 %collective-permute-start.15 = (bf16[64,2048]{1,0:T(8,128)(2,1)S(1)}, bf16[64,2048]{1,0:T(8,128)(2,1)S(1)}, u32[]{:S(2)}, u32[]{:S(2)}) collective-permute-start(bf16[64,2048]{1,0:T(8,128)(2,1)S(1)} %get-tuple-element.65), channel_id=1, source_target_pairs={{0,3},{1,0},{2,1},{3,2},{4,7},{5,4},{6,5},{7,6},{8,11},{9,8},{10,9... | collective-permute-start | bytes 786440 | tf_op jit(solution)/shard_map/ppermute | solution.py:420
  81.3 3.1 %collective-permute-start.12 = (f32[104,256]{1,0:T(8,128)S(1)}, f32[104,256]{1,0:T(8,128)S(1)}, u32[]{:S(2)}, u32[]{:S(2)}) collective-permute-start(f32[104,256]{1,0:T(8,128)S(1)} %fusion.half), channel_id=1, source_target_pairs={{0,4},{4,0},{1,5},{5,1},{2,6},{6,2},{3,7},{7,3},{8,12},{12,8},{9,1... | collective-permute-start | bytes 319496 | tf_op jit(solution)/shard_map/ppermute | solution.py:400

commit v3 on v0

v3 whole, which is shorter than its diff:
```python
import math

import jax
import jax.numpy as jnp
import numpy as np
from jax import lax
from jax.experimental import pallas as pl
from jax.experimental.pallas import tpu as pltpu
from jax.sharding import Mesh
from jax.sharding import PartitionSpec as P

F32 = jnp.float32
BF16 = jnp.bfloat16
LOG2E = 1.4426950408889634
PTS = ("y", "z", "core")
NN = (((1,), (0,)), ((), ()))
NT = (((1,), (1,)), ((), ()))
TN = (((0,), (0,)), ((), ()))
SMEM = pl.BlockSpec(memory_space=pltpu.SMEM)
VM = pl.BlockSpec(memory_space=pltpu.VMEM)
HB = pl.BlockSpec(memory_space=pltpu.HBM)
PARAMS = pltpu.CompilerParams(vmem_limit_bytes=24 * 1024 * 1024)
PACK = (144, 256)


def bdot(left, right, dims=NN):
    return lax.dot_general(left, right, dims, preferred_element_type=F32)


def halves(value):
    high = value.astype(BF16)
    return high, (value - high.astype(F32)).astype(BF16)


def edot(exact, value, dims=NN):
    high, low = halves(value)
    return bdot(exact, high, dims) + bdot(exact, low, dims)


def fdot(left, right, dims=NN):
    left_high, left_low = halves(left)
    right_high, right_low = halves(right)
    return (bdot(left_high, right_low, dims) + bdot(left_low, right_high, dims)) + bdot(
        left_high, right_high, dims
    )


def slice_weights(logits):
    expo = jnp.exp2(logits)
    return expo * (1.0 / jnp.sum(expo, axis=0, keepdims=True))


def all_weights(logits):
    rows, cols = logits.shape
    expo = jnp.exp2(logits).reshape(rows // 64, 64, cols)
    weights = expo * (1.0 / jnp.sum(expo, axis=1, keepdims=True))
    return weights.reshape(rows, cols)


def all_logit_grads(weights, grad_w):
    rows, cols = weights.shape
    weights = weights.reshape(rows // 64, 64, cols)
    prod = weights * grad_w.reshape(rows // 64, 64, cols)
    grad = prod - weights * jnp.sum(prod, axis=1, keepdims=True)
    return grad.reshape(rows, cols).astype(BF16)


def logit_grad(weights, grad_w):
    mean = jnp.sum(weights * grad_w, axis=0, keepdims=True)
    return (weights * (grad_w - mean)).astype(BF16)


def tiles(heads, cols, width):
    for h in range(heads):
        for lo in range(0, cols, width):
            yield slice(64 * h, 64 * h + 64), slice(lo, lo + width)


def row_copies(x_hbm, u_hbm, xu, sems, chunk):
    def copies(i):
        rows = pl.ds(pl.multiple_of(i * chunk, chunk), chunk)
        return [
            pltpu.make_async_copy(
                src.at[rows, :], xu.at[rows, 256 * j : 256 * j + 256], sems.at[j, i]
            )
            for j, src in enumerate((x_hbm, u_hbm))
        ]

    def start(i):
        for copy in copies(i):
            copy.start()

    def wait(i):
        for copy in copies(i):
            copy.wait()

    return start, wait


def pool_kernel(
    chunk, sub, me, sharp, x_hbm, u_hbm, wmid, ws, wfx, wout,
    mine_ref, rest_ref, ab_ref, mq, x, u, pay, nacc, sems,
):
    waits = []
    for k, lo in enumerate(range(0, x.shape[0], chunk)):
        copies = [
            pltpu.make_async_copy(src.at[lo : lo + chunk, :], dst.at[lo : lo + chunk, :], sems.at[j, k])
            for j, (src, dst) in enumerate(((x_hbm, x), (u_hbm, u)))
        ]
        for copy in copies:
            copy.start()
        waits.append(copies)
    ab_ref[...] = jnp.zeros_like(ab_ref)
    nacc[...] = jnp.zeros_like(nacc)
    for h in range(2):
        full = bdot(ws[h], wmid[32 * h : 32 * h + 32, :], TN) * (LOG2E / sharp[h])
        mq[64 * h : 64 * h + 64, :], mq[128 + 64 * h : 192 + 64 * h, :] = halves(full)
    for k, copies in enumerate(waits):
        for copy in copies:
            copy.wait()
        for lo in range(k * chunk, k * chunk + chunk, sub):
            xs = x[lo : lo + sub, :]
            both = bdot(mq[...], xs, NT)
            weights = all_weights(both[:128] + both[128:])
            total = weights[:, :128]
            for tile in range(1, sub // 128):
                total = total + weights[:, 128 * tile : 128 * tile + 128]
            nacc[...] += total
            weights_b = weights.astype(BF16)
            ab_ref[:, :256] += bdot(weights_b, xs)
            ab_ref[:, 256:] += bdot(weights_b, u[lo : lo + sub, :])
    for h in range(2):
        feat = slice(32 * h, 32 * h + 32)
        rows = slice(64 * h, 64 * h + 64)
        pay[h, 0:32, 0:64] = edot(wfx[feat, :], ab_ref[rows, :256], NT)
        pay[h, 0:32, 64:128] = edot(wout[feat, :], ab_ref[rows, 256:], NT)
        norm = edot(jnp.ones((16, 128), BF16), nacc[rows, :], NT)[:8]
        pay[h, 32:40, 0:64] = norm
        pay[h, 32:40, 64:128] = norm
    mine_ref[...] = pay[me[1]]
    rest_ref[...] = pay[1 - me[1]]


def split3(value):
    high = value.astype(BF16)
    rest = value - high.astype(F32)
    mid = rest.astype(BF16)
    return [high, mid, (rest - mid.astype(F32)).astype(BF16)]


def token_kernel(me, sharp, pay, qkv, ws, wmid, wfx, wout, pack, attn_ref):
    head = me[1]
    feat = pl.ds(pl.multiple_of(32 * head, 32), 32)
    pack[0:32, :] = wfx[feat, :]
    pack[32:64, :] = wmid[feat, :]
    pack[64:96, :] = wout[feat, :]
    pack[96:128, 128:192] = ws[head]
    pack[96:128, 192:256] = jnp.zeros((32, 64), BF16)
    pack[128:144, :] = jnp.zeros((16, 256), BF16)
    root = 1.0 / math.sqrt(32.0)
    norm = pay[32:33, 0:64]
    token = pay[0:32, 0:64] / norm
    grad_so = pay[0:32, 64:128]
    maps = jnp.concatenate([qkv[head, 0], qkv[head, 1], qkv[head, 2]], axis=1)
    proj = fdot(maps, token, TN)
    query, key, value = proj[:32], proj[32:64], proj[64:]
    expo = jnp.exp(fdot(key, query, TN) * root)
    prob = expo / jnp.sum(expo, axis=0, keepdims=True)
    so = fdot(value, prob)
    grad_prob = fdot(value, grad_so, TN)
    grad_value = fdot(grad_so, prob, NT)
    grad_score = prob * (grad_prob - jnp.sum(prob * grad_prob, axis=0, keepdims=True)) * root
    grad_query = fdot(key, grad_score)
    grad_key = fdot(query, grad_score, NT)
    grads = jnp.concatenate([grad_query, grad_key, grad_value], axis=0)
    grad_token = fdot(maps, grads)
    grad_norm = -jnp.sum(grad_token * token, axis=0, keepdims=True) / norm
    inv = 1.0 / (jnp.zeros((1, 64), F32) + sharp[head])
    pack[96:128, 0:64] = so.astype(BF16)
    pack[96:128, 64:128] = (grad_token / norm).astype(BF16)
    parts = split3(grad_norm) + split3(inv) + [jnp.zeros((10, 64), BF16)]
    pack[128:144, 0:64] = jnp.concatenate(parts, axis=0)
    attn = fdot(token, grads, NT)
    for j in range(3):
        attn_ref[j] = attn[:, 32 * j : 32 * j + 32]


def centre(block):
    return block - jnp.mean(block, axis=0, keepdims=True)


def unpack_columns(parts):
    pick = lax.broadcasted_iota(jnp.int32, (16, 256), 0)
    lane = lax.broadcasted_iota(jnp.int32, (16, 256), 1)
    first = jnp.where(lane < 128, 0, 3)
    chosen = jnp.where((pick >= first) & (pick < first + 3), 1.0, 0.0).astype(BF16)
    cols = bdot(parts, chosen, TN)
    return cols[:, 128:], cols[:, :128] * cols[:, 128:]


def weight_kernel(
    scale, sub, unroll, me, own, other, ws, wmid, ab, mq, x, u, mine, rest,
    packs, grads, maps, mu, gn, gacc,
):
    points = x.shape[0]
    packs[me[1]] = own[...]
    packs[1 - me[1]] = other[...]
    maps[0:256, :] = mq[...]
    for h in range(2):
        rows = slice(64 * h, 64 * h + 64)
        pack = packs.at[h]
        inv, gn[rows, :] = unpack_columns(pack[128:144, 0:64])
        mu_h = centre(bdot(pack[96:128, 0:64], pack[64:96, :], TN)) * inv[:, :1]
        mx_h = centre(bdot(pack[96:128, 64:128], pack[0:32, :], TN)) * inv[:, :1]
        mu[rows, :] = mu_h.astype(BF16)
        maps[256 + 64 * h : 320 + 64 * h, :] = mx_h.astype(BF16)
    gacc[...] = jnp.zeros_like(gacc)

    def body(i, _):
        for j in range(unroll):
            here = pl.ds(pl.multiple_of((i * unroll + j) * sub, sub), sub)
            xs = x[here, :]
            both = bdot(maps[...], xs, NT)
            weights = all_weights(both[:128] + both[128:256])
            grad_w = both[256:] + bdot(mu[...], u[here, :], NT) + gn[:, :1]
            gacc[...] += bdot(all_logit_grads(weights, grad_w), xs)
        return 0

    lax.fori_loop(0, points // (sub * unroll), body, 0)
    for h in range(2):
        rows = slice(64 * h, 64 * h + 64)
        lo = 32 * h
        grads[lo : lo + 32, :] = edot(packs[h, 96:128, 64:128], ab[rows, :256])
        grads[64 + lo : 96 + lo, :] = scale * edot(ws[h], gacc[rows, :])
        grads[128 + lo : 160 + lo, :] = scale * edot(packs[h, 96:128, 0:64], ab[rows, 256:])
    score = scale * edot(wmid[...], gacc[...], NT)
    first = lax.broadcasted_iota(jnp.int32, (32, 128), 1) < 64
    score = jnp.where(first, score[:32], score[32:])
    grads[192:208, :128] = score[:16]
    grads[192:208, 128:] = score[16:]
    half = mine.shape[0]
    mine[...] = grads[pl.ds(pl.multiple_of(me[1] * half, 8), half), :]
    rest[...] = grads[pl.ds(pl.multiple_of((1 - me[1]) * half, 8), half), :]


def prepare_kernel(me, *refs):
    mq, mxu, gn, wcr, packs, parts, wide, tall = refs[8:]
    for g in range(4):
        packs[g, me[1]] = refs[g][...]
        packs[g, 1 - me[1]] = refs[4 + g][...]
        for h in range(2):
            at = 128 * g + 64 * h
            parts[:, at : at + 64] = packs[g, h, 128:144, 0:64]
    inv, columns = unpack_columns(parts[...])
    gn[...] = columns
    inv = inv[:, :1]
    for g in range(4):
        for h in range(2):
            pack = packs.at[g, h]
            at = 128 * g + 64 * h
            rows = slice(at, at + 64)
            score = bdot(pack[96:128, 128:192], pack[32:64, :], TN)
            from_x = bdot(pack[96:128, 64:128], pack[0:32, :], TN)
            wide[rows, :] = score
            wide[512 + at : 576 + at, :] = from_x
            from_u = bdot(pack[96:128, 0:64], pack[64:96, :], TN)
            mq[rows, :] = (score * (LOG2E * inv[rows])).astype(BF16)
            mxu[rows, :256] = (centre(from_x) * inv[rows]).astype(BF16)
            mxu[rows, 256:] = (centre(from_u) * inv[rows]).astype(BF16)
    half = pl.multiple_of(lax.div(me[0], 2) * 128, 128)
    tall[...] = wide[:, pl.ds(half, 128)].T
    wcr[...] = tall[pl.ds(pl.multiple_of(lax.rem(me[0], 2) * 64, 64), 64), :].astype(BF16)


def input_kernel(
    chunk, sub, mq, mxu, gn, wcr, x_hbm, u_hbm, grad,
    xu, out, logits, grad_w, pair, sems, out_sems,
):
    points = xu.shape[0]

    def project(slot, at):
        logits[slot] = bdot(mq[...], xu[pl.ds(at, sub), :256], NT)
        grad_w[slot] = bdot(mxu[...], xu[pl.ds(at, sub), :], NT)

    def derive(slot, at):
        for rows, cols in tiles(8, sub, 128):
            weights = slice_weights(logits[slot, rows, cols])
            full = grad_w[slot, rows, cols] + gn[rows, :]
            pair[slot, rows, cols] = logit_grad(weights, full)
            pair[slot, 512 + rows.start : 576 + rows.start, cols] = weights.astype(BF16)

    def emit(slot, at):
        out[:, pl.ds(at, sub)] = bdot(wcr[...], pair[slot]).astype(BF16)

    def sent(i):
        cols = pl.ds(pl.multiple_of(i * chunk, chunk), chunk)
        return pltpu.make_async_copy(out.at[:, cols], grad.at[:, cols], out_sems.at[i])

    start, wait = row_copies(x_hbm, u_hbm, xu, sems, chunk)
    count, per = points // chunk, chunk // sub
    for i in range(2):
        start(i)

    def body(i, _):
        wait(i)

        @pl.when(i + 2 < count)
        def _():
            start(i + 2)

        for part in range(per):
            at = pl.multiple_of(i * chunk + part * sub, sub)
            before = pl.multiple_of(jnp.maximum(at - sub, 0), sub)
            derive((part + 1) % 2, before)
            project(part % 2, at)
            emit((part + 1) % 2, before)

        @pl.when(i > 0)
        def _():
            sent(i - 1).start()

        return 0

    lax.fori_loop(0, count, body, 0)
    derive(1, points - sub)
    emit(1, points - sub)
    sent(count - 1).start()
    for i in range(count):
        sent(i).wait()


def final_kernel(me, half, other, attn_own, attn_other, fx, mid, out, score, attn, grads):
    rows = half.shape[0]
    grads[pl.ds(pl.multiple_of(me[1] * rows, 8), rows), :] = half[...]
    grads[pl.ds(pl.multiple_of((1 - me[1]) * rows, 8), rows), :] = other[...]
    attn[me[1]] = attn_own[...]
    attn[1 - me[1]] = attn_other[...]
    fx[...] = grads[0:64, :]
    mid[...] = grads[64:128, :]
    out[...] = grads[128:192, :]
    for h in range(2):
        for j in range(2):
            score[h, 16 * j : 16 * j + 16, :] = grads[
                192:208, 128 * j + 64 * h : 128 * j + 64 * h + 64
            ]


def shape(*dims, kind=F32):
    return jax.ShapeDtypeStruct(dims, kind)


def call(kernel, name, in_specs, out_shape, scratch, args, out_specs=None, flops=None):
    cost = None
    if flops is not None:
        cost = pl.CostEstimate(flops=flops, bytes_accessed=1 << 23, transcendentals=0)
    return pl.pallas_call(
        kernel,
        in_specs=in_specs,
        out_specs=out_specs if out_specs is not None else [VM] * len(out_shape),
        out_shape=out_shape,
        scratch_shapes=scratch,
        compiler_params=PARAMS,
        cost_estimate=cost,
        name=name,
    )(*args)


def first_pass(me, sharp, x, u, wmid, ws, wfx, wout, chunk=2048, sub=256):
    points = x.shape[0]

    def kernel(*refs):
        pool_kernel(chunk, sub, *refs)

    return call(
        kernel,
        "pool_pass",
        [SMEM, SMEM, HB, HB, VM, VM, VM, VM],
        [shape(40, 128), shape(40, 128), shape(128, 512), shape(256, 256, kind=BF16)]
        + [shape(points, 256, kind=BF16)] * 2,
        [
            pltpu.VMEM((2, 40, 128), F32),
            pltpu.VMEM((128, 128), F32),
            pltpu.SemaphoreType.DMA((2, points // chunk)),
        ],
        (me, sharp, x, u, wmid, ws, wfx, wout),
        flops=1 << 33,
    )


def token_pass(me, sharp, pay, qkv, ws, wmid, wfx, wout):
    return call(
        token_kernel,
        "token_pass",
        [SMEM, SMEM] + [VM] * 6,
        [shape(*PACK, kind=BF16), shape(3, 32, 32)],
        [],
        (me, sharp, pay, qkv, ws, wmid, wfx, wout),
    )


def weight_pass(me, scale, own, other, ws, wmid, ab, mq, x, u, sub=512, unroll=8):
    def kernel(*refs):
        weight_kernel(scale, sub, unroll, *refs)

    return call(
        kernel,
        "weight_pass",
        [SMEM] + [VM] * 8,
        [shape(104, 256)] * 2,
        [
            pltpu.VMEM((2,) + PACK, BF16),
            pltpu.VMEM((208, 256), F32),
            pltpu.VMEM((384, 256), BF16),
            pltpu.VMEM((128, 256), BF16),
            pltpu.VMEM((128, 128), F32),
            pltpu.VMEM((128, 256), F32),
        ],
        (me, own, other, ws, wmid, ab, mq, x, u),
        flops=1 << 33,
    )


def prepare(me, packs, others):
    return call(
        prepare_kernel,
        "prepare",
        [SMEM] + [VM] * 8,
        [
            shape(512, 256, kind=BF16),
            shape(512, 512, kind=BF16),
            shape(512, 128),
            shape(64, 1024, kind=BF16),
        ],
        [
            pltpu.VMEM((4, 2) + PACK, BF16),
            pltpu.VMEM((16, 512), BF16),
            pltpu.VMEM((1024, 256), F32),
            pltpu.VMEM((128, 1024), F32),
        ],
        (me, *packs, *others),
        flops=1 << 31,
    )


def input_pass(maps, x, u, chunk=2048, sub=256):
    points = x.shape[0]

    def kernel(*refs):
        input_kernel(chunk, sub, *refs)

    return call(
        kernel,
        "input_pass",
        [VM] * 4 + [HB] * 2,
        shape(64, points, kind=BF16),
        [
            pltpu.VMEM((points, 512), BF16),
            pltpu.VMEM((64, points), BF16),
            pltpu.VMEM((2, 512, sub), F32),
            pltpu.VMEM((2, 512, sub), F32),
            pltpu.VMEM((2, 1024, sub), BF16),
            pltpu.SemaphoreType.DMA((2, points // chunk)),
            pltpu.SemaphoreType.DMA((points // chunk,)),
        ],
        (*maps, x, u),
        out_specs=HB,
        flops=1 << 33,
    )


def final_pass(me, half, other, attn, attn_other):
    return call(
        final_kernel,
        "final_pass",
        [SMEM] + [VM] * 4,
        [shape(64, 256)] * 3 + [shape(2, 32, 64), shape(2, 3, 32, 32)],
        [pltpu.VMEM((208, 256), F32)],
        (me, half, other, attn, attn_other),
    )


def core_swap(value):
    return lax.ppermute(value, "core", [(0, 1), (1, 0)])


def y_sum(value):
    parts = [
        lax.ppermute(value, "y", [(i, i ^ k) for i in range(4)]).astype(F32) for k in range(1, 4)
    ]
    return (value.astype(F32) + parts[0]) + (parts[1] + parts[2])


def z_sum(value, beside=None):
    sent = jnp.broadcast_to(value[None], (8,) + value.shape)
    got = lax.all_to_all(sent, "z", 0, 0)
    if beside is not None:
        got, _ = lax.optimization_barrier((got, beside))
    got = got.astype(F32)
    total = got[0]
    for part in range(1, 8):
        total = total + got[part]
    return total


def shifted(value, k):
    return lax.ppermute(value, "head", [(i, (i + k) % 4) for i in range(4)])


def per_device(x, u, wfx, wmid, ws, sharp, qkv, wout):
    points = x.shape[0]
    scale = 1.0 / math.sqrt(points * 64)
    me = jnp.stack([lax.axis_index("head"), lax.axis_index("core")]).astype(jnp.int32)
    wfx = wfx.T
    wmid = wmid.T
    held = [
        pltpu.with_memory_space_constraint(v, pltpu.HBM) for v in (sharp, x, u, wmid, ws, wfx, wout)
    ]
    mine, rest, ab, mq, x, u = first_pass(me, *held)
    pay = z_sum(y_sum(mine + core_swap(rest)))
    pack, attn = token_pass(me, sharp, pay, qkv, ws, wmid, wfx, wout)
    other = core_swap(pack)
    attn_other = core_swap(attn)
    packs = [shifted(pack, k) for k in (1, 2, 3)]
    mine, rest = weight_pass(me, scale, pack, other, ws, wmid, ab, mq, x, u)
    mine, rest, packs, attn_other = lax.optimization_barrier((mine, rest, packs, attn_other))
    half = (mine + core_swap(rest)).astype(BF16)
    others = [core_swap(p) for p in packs]
    half = y_sum(half).astype(BF16)
    maps = prepare(me, [pack] + packs, [other] + others)
    half, maps = lax.optimization_barrier((half, maps))
    grad = input_pass(maps, held[1], held[2])
    half = z_sum(half, grad)
    fx, mid, out, score, attn = final_pass(me, half, core_swap(half), attn, attn_other)
    return grad.T, fx.T, mid.T, score, attn, out


def solution(mesh):
    fine = Mesh(np.asarray(mesh.devices).reshape(4, 8, 2, 4), PTS + ("head",))
    in_specs = (
        P(PTS, None),
        P(PTS, None),
        P(None, "head"),
        P(None, "head"),
        P("head", None, None),
        P("head"),
        P("head", None, None, None),
        P("head", None),
    )
    out_specs = (
        P(PTS, "head"),
        P(None, "head"),
        P(None, "head"),
        P("head", None, None),
        P("head", None, None, None),
        P("head", None),
    )
    return jax.shard_map(
        per_device, mesh=fine, in_specs=in_specs, out_specs=out_specs, check_vma=False
    )
```

time: 577 us -> 81.1 us (0.14)
  blocking collectives: 496 us -> 16.4 us
  matrix products: 44.7 us -> 0 us
  Pallas kernels: 0 us -> 31.3 us
  starting transfers between devices: 0.08 us -> 26.4 us
  between operations: 15.8 us -> 0.86 us
  local copies, waits for them, and re-layouts: 13.1 us -> 0.84 us
    psum x2 -> x0, blocking collectives: 496 us -> none  [the longest x1 250 us: reduce_slices(): pool, norm = lax.psum((pool_part, norm_part), 'pts')]
    dot_general x31 -> x0, matrix products: 44.7 us -> none  [the longest x13 28 us: batched_product(): return jnp.dot(left, right, preferred_element_type=jnp.float32)]
    pallas_call x0 -> x6, Pallas kernels: none -> 31.3 us  [call(): pl.pallas_call(kernel, in_specs=in_specs, out_specs=out_specs if out_spec...]
    ppermute x0 -> x17, starting transfers between devices: none -> 22.9 us  [the longest x8 10.3 us: core_swap(): return lax.ppermute(value, 'core', [(0, 1), (1, 0)])]
    all_to_all x0 -> x1, blocking collectives: none -> 16.4 us  [z_sum(): got = lax.all_to_all(sent, 'z', 0, 0)]
    unnamed x21 -> x12, local copies, waits for them, and re-layouts: 10.3 us -> 0.03 us
  transfers between devices with their start and end apart: 2 -> 18, of which waited for: 0 -> 6; matrix products, arithmetic and copies ran while one was open for 1% -> 0% of each run, Pallas kernels for 0% -> 28%
where the time goes in v3:
time: 81.1 us; the launch traced here: 80.9 us
  Pallas kernels  31.3 us (39%)
  starting transfers between devices  26.4 us (33%)
  blocking collectives  16.4 us (20%)
  waiting for transfers between devices  4.8 us (6%)
  between operations  0.86 us (1%)
  local copies, waits for them, and re-layouts  0.84 us (1%)
    pallas_call x6, Pallas kernels, call(): pl.pallas_call(kernel, in_specs=in_specs, out_specs=out_specs if out_spec...  31.3 us
    all_to_all x1, blocking collectives, z_sum(): got = lax.all_to_all(sent, 'z', 0, 0)  16.4 us
    ppermute x8, starting transfers between devices, core_swap(): return lax.ppermute(value, 'core', [(0, 1), (1, 0)])  10.3 us
    ppermute x6, starting transfers between devices, y_sum(): lax.ppermute(value, 'y', [(i, i ^ k) for i in range(4)]).astype(F32)  7.8 us
    ppermute x3, starting transfers between devices, shifted(): return lax.ppermute(value, 'head', [(i, (i + k) % 4) for i in range(4)])  4.82 us
    all_to_all x1, starting transfers between devices, z_sum(): got = lax.all_to_all(sent, 'z', 0, 0)  3.46 us
    ppermute x6, waiting for transfers between devices, y_sum(): lax.ppermute(value, 'y', [(i, i ^ k) for i in range(4)]).astype(F32)  2.69 us
    ppermute x8, waiting for transfers between devices, core_swap(): return lax.ppermute(value, 'core', [(0, 1), (1, 0)])  2.1 us
  transfers between devices with their start and end apart: 18, of which 6 were waited for; matrix products, arithmetic and copies ran while one was open for 0% of the time, Pallas kernels for 28%

profile of v3, /device:TPU:1, one launch (start us, length us, event | category | flops | bytes accessed | tf_op | source)
XLA Modules:
  0.0 80.9 jit_solution(16009509462004966169)
XLA Ops:
  0.6 0.1 pad_add_fusion.refs_0_.me
  0.7 0.0 copy-start.4
  0.7 0.0 copy-start.5
  0.7 6.1 %pool_pass.1 = (f32[40,128]{1,0:T(8,128)S(1)}, f32[40,128]{1,0:T(8,128)S(1)}, f32[128,512]{1,0:T(8,128)S(1)}, bf16[256,256]{1,0:T(8,128)(2,1)S(1)}, bf16[8192,25...) custom-call(s32[2]{0:T(128)S(1)} %pad_add_fusion.refs_0_.me, f32[2]{0:T(128)} %sharp.1, bf16[8192,256]{1,0:T(8,128)(2,1)} %refs_4_.1, ...), custom_call_target="tpu_custom_call" | custom-call | flops 8589934592 | bytes 8388608 | tf_op jit(solution)/shard_map/pool_pass/pallas_call | solution.py:356
  6.9 3.3 %collective-permute-start = (f32[40,128]{1,0:T(8,128)S(1)}, f32[40,128]{1,0:T(8,128)S(1)}, u32[]{:S(2)}, u32[]{:S(2)}) collective-permute-start(f32[40,128]{1,0:T(8,128)S(1)} %get-tuple-element.38), channel_id=1, source_target_pairs={{0,4},{4,0},{1,5},{5,1},{2,6},{6,2},{3,7},{7,3},{8,12},{12,8},{9,1... | collective-permute-start | bytes 61448 | tf_op jit(solution)/shard_map/ppermute | solution.py:483
  10.2 0.8 %collective-permute-done = f32[40,128]{1,0:T(8,128)S(1)} collective-permute-done((f32[40,128]{1,0:T(8,128)S(1)}, f32[40,128]{1,0:T(8,128)S(1)}, u32[]{:S(2)}, u32[]{:S(2)}) %collective-permute-start) | collective-permute-done | bytes 20512 | tf_op jit(solution)/shard_map/ppermute | solution.py:483
  11.1 0.0 collective-permute-start.1
  11.1 2.2 %collective-permute-start.2 = (f32[40,128]{1,0:T(8,128)S(1)}, f32[40,128]{1,0:T(8,128)S(1)}, u32[]{:S(2)}, u32[]{:S(2)}) collective-permute-start(f32[40,128]{1,0:T(8,128)S(1)} %add.78), channel_id=1, source_target_pairs={{0,128},{64,192},{128,0},{192,64},{1,129},{65,193},{129,1},{193,65... | collective-permute-start | bytes 61448 | tf_op jit(solution)/shard_map/ppermute | solution.py:488
  13.2 1.7 %collective-permute-start.3 = (f32[40,128]{1,0:T(8,128)S(1)}, f32[40,128]{1,0:T(8,128)S(1)}, u32[]{:S(2)}, u32[]{:S(2)}) collective-permute-start(f32[40,128]{1,0:T(8,128)S(1)} %add.78), channel_id=1, source_target_pairs={{0,192},{64,128},{128,64},{192,0},{1,193},{65,129},{129,65},{193,1... | collective-permute-start | bytes 61448 | tf_op jit(solution)/shard_map/ppermute | solution.py:488
  14.9 0.0 collective-permute-done.1
  14.9 0.5 collective-permute-done.2
  15.4 1.7 %collective-permute-done.3 = f32[40,128]{1,0:T(8,128)S(1)} collective-permute-done((f32[40,128]{1,0:T(8,128)S(1)}, f32[40,128]{1,0:T(8,128)S(1)}, u32[]{:S(2)}, u32[]{:S(2)}) %collective-permute-start.3) | collective-permute-done | bytes 20512 | tf_op jit(solution)/shard_map/ppermute | solution.py:488
  17.1 16.4 %all_to_all.10 = f32[8,40,128]{2,1,0:T(8,128)S(1)} all-to-all(f32[8,40,128]{2,1,0:T(8,128)S(1)} %broadcast_in_dim.4), channel_id=1, replica_groups=mesh['y'=4,'z'=8,'core'=2,'head'=4] {'z'}, dimensions={0} | all-to-all | bytes 327680 | tf_op jit(solution)/shard_map/all_to_all | solution.py:495
  33.6 1.5 %token_pass.1 = (bf16[144,256]{1,0:T(8,128)(2,1)S(1)}, f32[3,32,32]{2,1,0:T(8,128)S(1)}) custom-call(s32[2]{0:T(128)S(1)} %pad_add_fusion.refs_0_.me, f32[2]{0:T(128)S(1)} %copy-done.5, f32[40,128]{1,0:T(8,128)S(1)} %fusion.1.pay, f32[2,3,32,32]{3,2,1,0:T(8,128)S(1)} %copy-done, bf16[2,32,64]{2,1,0:T(8,128)(2,1)S(1)} %copy-done.4, ...), custom_call_target="tpu_custom_call" | custom-call | tf_op jit(solution)/shard_map/token_pass/pallas_call | solution.py:356
  35.1 3.5 %collective-permute-start.4 = (bf16[144,256]{1,0:T(8,128)(2,1)S(1)}, bf16[144,256]{1,0:T(8,128)(2,1)S(1)}, u32[]{:S(2)}, u32[]{:S(2)}) collective-permute-start(bf16[144,256]{1,0:T(8,128)(2,1)S(1)} %get-tuple-element.39.refs_1_.refs_0_), channel_id=1, source_target_pairs={{0,4},{4,0},{1,5},{5,1},{2,6},{6,2},{3,7},{7,3},{8,12},{12,8},{9,1... | collective-permute-start | bytes 221192 | tf_op jit(solution)/shard_map/ppermute | solution.py:483
  38.5 1.2 %collective-permute-start.5 = (bf16[144,256]{1,0:T(8,128)(2,1)S(1)}, bf16[144,256]{1,0:T(8,128)(2,1)S(1)}, u32[]{:S(2)}, u32[]{:S(2)}) collective-permute-start(bf16[144,256]{1,0:T(8,128)(2,1)S(1)} %get-tuple-element.39.refs_1_.refs_0_), channel_id=1, source_target_pairs={{0,1},{1,2},{2,3},{3,0},{4,5},{5,6},{6,7},{7,4},{8,9},{9,10},{10,1... | collective-permute-start | bytes 221192 | tf_op jit(solution)/shard_map/ppermute | solution.py:506
  39.8 2.4 %collective-permute-start.6 = (bf16[144,256]{1,0:T(8,128)(2,1)S(1)}, bf16[144,256]{1,0:T(8,128)(2,1)S(1)}, u32[]{:S(2)}, u32[]{:S(2)}) collective-permute-start(bf16[144,256]{1,0:T(8,128)(2,1)S(1)} %get-tuple-element.39.refs_1_.refs_0_), channel_id=1, source_target_pairs={{0,2},{1,3},{2,0},{3,1},{4,6},{5,7},{6,4},{7,5},{8,10},{9,11},{10,... | collective-permute-start | bytes 221192 | tf_op jit(solution)/shard_map/ppermute | solution.py:506
  42.2 1.2 %collective-permute-start.7 = (bf16[144,256]{1,0:T(8,128)(2,1)S(1)}, bf16[144,256]{1,0:T(8,128)(2,1)S(1)}, u32[]{:S(2)}, u32[]{:S(2)}) collective-permute-start(bf16[144,256]{1,0:T(8,128)(2,1)S(1)} %get-tuple-element.39.refs_1_.refs_0_), channel_id=1, source_target_pairs={{0,3},{1,0},{2,1},{3,2},{4,7},{5,4},{6,5},{7,6},{8,11},{9,8},{10,9... | collective-permute-start | bytes 221192 | tf_op jit(solution)/shard_map/ppermute | solution.py:506
  43.4 0.9 %collective-permute-start.8 = (f32[3,32,32]{2,1,0:T(8,128)S(1)}, f32[3,32,32]{2,1,0:T(8,128)S(1)}, u32[]{:S(2)}, u32[]{:S(2)}) collective-permute-start(f32[3,32,32]{2,1,0:T(8,128)S(1)} %get-tuple-element.46.attn_own), channel_id=1, source_target_pairs={{0,4},{4,0},{1,5},{5,1},{2,6},{6,2},{3,7},{7,3},{8,12},{12,8},{9,1... | collective-permute-start | bytes 36872 | tf_op jit(solution)/shard_map/ppermute | solution.py:483
  44.3 0.0 collective-permute-done.4.refs_2_.refs_4_
  44.3 5.9 %weight_pass.1 = (f32[104,256]{1,0:T(8,128)S(1)}, f32[104,256]{1,0:T(8,128)S(1)}) custom-call(s32[2]{0:T(128)S(1)} %pad_add_fusion.refs_0_.me, bf16[144,256]{1,0:T(8,128)(2,1)S(1)} %get-tuple-element.39.refs_1_.refs_0_, bf16[144,256]{1,0:T(8,128)(2,1)S(1)} %collective-permute-done.4.refs_2_.refs_4_, bf16[2,32,64]{2,1,0:T(8,128)(2,1)S(1)} %copy-done.4, ...), custom_call_target="tpu_custom_call" | custom-call | flops 8589934592 | bytes 8388608 | tf_op jit(solution)/shard_map/weight_pass/pallas_call | solution.py:356
  50.2 0.0 collective-permute-done.8.attn_other
  50.2 0.0 collective-permute-done.5.refs_1_
  50.2 0.0 collective-permute-done.6.refs_2_
  50.2 0.0 collective-permute-done.7.refs_3_
  50.2 0.1 collective-permute-start.9
  50.3 0.5 collective-permute-start.13
  50.8 0.3 collective-permute-start.14
  51.1 0.2 collective-permute-start.15
  51.3 0.3 collective-permute-done.9
  51.6 0.1 collective-permute-start.10
  51.7 1.1 %collective-permute-start.11 = (bf16[104,256]{1,0:T(8,128)(2,1)S(1)}, bf16[104,256]{1,0:T(8,128)(2,1)S(1)}, u32[]{:S(2)}, u32[]{:S(2)}) collective-permute-start(bf16[104,256]{1,0:T(8,128)(2,1)S(1)} %add_convert_fusion.1), channel_id=1, source_target_pairs={{0,128},{64,192},{128,0},{192,64},{1,129},{65,193},{129,1},{193,65... | collective-permute-start | bytes 159752 | tf_op jit(solution)/shard_map/ppermute | solution.py:488
  52.8 0.0 collective-permute-done.13.refs_5_
  52.8 2.7 %collective-permute-start.12 = (bf16[104,256]{1,0:T(8,128)(2,1)S(1)}, bf16[104,256]{1,0:T(8,128)(2,1)S(1)}, u32[]{:S(2)}, u32[]{:S(2)}) collective-permute-start(bf16[104,256]{1,0:T(8,128)(2,1)S(1)} %add_convert_fusion.1), channel_id=1, source_target_pairs={{0,192},{64,128},{128,64},{192,0},{1,193},{65,129},{129,65},{193,1... | collective-permute-start | bytes 159752 | tf_op jit(solution)/shard_map/ppermute | solution.py:488
  55.6 0.0 collective-permute-done.14.refs_6_
  55.6 0.0 collective-permute-done.15.refs_7_
  55.6 1.4 %prepare.1 = (bf16[512,256]{1,0:T(8,128)(2,1)S(1)}, bf16[512,512]{1,0:T(8,128)(2,1)S(1)}, f32[512,128]{1,0:T(8,128)S(1)}, bf16[64,1024]{1,0:T(8,128)(2,1)S(1)}) custom-call(s32[2]{0:T(128)S(1)} %pad_add_fusion.refs_0_.me, bf16[144,256]{1,0:T(8,128)(2,1)S(1)} %get-tuple-element.39.refs_1_.refs_0_, bf16[144,256]{1,0:T(8,128)(2,1)S(1)} %collective-permute-done.5.refs_1_, ...), custom_call_target="tpu_custom_call" | custom-call | flops 2147483648 | bytes 8388608 | tf_op jit(solution)/shard_map/prepare/pallas_call | solution.py:356
  57.0 0.0 collective-permute-done.11
  57.0 0.5 collective-permute-done.12
  57.5 0.8 broadcast_in_dim.5
  58.3 3.5 %all-to-all-start.1 = ((bf16[8,104,256]{2,1,0:T(8,128)(2,1)}), bf16[8,104,256]{2,1,0:T(8,128)(2,1)S(1)}, u32[]{:S(2)}, u32[]{:S(2)}) async-start(bf16[8,104,256]{2,1,0:T(8,128)(2,1)} %broadcast_in_dim.5), calls=%async_computation.1 | async-start | bytes 851968 | tf_op jit(solution)/shard_map/all_to_all | solution.py:495
  61.8 15.2 %input_pass.1 = bf16[64,8192]{1,0:T(8,128)(2,1)} custom-call(bf16[512,256]{1,0:T(8,128)(2,1)S(1)} %get-tuple-element.56.refs_0_, bf16[512,512]{1,0:T(8,128)(2,1)S(1)} %get-tuple-element.57.refs_1_, f32[512,128]{1,0:T(8,128)S(1)} %get-tuple-element.58.refs_2_, bf16[64,1024]{1,0:T(8,128)(2,1)S(1)} %get-tuple-element.59.refs_3_, bf16[8192,256]{1,0:T(8,128)(2,1)} %refs_4_.1, ...), custom_call_target="tpu_custom_call" | custom-call | flops 8589934592 | bytes 8388608 | tf_op jit(solution)/shard_map/input_pass/pallas_call | solution.py:356
  77.0 0.0 all-to-all-done.1
  77.0 0.1 convert_element_type.27
  77.1 0.1 fusion.half
  77.1 1.5 %collective-permute-start.16 = (f32[104,256]{1,0:T(8,128)S(1)}, f32[104,256]{1,0:T(8,128)S(1)}, u32[]{:S(2)}, u32[]{:S(2)}) collective-permute-start(f32[104,256]{1,0:T(8,128)S(1)} %fusion.half), channel_id=1, source_target_pairs={{0,4},{4,0},{1,5},{5,1},{2,6},{6,2},{3,7},{7,3},{8,12},{12,8},{9,1... | collective-permute-start | bytes 319496 | tf_op jit(solution)/shard_map/ppermute | solution.py:483
  78.6 1.0 %collective-permute-done.16.other = f32[104,256]{1,0:T(8,128)S(1)} collective-permute-done((f32[104,256]{1,0:T(8,128)S(1)}, f32[104,256]{1,0:T(8,128)S(1)}, u32[]{:S(2)}, u32[]{:S(2)}) %collective-permute-start.16) | collective-permute-done | bytes 106528 | tf_op jit(solution)/shard_map/ppermute | solution.py:483
  79.6 1.3 %final_pass.1 = (f32[64,256]{1,0:T(8,128)}, f32[64,256]{1,0:T(8,128)}, f32[64,256]{1,0:T(8,128)}, f32[2,32,64]{2,1,0:T(8,128)}, f32[2,3,32,32]{3,2,1,0:T(8,128)}) custom-call(s32[2]{0:T(128)S(1)} %pad_add_fusion.refs_0_.me, f32[104,256]{1,0:T(8,128)S(1)} %fusion.half, f32[104,256]{1,0:T(8,128)S(1)} %collective-permute-done.16.other, ...), custom_call_target="tpu_custom_call" | custom-call | tf_op jit(solution)/shard_map/final_pass/pallas_call | solution.py:356
  (17 shorter events, 0.1 us)
Async XLA Ops:
  0.7 32.8 %copy-start = (f32[2,3,32,32]{3,2,1,0:T(8,128)S(1)}, f32[2,3,32,32]{3,2,1,0:T(8,128)}, u32[]{:S(2)}) copy-start(f32[2,3,32,32]{3,2,1,0:T(8,128)} %qkv.1) | copy-start | bytes 73732
  0.7 32.8 %copy-start.1 = (bf16[256,64]{0,1:T(8,128)(2,1)S(1)}, bf16[256,64]{0,1:T(8,128)(2,1)}, u32[]{:S(2)}) copy-start(bf16[256,64]{0,1:T(8,128)(2,1)} %param.10) | copy-start | bytes 98308
  0.7 32.8 %copy-start.2 = (bf16[64,256]{1,0:T(8,128)(2,1)S(1)}, bf16[64,256]{1,0:T(8,128)(2,1)}, u32[]{:S(2)}) copy-start(bf16[64,256]{1,0:T(8,128)(2,1)} %wout.1) | copy-start | bytes 98308
  0.7 32.8 %copy-start.3 = (bf16[256,64]{0,1:T(8,128)(2,1)S(1)}, bf16[256,64]{0,1:T(8,128)(2,1)}, u32[]{:S(2)}) copy-start(bf16[256,64]{0,1:T(8,128)(2,1)} %param.11) | copy-start | bytes 98308
  0.7 32.8 %copy-start.4 = (bf16[2,32,64]{2,1,0:T(8,128)(2,1)S(1)}, bf16[2,32,64]{2,1,0:T(8,128)(2,1)}, u32[]{:S(2)}) copy-start(bf16[2,32,64]{2,1,0:T(8,128)(2,1)} %refs_3_.3) | copy-start | bytes 24580
  0.7 32.8 %copy-start.5 = (f32[2]{0:T(128)S(1)}, f32[2]{0:T(128)}, u32[]{:S(2)}) copy-start(f32[2]{0:T(128)} %sharp.1) | copy-start | bytes 28
  6.9 4.2 %collective-permute-start = (f32[40,128]{1,0:T(8,128)S(1)}, f32[40,128]{1,0:T(8,128)S(1)}, u32[]{:S(2)}, u32[]{:S(2)}) collective-permute-start(f32[40,128]{1,0:T(8,128)S(1)} %get-tuple-element.38), channel_id=1, source_target_pairs={{0,4},{4,0},{1,5},{5,1},{2,6},{6,2},{3,7},{7,3},{8,12},{12,8},{9,1... | collective-permute-start | bytes 61448 | tf_op jit(solution)/shard_map/ppermute | solution.py:483
  11.1 3.9 %collective-permute-start.1 = (f32[40,128]{1,0:T(8,128)S(1)}, f32[40,128]{1,0:T(8,128)S(1)}, u32[]{:S(2)}, u32[]{:S(2)}) collective-permute-start(f32[40,128]{1,0:T(8,128)S(1)} %add.78), channel_id=1, source_target_pairs={{0,64},{64,0},{128,192},{192,128},{1,65},{65,1},{129,193},{193,129... | collective-permute-start | bytes 61448 | tf_op jit(solution)/shard_map/ppermute | solution.py:488
  11.1 4.4 %collective-permute-start.2 = (f32[40,128]{1,0:T(8,128)S(1)}, f32[40,128]{1,0:T(8,128)S(1)}, u32[]{:S(2)}, u32[]{:S(2)}) collective-permute-start(f32[40,128]{1,0:T(8,128)S(1)} %add.78), channel_id=1, source_target_pairs={{0,128},{64,192},{128,0},{192,64},{1,129},{65,193},{129,1},{193,65... | collective-permute-start | bytes 61448 | tf_op jit(solution)/shard_map/ppermute | solution.py:488
  13.2 3.8 %collective-permute-start.3 = (f32[40,128]{1,0:T(8,128)S(1)}, f32[40,128]{1,0:T(8,128)S(1)}, u32[]{:S(2)}, u32[]{:S(2)}) collective-permute-start(f32[40,128]{1,0:T(8,128)S(1)} %add.78), channel_id=1, source_target_pairs={{0,192},{64,128},{128,64},{192,0},{1,193},{65,129},{129,65},{193,1... | collective-permute-start | bytes 61448 | tf_op jit(solution)/shard_map/ppermute | solution.py:488
  35.1 9.2 %collective-permute-start.4 = (bf16[144,256]{1,0:T(8,128)(2,1)S(1)}, bf16[144,256]{1,0:T(8,128)(2,1)S(1)}, u32[]{:S(2)}, u32[]{:S(2)}) collective-permute-start(bf16[144,256]{1,0:T(8,128)(2,1)S(1)} %get-tuple-element.39.refs_1_.refs_0_), channel_id=1, source_target_pairs={{0,4},{4,0},{1,5},{5,1},{2,6},{6,2},{3,7},{7,3},{8,12},{12,8},{9,1... | collective-permute-start | bytes 221192 | tf_op jit(solution)/shard_map/ppermute | solution.py:483
  38.5 11.6 %collective-permute-start.5 = (bf16[144,256]{1,0:T(8,128)(2,1)S(1)}, bf16[144,256]{1,0:T(8,128)(2,1)S(1)}, u32[]{:S(2)}, u32[]{:S(2)}) collective-permute-start(bf16[144,256]{1,0:T(8,128)(2,1)S(1)} %get-tuple-element.39.refs_1_.refs_0_), channel_id=1, source_target_pairs={{0,1},{1,2},{2,3},{3,0},{4,5},{5,6},{6,7},{7,4},{8,9},{9,10},{10,1... | collective-permute-start | bytes 221192 | tf_op jit(solution)/shard_map/ppermute | solution.py:506
  39.8 10.4 %collective-permute-start.6 = (bf16[144,256]{1,0:T(8,128)(2,1)S(1)}, bf16[144,256]{1,0:T(8,128)(2,1)S(1)}, u32[]{:S(2)}, u32[]{:S(2)}) collective-permute-start(bf16[144,256]{1,0:T(8,128)(2,1)S(1)} %get-tuple-element.39.refs_1_.refs_0_), channel_id=1, source_target_pairs={{0,2},{1,3},{2,0},{3,1},{4,6},{5,7},{6,4},{7,5},{8,10},{9,11},{10,... | collective-permute-start | bytes 221192 | tf_op jit(solution)/shard_map/ppermute | solution.py:506
  42.2 8.0 %collective-permute-start.7 = (bf16[144,256]{1,0:T(8,128)(2,1)S(1)}, bf16[144,256]{1,0:T(8,128)(2,1)S(1)}, u32[]{:S(2)}, u32[]{:S(2)}) collective-permute-start(bf16[144,256]{1,0:T(8,128)(2,1)S(1)} %get-tuple-element.39.refs_1_.refs_0_), channel_id=1, source_target_pairs={{0,3},{1,0},{2,1},{3,2},{4,7},{5,4},{6,5},{7,6},{8,11},{9,8},{10,9... | collective-permute-start | bytes 221192 | tf_op jit(solution)/shard_map/ppermute | solution.py:506
  43.4 6.8 %collective-permute-start.8 = (f32[3,32,32]{2,1,0:T(8,128)S(1)}, f32[3,32,32]{2,1,0:T(8,128)S(1)}, u32[]{:S(2)}, u32[]{:S(2)}) collective-permute-start(f32[3,32,32]{2,1,0:T(8,128)S(1)} %get-tuple-element.46.attn_own), channel_id=1, source_target_pairs={{0,4},{4,0},{1,5},{5,1},{2,6},{6,2},{3,7},{7,3},{8,12},{12,8},{9,1... | collective-permute-start | bytes 36872 | tf_op jit(solution)/shard_map/ppermute | solution.py:483
  50.2 1.4 %collective-permute-start.9 = (f32[104,256]{1,0:T(8,128)S(1)}, f32[104,256]{1,0:T(8,128)S(1)}, u32[]{:S(2)}, u32[]{:S(2)}) collective-permute-start(f32[104,256]{1,0:T(8,128)S(1)} %get-tuple-element.48), channel_id=1, source_target_pairs={{0,4},{4,0},{1,5},{5,1},{2,6},{6,2},{3,7},{7,3},{8,12},{12,8},{9,1... | collective-permute-start | bytes 319496 | tf_op jit(solution)/shard_map/ppermute | solution.py:483
  50.3 2.5 %collective-permute-start.13 = (bf16[144,256]{1,0:T(8,128)(2,1)S(1)}, bf16[144,256]{1,0:T(8,128)(2,1)S(1)}, u32[]{:S(2)}, u32[]{:S(2)}) collective-permute-start(bf16[144,256]{1,0:T(8,128)(2,1)S(1)} %collective-permute-done.5.refs_1_), channel_id=1, source_target_pairs={{0,4},{4,0},{1,5},{5,1},{2,6},{6,2},{3,7},{7,3},{8,12},{12,8},{9,1... | collective-permute-start | bytes 221192 | tf_op jit(solution)/shard_map/ppermute | solution.py:483
  50.8 4.8 %collective-permute-start.14 = (bf16[144,256]{1,0:T(8,128)(2,1)S(1)}, bf16[144,256]{1,0:T(8,128)(2,1)S(1)}, u32[]{:S(2)}, u32[]{:S(2)}) collective-permute-start(bf16[144,256]{1,0:T(8,128)(2,1)S(1)} %collective-permute-done.6.refs_2_), channel_id=1, source_target_pairs={{0,4},{4,0},{1,5},{5,1},{2,6},{6,2},{3,7},{7,3},{8,12},{12,8},{9,1... | collective-permute-start | bytes 221192 | tf_op jit(solution)/shard_map/ppermute | solution.py:483
  51.1 4.5 %collective-permute-start.15 = (bf16[144,256]{1,0:T(8,128)(2,1)S(1)}, bf16[144,256]{1,0:T(8,128)(2,1)S(1)}, u32[]{:S(2)}, u32[]{:S(2)}) collective-permute-start(bf16[144,256]{1,0:T(8,128)(2,1)S(1)} %collective-permute-done.7.refs_3_), channel_id=1, source_target_pairs={{0,4},{4,0},{1,5},{5,1},{2,6},{6,2},{3,7},{7,3},{8,12},{12,8},{9,1... | collective-permute-start | bytes 221192 | tf_op jit(solution)/shard_map/ppermute | solution.py:483
  51.6 5.3 %collective-permute-start.10 = (bf16[104,256]{1,0:T(8,128)(2,1)S(1)}, bf16[104,256]{1,0:T(8,128)(2,1)S(1)}, u32[]{:S(2)}, u32[]{:S(2)}) collective-permute-start(bf16[104,256]{1,0:T(8,128)(2,1)S(1)} %add_convert_fusion.1), channel_id=1, source_target_pairs={{0,64},{64,0},{128,192},{192,128},{1,65},{65,1},{129,193},{193,129... | collective-permute-start | bytes 159752 | tf_op jit(solution)/shard_map/ppermute | solution.py:488
  51.7 5.2 %collective-permute-start.11 = (bf16[104,256]{1,0:T(8,128)(2,1)S(1)}, bf16[104,256]{1,0:T(8,128)(2,1)S(1)}, u32[]{:S(2)}, u32[]{:S(2)}) collective-permute-start(bf16[104,256]{1,0:T(8,128)(2,1)S(1)} %add_convert_fusion.1), channel_id=1, source_target_pairs={{0,128},{64,192},{128,0},{192,64},{1,129},{65,193},{129,1},{193,65... | collective-permute-start | bytes 159752 | tf_op jit(solution)/shard_map/ppermute | solution.py:488
  52.8 4.7 %collective-permute-start.12 = (bf16[104,256]{1,0:T(8,128)(2,1)S(1)}, bf16[104,256]{1,0:T(8,128)(2,1)S(1)}, u32[]{:S(2)}, u32[]{:S(2)}) collective-permute-start(bf16[104,256]{1,0:T(8,128)(2,1)S(1)} %add_convert_fusion.1), channel_id=1, source_target_pairs={{0,192},{64,128},{128,64},{192,0},{1,193},{65,129},{129,65},{193,1... | collective-permute-start | bytes 159752 | tf_op jit(solution)/shard_map/ppermute | solution.py:488
  58.3 18.7 %all-to-all-start.1 = ((bf16[8,104,256]{2,1,0:T(8,128)(2,1)}), bf16[8,104,256]{2,1,0:T(8,128)(2,1)S(1)}, u32[]{:S(2)}, u32[]{:S(2)}) async-start(bf16[8,104,256]{2,1,0:T(8,128)(2,1)} %broadcast_in_dim.5), calls=%async_computation.1 | async-start | bytes 851968 | tf_op jit(solution)/shard_map/all_to_all | solution.py:495
  77.1 2.5 %collective-permute-start.16 = (f32[104,256]{1,0:T(8,128)S(1)}, f32[104,256]{1,0:T(8,128)S(1)}, u32[]{:S(2)}, u32[]{:S(2)}) collective-permute-start(f32[104,256]{1,0:T(8,128)S(1)} %fusion.half), channel_id=1, source_target_pairs={{0,4},{4,0},{1,5},{5,1},{2,6},{6,2},{3,7},{7,3},{8,12},{12,8},{9,1... | collective-permute-start | bytes 319496 | tf_op jit(solution)/shard_map/ppermute | solution.py:483

commit v4 on v3

--- a/solution.py
+++ b/solution.py
@@ -21,6 +21,7 @@
 HB = pl.BlockSpec(memory_space=pltpu.HBM)
 PARAMS = pltpu.CompilerParams(vmem_limit_bytes=24 * 1024 * 1024)
 PACK = (144, 256)
+EARLY = 1024
 
 
 def bdot(left, right, dims=NN):
@@ -74,27 +75,6 @@
     for h in range(heads):
         for lo in range(0, cols, width):
             yield slice(64 * h, 64 * h + 64), slice(lo, lo + width)
-
-
-def row_copies(x_hbm, u_hbm, xu, sems, chunk):
-    def copies(i):
-        rows = pl.ds(pl.multiple_of(i * chunk, chunk), chunk)
-        return [
-            pltpu.make_async_copy(
-                src.at[rows, :], xu.at[rows, 256 * j : 256 * j + 256], sems.at[j, i]
-            )
-            for j, src in enumerate((x_hbm, u_hbm))
-        ]
-
-    def start(i):
-        for copy in copies(i):
-            copy.start()
-
-    def wait(i):
-        for copy in copies(i):
-            copy.wait()
-
-    return start, wait
 
 
 def pool_kernel(
@@ -272,61 +252,87 @@
     wcr[...] = tall[pl.ds(pl.multiple_of(lax.rem(me[0], 2) * 64, 64), 64), :].astype(BF16)
 
 
-def input_kernel(
-    chunk, sub, mq, mxu, gn, wcr, x_hbm, u_hbm, grad,
-    xu, out, logits, grad_w, pair, sems, out_sems,
-):
-    points = xu.shape[0]
-
+def columns_stages(sub, mq, mxu, gn, wcr, x, u, out, logits, grad_w, pair):
     def project(slot, at):
-        logits[slot] = bdot(mq[...], xu[pl.ds(at, sub), :256], NT)
-        grad_w[slot] = bdot(mxu[...], xu[pl.ds(at, sub), :], NT)
-
-    def derive(slot, at):
-        for rows, cols in tiles(8, sub, 128):
+        here = pl.ds(at, sub)
+        xs = x[here, :]
+        logits[slot] = bdot(mq[...], xs, NT)
+        grad_w[slot] = bdot(mxu[:, :256], xs, NT) + bdot(mxu[:, 256:], u[here, :], NT)
+
+    def derive(slot):
+        for rows, cols in tiles(8, sub, 256):
             weights = slice_weights(logits[slot, rows, cols])
-            full = grad_w[slot, rows, cols] + gn[rows, :]
+            full = grad_w[slot, rows, cols] + gn[rows, :1]
             pair[slot, rows, cols] = logit_grad(weights, full)
             pair[slot, 512 + rows.start : 576 + rows.start, cols] = weights.astype(BF16)
 
     def emit(slot, at):
         out[:, pl.ds(at, sub)] = bdot(wcr[...], pair[slot]).astype(BF16)
 
-    def sent(i):
-        cols = pl.ds(pl.multiple_of(i * chunk, chunk), chunk)
-        return pltpu.make_async_copy(out.at[:, cols], grad.at[:, cols], out_sems.at[i])
-
-    start, wait = row_copies(x_hbm, u_hbm, xu, sems, chunk)
-    count, per = points // chunk, chunk // sub
-    for i in range(2):
-        start(i)
-
-    def body(i, _):
-        wait(i)
-
-        @pl.when(i + 2 < count)
-        def _():
-            start(i + 2)
-
-        for part in range(per):
-            at = pl.multiple_of(i * chunk + part * sub, sub)
-            before = pl.multiple_of(jnp.maximum(at - sub, 0), sub)
-            derive((part + 1) % 2, before)
-            project(part % 2, at)
-            emit((part + 1) % 2, before)
-
-        @pl.when(i > 0)
-        def _():
-            sent(i - 1).start()
-
-        return 0
-
-    lax.fori_loop(0, count, body, 0)
-    derive(1, points - sub)
-    emit(1, points - sub)
-    sent(count - 1).start()
-    for i in range(count):
-        sent(i).wait()
+    return project, derive, emit
+
+
+def early_kernel(sub, mq, mxu, gn, wcr, x, u, grad, out, logits, grad_w, pair, sem):
+    points = out.shape[1]
+    project, derive, emit = columns_stages(
+        sub, mq, mxu, gn, wcr, x, u, out, logits, grad_w, pair
+    )
+    for n in range(points // sub + 1):
+        if n > 0:
+            derive((n + 1) % 2)
+        if n < points // sub:
+            project(n % 2, n * sub)
+        if n > 0:
+            emit((n + 1) % 2, (n - 1) * sub)
+    copy = pltpu.make_async_copy(out, grad.at[:, 0:points], sem)
+    copy.start()
+    copy.wait()
+
+
+def late_kernel(
+    cuts, sub, skip, mq, mxu, gn, wcr, x_hbm, u_hbm, begun, grad,
+    x, u, out, logits, grad_w, pair, sems, out_sems,
+):
+    project, derive, emit = columns_stages(
+        sub, mq, mxu, gn, wcr, x, u, out, logits, grad_w, pair
+    )
+    loads, stores = [], []
+    for k, (lo, hi) in enumerate(cuts):
+        loads.append(
+            [
+                pltpu.make_async_copy(
+                    src.at[skip + lo : skip + hi, :], dst.at[lo:hi, :], sems.at[j, k]
+                )
+                for j, (src, dst) in enumerate(((x_hbm, x), (u_hbm, u)))
+            ]
+        )
+        stores.append(
+            pltpu.make_async_copy(out.at[:, lo:hi], grad.at[:, skip + lo : skip + hi], out_sems.at[k])
+        )
+    for copies in loads[:2]:
+        for copy in copies:
+            copy.start()
+    for k, (lo, hi) in enumerate(cuts):
+        for copy in loads[k]:
+            copy.wait()
+        if k + 2 < len(cuts):
+            for copy in loads[k + 2]:
+                copy.start()
+        for at in range(lo, hi, sub):
+            slot = (at // sub) % 2
+            if at > 0:
+                derive(1 - slot)
+            project(slot, at)
+            if at > 0:
+                emit(1 - slot, at - sub)
+        if k > 0:
+            stores[k - 1].start()
+    slot = (cuts[-1][1] // sub - 1) % 2
+    derive(slot)
+    emit(slot, cuts[-1][1] - sub)
+    stores[-1].start()
+    for store in stores:
+        store.wait()
 
 
 def final_kernel(me, half, other, attn_own, attn_other, fx, mid, out, score, attn, grads):
@@ -349,7 +355,9 @@
     return jax.ShapeDtypeStruct(dims, kind)
 
 
-def call(kernel, name, in_specs, out_shape, scratch, args, out_specs=None, flops=None):
+def call(
+    kernel, name, in_specs, out_shape, scratch, args, out_specs=None, flops=None, aliases=None
+):
     cost = None
     if flops is not None:
         cost = pl.CostEstimate(flops=flops, bytes_accessed=1 << 23, transcendentals=0)
@@ -361,6 +369,7 @@
         scratch_shapes=scratch,
         compiler_params=PARAMS,
         cost_estimate=cost,
+        input_output_aliases=aliases or {},
         name=name,
     )(*args)
 
@@ -442,29 +451,54 @@
     )
 
 
-def input_pass(maps, x, u, chunk=2048, sub=256):
-    points = x.shape[0]
-
+def stage_scratch(points, sub):
+    return [
+        pltpu.VMEM((64, points), BF16),
+        pltpu.VMEM((2, 512, sub), F32),
+        pltpu.VMEM((2, 512, sub), F32),
+        pltpu.VMEM((2, 1024, sub), BF16),
+    ]
+
+
+def early_pass(maps, x, u, points, sub=256):
     def kernel(*refs):
-        input_kernel(chunk, sub, *refs)
+        early_kernel(sub, *refs)
 
     return call(
         kernel,
-        "input_pass",
-        [VM] * 4 + [HB] * 2,
-        shape(64, points, kind=BF16),
-        [
-            pltpu.VMEM((points, 512), BF16),
-            pltpu.VMEM((64, points), BF16),
-            pltpu.VMEM((2, 512, sub), F32),
-            pltpu.VMEM((2, 512, sub), F32),
-            pltpu.VMEM((2, 1024, sub), BF16),
-            pltpu.SemaphoreType.DMA((2, points // chunk)),
-            pltpu.SemaphoreType.DMA((points // chunk,)),
-        ],
+        "early_pass",
+        [VM] * 6,
+        shape(64, x.shape[0], kind=BF16),
+        stage_scratch(points, sub) + [pltpu.SemaphoreType.DMA],
         (*maps, x, u),
         out_specs=HB,
+        flops=1 << 32,
+    )
+
+
+def late_pass(maps, x, u, begun, skip, chunk=2048, sub=256):
+    points = x.shape[0] - skip
+    marks = list(range(points, 0, -chunk))[::-1]
+    cuts = list(zip([0] + marks[:-1], marks))
+
+    def kernel(*refs):
+        late_kernel(cuts, sub, skip, *refs)
+
+    return call(
+        kernel,
+        "late_pass",
+        [VM] * 4 + [HB] * 3,
+        shape(64, x.shape[0], kind=BF16),
+        [pltpu.VMEM((points, 256), BF16)] * 2
+        + stage_scratch(points, sub)
+        + [
+            pltpu.SemaphoreType.DMA((2, len(cuts))),
+            pltpu.SemaphoreType.DMA((len(cuts),)),
+        ],
+        (*maps, x, u, begun),
+        out_specs=HB,
         flops=1 << 33,
+        aliases={6: 0},
     )
 
 
@@ -527,8 +561,9 @@
     others = [core_swap(p) for p in packs]
     half = y_sum(half).astype(BF16)
     maps = prepare(me, [pack] + packs, [other] + others)
-    half, maps = lax.optimization_barrier((half, maps))
-    grad = input_pass(maps, held[1], held[2])
+    grad = early_pass(maps, x, u, EARLY)
+    half, maps, grad = lax.optimization_barrier((half, maps, grad))
+    grad = late_pass(maps, held[1], held[2], grad, EARLY)
     half = z_sum(half, grad)
     fx, mid, out, score, attn = final_pass(me, half, core_swap(half), attn, attn_other)
     return grad.T, fx.T, mid.T, score, attn, out

time: 81.1 us -> 79.4 us (0.979)
  starting transfers between devices: 26.4 us -> 25.4 us
    ppermute x6, starting transfers between devices: 7.8 us -> 6.59 us  [y_sum(): lax.ppermute(value, 'y', [(i, i ^ k) for i in range(4)]).astype(F32)]
    ppermute x3, starting transfers between devices: 4.82 us -> 3.62 us  [shifted(): return lax.ppermute(value, 'head', [(i, (i + k) % 4) for i in range(4)])]
    ppermute x8, starting transfers between devices: 10.3 us -> 11.5 us  [core_swap(): return lax.ppermute(value, 'core', [(0, 1), (1, 0)])]
    pallas_call x6 -> x7, Pallas kernels: 31.3 us -> 30.9 us  [call(): pl.pallas_call(kernel, in_specs=in_specs, out_specs=out_specs if out_spec...]
  transfers between devices with their start and end apart: 18 -> 18, of which waited for: 6 -> 7; matrix products, arithmetic and copies ran while one was open for 0% -> 0% of each run, Pallas kernels for 28% -> 28%
where the time goes in v4:
time: 79.4 us; the launch traced here: 79.1 us
  Pallas kernels  30.9 us (39%)
  starting transfers between devices  25.4 us (32%)
  blocking collectives  16.3 us (21%)
  waiting for transfers between devices  4.48 us (6%)
  between operations  0.88 us (1%)
  local copies, waits for them, and re-layouts  0.84 us (1%)
    pallas_call x7, Pallas kernels, call(): pl.pallas_call(kernel, in_specs=in_specs, out_specs=out_specs if out_spec...  30.9 us
    all_to_all x1, blocking collectives, z_sum(): got = lax.all_to_all(sent, 'z', 0, 0)  16.3 us
    ppermute x8, starting transfers between devices, core_swap(): return lax.ppermute(value, 'core', [(0, 1), (1, 0)])  11.5 us
    ppermute x6, starting transfers between devices, y_sum(): lax.ppermute(value, 'y', [(i, i ^ k) for i in range(4)]).astype(F32)  6.59 us
    all_to_all x1, starting transfers between devices, z_sum(): got = lax.all_to_all(sent, 'z', 0, 0)  3.68 us
    ppermute x3, starting transfers between devices, shifted(): return lax.ppermute(value, 'head', [(i, (i + k) % 4) for i in range(4)])  3.62 us
    ppermute x8, waiting for transfers between devices, core_swap(): return lax.ppermute(value, 'core', [(0, 1), (1, 0)])  2.56 us
    ppermute x6, waiting for transfers between devices, y_sum(): lax.ppermute(value, 'y', [(i, i ^ k) for i in range(4)]).astype(F32)  1.89 us
  transfers between devices with their start and end apart: 18, of which 7 were waited for; matrix products, arithmetic and copies ran while one was open for 0% of the time, Pallas kernels for 28%

profile of v4, /device:TPU:1, one launch (start us, length us, event | category | flops | bytes accessed | tf_op | source)
XLA Modules:
  0.0 79.1 jit_solution(13550918637678155042)
XLA Ops:
  0.6 0.1 pad_add_fusion.refs_0_.me
  0.7 0.0 copy-start.4
  0.7 0.0 copy-start.5
  0.7 6.1 %pool_pass.1 = (f32[40,128]{1,0:T(8,128)S(1)}, f32[40,128]{1,0:T(8,128)S(1)}, f32[128,512]{1,0:T(8,128)S(1)}, bf16[256,256]{1,0:T(8,128)(2,1)S(1)}, bf16[8192,25...) custom-call(s32[2]{0:T(128)S(1)} %pad_add_fusion.refs_0_.me, f32[2]{0:T(128)} %sharp.1, bf16[8192,256]{1,0:T(8,128)(2,1)} %refs_4_.1, ...), custom_call_target="tpu_custom_call" | custom-call | flops 8589934592 | bytes 8388608 | tf_op jit(solution)/shard_map/pool_pass/pallas_call | solution.py:364
  6.9 3.3 %collective-permute-start = (f32[40,128]{1,0:T(8,128)S(1)}, f32[40,128]{1,0:T(8,128)S(1)}, u32[]{:S(2)}, u32[]{:S(2)}) collective-permute-start(f32[40,128]{1,0:T(8,128)S(1)} %get-tuple-element.39), channel_id=1, source_target_pairs={{0,4},{4,0},{1,5},{5,1},{2,6},{6,2},{3,7},{7,3},{8,12},{12,8},{9,1... | collective-permute-start | bytes 61448 | tf_op jit(solution)/shard_map/ppermute | solution.py:517
  10.2 0.8 %collective-permute-done = f32[40,128]{1,0:T(8,128)S(1)} collective-permute-done((f32[40,128]{1,0:T(8,128)S(1)}, f32[40,128]{1,0:T(8,128)S(1)}, u32[]{:S(2)}, u32[]{:S(2)}) %collective-permute-start) | collective-permute-done | bytes 20512 | tf_op jit(solution)/shard_map/ppermute | solution.py:517
  11.1 1.0 %collective-permute-start.3 = (f32[40,128]{1,0:T(8,128)S(1)}, f32[40,128]{1,0:T(8,128)S(1)}, u32[]{:S(2)}, u32[]{:S(2)}) collective-permute-start(f32[40,128]{1,0:T(8,128)S(1)} %add.78), channel_id=1, source_target_pairs={{0,192},{64,128},{128,64},{192,0},{1,193},{65,129},{129,65},{193,1... | collective-permute-start | bytes 61448 | tf_op jit(solution)/shard_map/ppermute | solution.py:522
  12.1 0.3 collective-permute-start.2
  12.4 1.9 %collective-permute-start.1 = (f32[40,128]{1,0:T(8,128)S(1)}, f32[40,128]{1,0:T(8,128)S(1)}, u32[]{:S(2)}, u32[]{:S(2)}) collective-permute-start(f32[40,128]{1,0:T(8,128)S(1)} %add.78), channel_id=1, source_target_pairs={{0,64},{64,0},{128,192},{192,128},{1,65},{65,1},{129,193},{193,129... | collective-permute-start | bytes 61448 | tf_op jit(solution)/shard_map/ppermute | solution.py:522
  14.3 0.6 collective-permute-done.3
  14.9 1.3 %collective-permute-done.2 = f32[40,128]{1,0:T(8,128)S(1)} collective-permute-done((f32[40,128]{1,0:T(8,128)S(1)}, f32[40,128]{1,0:T(8,128)S(1)}, u32[]{:S(2)}, u32[]{:S(2)}) %collective-permute-start.2) | collective-permute-done | bytes 20512 | tf_op jit(solution)/shard_map/ppermute | solution.py:522
  16.2 0.0 collective-permute-done.1
  16.2 16.3 %all_to_all.10 = f32[8,40,128]{2,1,0:T(8,128)S(1)} all-to-all(f32[8,40,128]{2,1,0:T(8,128)S(1)} %broadcast_in_dim.4), channel_id=1, replica_groups=mesh['y'=4,'z'=8,'core'=2,'head'=4] {'z'}, dimensions={0} | all-to-all | bytes 327680 | tf_op jit(solution)/shard_map/all_to_all | solution.py:529
  32.6 1.5 %token_pass.1 = (bf16[144,256]{1,0:T(8,128)(2,1)S(1)}, f32[3,32,32]{2,1,0:T(8,128)S(1)}) custom-call(s32[2]{0:T(128)S(1)} %pad_add_fusion.refs_0_.me, f32[2]{0:T(128)S(1)} %copy-done.5, f32[40,128]{1,0:T(8,128)S(1)} %fusion.1.pay, f32[2,3,32,32]{3,2,1,0:T(8,128)S(1)} %copy-done, bf16[2,32,64]{2,1,0:T(8,128)(2,1)S(1)} %copy-done.4, ...), custom_call_target="tpu_custom_call" | custom-call | tf_op jit(solution)/shard_map/token_pass/pallas_call | solution.py:364
  34.2 3.2 %collective-permute-start.4 = (bf16[144,256]{1,0:T(8,128)(2,1)S(1)}, bf16[144,256]{1,0:T(8,128)(2,1)S(1)}, u32[]{:S(2)}, u32[]{:S(2)}) collective-permute-start(bf16[144,256]{1,0:T(8,128)(2,1)S(1)} %get-tuple-element.40.refs_1_.refs_0_), channel_id=1, source_target_pairs={{0,4},{4,0},{1,5},{5,1},{2,6},{6,2},{3,7},{7,3},{8,12},{12,8},{9,1... | collective-permute-start | bytes 221192 | tf_op jit(solution)/shard_map/ppermute | solution.py:517
  37.4 2.5 %collective-permute-start.7 = (bf16[144,256]{1,0:T(8,128)(2,1)S(1)}, bf16[144,256]{1,0:T(8,128)(2,1)S(1)}, u32[]{:S(2)}, u32[]{:S(2)}) collective-permute-start(bf16[144,256]{1,0:T(8,128)(2,1)S(1)} %get-tuple-element.40.refs_1_.refs_0_), channel_id=1, source_target_pairs={{0,3},{1,0},{2,1},{3,2},{4,7},{5,4},{6,5},{7,6},{8,11},{9,8},{10,9... | collective-permute-start | bytes 221192 | tf_op jit(solution)/shard_map/ppermute | solution.py:540
  39.9 0.5 collective-permute-start.6
  40.4 0.6 collective-permute-start.5
  41.0 0.9 %collective-permute-start.8 = (f32[3,32,32]{2,1,0:T(8,128)S(1)}, f32[3,32,32]{2,1,0:T(8,128)S(1)}, u32[]{:S(2)}, u32[]{:S(2)}) collective-permute-start(f32[3,32,32]{2,1,0:T(8,128)S(1)} %get-tuple-element.47.attn_own), channel_id=1, source_target_pairs={{0,4},{4,0},{1,5},{5,1},{2,6},{6,2},{3,7},{7,3},{8,12},{12,8},{9,1... | collective-permute-start | bytes 36872 | tf_op jit(solution)/shard_map/ppermute | solution.py:517
  41.9 0.0 collective-permute-done.4.refs_2_.refs_4_
  41.9 5.7 %weight_pass.1 = (f32[104,256]{1,0:T(8,128)S(1)}, f32[104,256]{1,0:T(8,128)S(1)}) custom-call(s32[2]{0:T(128)S(1)} %pad_add_fusion.refs_0_.me, bf16[144,256]{1,0:T(8,128)(2,1)S(1)} %get-tuple-element.40.refs_1_.refs_0_, bf16[144,256]{1,0:T(8,128)(2,1)S(1)} %collective-permute-done.4.refs_2_.refs_4_, bf16[2,32,64]{2,1,0:T(8,128)(2,1)S(1)} %copy-done.4, ...), custom_call_target="tpu_custom_call" | custom-call | flops 8589934592 | bytes 8388608 | tf_op jit(solution)/shard_map/weight_pass/pallas_call | solution.py:364
  47.7 0.0 collective-permute-done.8.attn_other
  47.7 0.0 collective-permute-done.7.refs_3_
  47.7 0.0 collective-permute-done.6.refs_2_
  47.7 0.0 collective-permute-done.5.refs_1_
  47.7 0.1 collective-permute-start.13
  47.8 0.5 collective-permute-start.14
  48.3 0.3 collective-permute-start.15
  48.6 0.2 collective-permute-start.9
  48.8 0.2 collective-permute-done.13.refs_5_
  49.1 0.3 collective-permute-done.14.refs_6_
  49.3 0.2 collective-permute-done.15.refs_7_
  49.6 1.4 %prepare.1 = (bf16[512,256]{1,0:T(8,128)(2,1)S(1)}, bf16[512,512]{1,0:T(8,128)(2,1)S(1)}, f32[512,128]{1,0:T(8,128)S(1)}, bf16[64,1024]{1,0:T(8,128)(2,1)S(1)}) custom-call(s32[2]{0:T(128)S(1)} %pad_add_fusion.refs_0_.me, bf16[144,256]{1,0:T(8,128)(2,1)S(1)} %get-tuple-element.40.refs_1_.refs_0_, bf16[144,256]{1,0:T(8,128)(2,1)S(1)} %collective-permute-done.5.refs_1_, ...), custom_call_target="tpu_custom_call" | custom-call | flops 2147483648 | bytes 8388608 | tf_op jit(solution)/shard_map/prepare/pallas_call | solution.py:364
  51.0 1.1 %collective-permute-start.12 = (bf16[104,256]{1,0:T(8,128)(2,1)S(1)}, bf16[104,256]{1,0:T(8,128)(2,1)S(1)}, u32[]{:S(2)}, u32[]{:S(2)}) collective-permute-start(bf16[104,256]{1,0:T(8,128)(2,1)S(1)} %add_convert_fusion.1), channel_id=1, source_target_pairs={{0,192},{64,128},{128,64},{192,0},{1,193},{65,129},{129,65},{193,1... | collective-permute-start | bytes 159752 | tf_op jit(solution)/shard_map/ppermute | solution.py:522
  52.1 0.8 %collective-permute-start.11 = (bf16[104,256]{1,0:T(8,128)(2,1)S(1)}, bf16[104,256]{1,0:T(8,128)(2,1)S(1)}, u32[]{:S(2)}, u32[]{:S(2)}) collective-permute-start(bf16[104,256]{1,0:T(8,128)(2,1)S(1)} %add_convert_fusion.1), channel_id=1, source_target_pairs={{0,128},{64,192},{128,0},{192,64},{1,129},{65,193},{129,1},{193,65... | collective-permute-start | bytes 159752 | tf_op jit(solution)/shard_map/ppermute | solution.py:522
  52.9 1.4 %collective-permute-start.10 = (bf16[104,256]{1,0:T(8,128)(2,1)S(1)}, bf16[104,256]{1,0:T(8,128)(2,1)S(1)}, u32[]{:S(2)}, u32[]{:S(2)}) collective-permute-start(bf16[104,256]{1,0:T(8,128)(2,1)S(1)} %add_convert_fusion.1), channel_id=1, source_target_pairs={{0,64},{64,0},{128,192},{192,128},{1,65},{65,1},{129,193},{193,129... | collective-permute-start | bytes 159752 | tf_op jit(solution)/shard_map/ppermute | solution.py:522
  54.3 2.3 %early_pass.1.refs_6_ = bf16[64,8192]{1,0:T(8,128)(2,1)} custom-call(bf16[512,256]{1,0:T(8,128)(2,1)S(1)} %get-tuple-element.57.refs_0_, bf16[512,512]{1,0:T(8,128)(2,1)S(1)} %get-tuple-element.58.refs_1_, f32[512,128]{1,0:T(8,128)S(1)} %get-tuple-element.59.refs_2_, bf16[64,1024]{1,0:T(8,128)(2,1)S(1)} %get-tuple-element.60.refs_3_, ...), custom_call_target="tpu_custom_call" | custom-call | flops 4294967296 | bytes 8388608 | tf_op jit(solution)/shard_map/early_pass/pallas_call | solution.py:364
  56.7 0.0 collective-permute-done.11
  56.7 0.0 collective-permute-done.10
  56.7 0.8 %broadcast_in_dim.5 = bf16[8,104,256]{2,1,0:T(8,128)(2,1)} broadcast(bf16[104,256]{1,0:T(8,128)(2,1)S(1)} %add_convert_fusion), dimensions={1,2} | broadcast | bytes 479232 | tf_op jit(solution)/shard_map/broadcast_in_dim | solution.py:528
  57.5 3.7 %all-to-all-start.1 = ((bf16[8,104,256]{2,1,0:T(8,128)(2,1)}), bf16[8,104,256]{2,1,0:T(8,128)(2,1)S(1)}, u32[]{:S(2)}, u32[]{:S(2)}) async-start(bf16[8,104,256]{2,1,0:T(8,128)(2,1)} %broadcast_in_dim.5), calls=%async_computation.1 | async-start | bytes 851968 | tf_op jit(solution)/shard_map/all_to_all | solution.py:529
  61.2 12.6 %late_pass.1 = bf16[64,8192]{1,0:T(8,128)(2,1)} custom-call(bf16[512,256]{1,0:T(8,128)(2,1)S(1)} %get-tuple-element.57.refs_0_, bf16[512,512]{1,0:T(8,128)(2,1)S(1)} %get-tuple-element.58.refs_1_, f32[512,128]{1,0:T(8,128)S(1)} %get-tuple-element.59.refs_2_, bf16[64,1024]{1,0:T(8,128)(2,1)S(1)} %get-tuple-element.60.refs_3_, ...), custom_call_target="tpu_custom_call", output_to_operand_aliasing={{}: (6, {})} | custom-call | flops 8589934592 | bytes 8388608 | tf_op jit(solution)/shard_map/late_pass/pallas_call | solution.py:364
  73.8 0.0 all-to-all-done.1
  73.8 0.1 convert_element_type.27
  73.9 0.1 fusion.half
  74.0 2.9 %collective-permute-start.16 = (f32[104,256]{1,0:T(8,128)S(1)}, f32[104,256]{1,0:T(8,128)S(1)}, u32[]{:S(2)}, u32[]{:S(2)}) collective-permute-start(f32[104,256]{1,0:T(8,128)S(1)} %fusion.half), channel_id=1, source_target_pairs={{0,4},{4,0},{1,5},{5,1},{2,6},{6,2},{3,7},{7,3},{8,12},{12,8},{9,1... | collective-permute-start | bytes 319496 | tf_op jit(solution)/shard_map/ppermute | solution.py:517
  76.9 1.0 %collective-permute-done.16.other = f32[104,256]{1,0:T(8,128)S(1)} collective-permute-done((f32[104,256]{1,0:T(8,128)S(1)}, f32[104,256]{1,0:T(8,128)S(1)}, u32[]{:S(2)}, u32[]{:S(2)}) %collective-permute-start.16) | collective-permute-done | bytes 106528 | tf_op jit(solution)/shard_map/ppermute | solution.py:517
  77.9 1.3 %final_pass.1 = (f32[64,256]{1,0:T(8,128)}, f32[64,256]{1,0:T(8,128)}, f32[64,256]{1,0:T(8,128)}, f32[2,32,64]{2,1,0:T(8,128)}, f32[2,3,32,32]{3,2,1,0:T(8,128)}) custom-call(s32[2]{0:T(128)S(1)} %pad_add_fusion.refs_0_.me, f32[104,256]{1,0:T(8,128)S(1)} %fusion.half, f32[104,256]{1,0:T(8,128)S(1)} %collective-permute-done.16.other, ...), custom_call_target="tpu_custom_call" | custom-call | tf_op jit(solution)/shard_map/final_pass/pallas_call | solution.py:364
  (18 shorter events, 0.1 us)
Async XLA Ops:
  0.7 31.9 %copy-start = (f32[2,3,32,32]{3,2,1,0:T(8,128)S(1)}, f32[2,3,32,32]{3,2,1,0:T(8,128)}, u32[]{:S(2)}) copy-start(f32[2,3,32,32]{3,2,1,0:T(8,128)} %qkv.1) | copy-start | bytes 73732
  0.7 31.9 %copy-start.1 = (bf16[256,64]{0,1:T(8,128)(2,1)S(1)}, bf16[256,64]{0,1:T(8,128)(2,1)}, u32[]{:S(2)}) copy-start(bf16[256,64]{0,1:T(8,128)(2,1)} %param.10) | copy-start | bytes 98308
  0.7 31.9 %copy-start.2 = (bf16[64,256]{1,0:T(8,128)(2,1)S(1)}, bf16[64,256]{1,0:T(8,128)(2,1)}, u32[]{:S(2)}) copy-start(bf16[64,256]{1,0:T(8,128)(2,1)} %wout.1) | copy-start | bytes 98308
  0.7 31.9 %copy-start.3 = (bf16[256,64]{0,1:T(8,128)(2,1)S(1)}, bf16[256,64]{0,1:T(8,128)(2,1)}, u32[]{:S(2)}) copy-start(bf16[256,64]{0,1:T(8,128)(2,1)} %param.11) | copy-start | bytes 98308
  0.7 31.9 %copy-start.4 = (bf16[2,32,64]{2,1,0:T(8,128)(2,1)S(1)}, bf16[2,32,64]{2,1,0:T(8,128)(2,1)}, u32[]{:S(2)}) copy-start(bf16[2,32,64]{2,1,0:T(8,128)(2,1)} %refs_3_.3) | copy-start | bytes 24580
  0.7 31.9 %copy-start.5 = (f32[2]{0:T(128)S(1)}, f32[2]{0:T(128)}, u32[]{:S(2)}) copy-start(f32[2]{0:T(128)} %sharp.1) | copy-start | bytes 28
  6.9 4.2 %collective-permute-start = (f32[40,128]{1,0:T(8,128)S(1)}, f32[40,128]{1,0:T(8,128)S(1)}, u32[]{:S(2)}, u32[]{:S(2)}) collective-permute-start(f32[40,128]{1,0:T(8,128)S(1)} %get-tuple-element.39), channel_id=1, source_target_pairs={{0,4},{4,0},{1,5},{5,1},{2,6},{6,2},{3,7},{7,3},{8,12},{12,8},{9,1... | collective-permute-start | bytes 61448 | tf_op jit(solution)/shard_map/ppermute | solution.py:517
  11.1 3.8 %collective-permute-start.3 = (f32[40,128]{1,0:T(8,128)S(1)}, f32[40,128]{1,0:T(8,128)S(1)}, u32[]{:S(2)}, u32[]{:S(2)}) collective-permute-start(f32[40,128]{1,0:T(8,128)S(1)} %add.78), channel_id=1, source_target_pairs={{0,192},{64,128},{128,64},{192,0},{1,193},{65,129},{129,65},{193,1... | collective-permute-start | bytes 61448 | tf_op jit(solution)/shard_map/ppermute | solution.py:522
  12.1 4.1 %collective-permute-start.2 = (f32[40,128]{1,0:T(8,128)S(1)}, f32[40,128]{1,0:T(8,128)S(1)}, u32[]{:S(2)}, u32[]{:S(2)}) collective-permute-start(f32[40,128]{1,0:T(8,128)S(1)} %add.78), channel_id=1, source_target_pairs={{0,128},{64,192},{128,0},{192,64},{1,129},{65,193},{129,1},{193,65... | collective-permute-start | bytes 61448 | tf_op jit(solution)/shard_map/ppermute | solution.py:522
  12.4 3.8 %collective-permute-start.1 = (f32[40,128]{1,0:T(8,128)S(1)}, f32[40,128]{1,0:T(8,128)S(1)}, u32[]{:S(2)}, u32[]{:S(2)}) collective-permute-start(f32[40,128]{1,0:T(8,128)S(1)} %add.78), channel_id=1, source_target_pairs={{0,64},{64,0},{128,192},{192,128},{1,65},{65,1},{129,193},{193,129... | collective-permute-start | bytes 61448 | tf_op jit(solution)/shard_map/ppermute | solution.py:522
  34.2 7.8 %collective-permute-start.4 = (bf16[144,256]{1,0:T(8,128)(2,1)S(1)}, bf16[144,256]{1,0:T(8,128)(2,1)S(1)}, u32[]{:S(2)}, u32[]{:S(2)}) collective-permute-start(bf16[144,256]{1,0:T(8,128)(2,1)S(1)} %get-tuple-element.40.refs_1_.refs_0_), channel_id=1, source_target_pairs={{0,4},{4,0},{1,5},{5,1},{2,6},{6,2},{3,7},{7,3},{8,12},{12,8},{9,1... | collective-permute-start | bytes 221192 | tf_op jit(solution)/shard_map/ppermute | solution.py:517
  37.4 10.3 %collective-permute-start.7 = (bf16[144,256]{1,0:T(8,128)(2,1)S(1)}, bf16[144,256]{1,0:T(8,128)(2,1)S(1)}, u32[]{:S(2)}, u32[]{:S(2)}) collective-permute-start(bf16[144,256]{1,0:T(8,128)(2,1)S(1)} %get-tuple-element.40.refs_1_.refs_0_), channel_id=1, source_target_pairs={{0,3},{1,0},{2,1},{3,2},{4,7},{5,4},{6,5},{7,6},{8,11},{9,8},{10,9... | collective-permute-start | bytes 221192 | tf_op jit(solution)/shard_map/ppermute | solution.py:540
  39.9 7.8 %collective-permute-start.6 = (bf16[144,256]{1,0:T(8,128)(2,1)S(1)}, bf16[144,256]{1,0:T(8,128)(2,1)S(1)}, u32[]{:S(2)}, u32[]{:S(2)}) collective-permute-start(bf16[144,256]{1,0:T(8,128)(2,1)S(1)} %get-tuple-element.40.refs_1_.refs_0_), channel_id=1, source_target_pairs={{0,2},{1,3},{2,0},{3,1},{4,6},{5,7},{6,4},{7,5},{8,10},{9,11},{10,... | collective-permute-start | bytes 221192 | tf_op jit(solution)/shard_map/ppermute | solution.py:540
  40.4 7.3 %collective-permute-start.5 = (bf16[144,256]{1,0:T(8,128)(2,1)S(1)}, bf16[144,256]{1,0:T(8,128)(2,1)S(1)}, u32[]{:S(2)}, u32[]{:S(2)}) collective-permute-start(bf16[144,256]{1,0:T(8,128)(2,1)S(1)} %get-tuple-element.40.refs_1_.refs_0_), channel_id=1, source_target_pairs={{0,1},{1,2},{2,3},{3,0},{4,5},{5,6},{6,7},{7,4},{8,9},{9,10},{10,1... | collective-permute-start | bytes 221192 | tf_op jit(solution)/shard_map/ppermute | solution.py:540
  41.0 6.7 %collective-permute-start.8 = (f32[3,32,32]{2,1,0:T(8,128)S(1)}, f32[3,32,32]{2,1,0:T(8,128)S(1)}, u32[]{:S(2)}, u32[]{:S(2)}) collective-permute-start(f32[3,32,32]{2,1,0:T(8,128)S(1)} %get-tuple-element.47.attn_own), channel_id=1, source_target_pairs={{0,4},{4,0},{1,5},{5,1},{2,6},{6,2},{3,7},{7,3},{8,12},{12,8},{9,1... | collective-permute-start | bytes 36872 | tf_op jit(solution)/shard_map/ppermute | solution.py:517
  47.7 1.4 %collective-permute-start.13 = (bf16[144,256]{1,0:T(8,128)(2,1)S(1)}, bf16[144,256]{1,0:T(8,128)(2,1)S(1)}, u32[]{:S(2)}, u32[]{:S(2)}) collective-permute-start(bf16[144,256]{1,0:T(8,128)(2,1)S(1)} %collective-permute-done.5.refs_1_), channel_id=1, source_target_pairs={{0,4},{4,0},{1,5},{5,1},{2,6},{6,2},{3,7},{7,3},{8,12},{12,8},{9,1... | collective-permute-start | bytes 221192 | tf_op jit(solution)/shard_map/ppermute | solution.py:517
  47.8 1.5 %collective-permute-start.14 = (bf16[144,256]{1,0:T(8,128)(2,1)S(1)}, bf16[144,256]{1,0:T(8,128)(2,1)S(1)}, u32[]{:S(2)}, u32[]{:S(2)}) collective-permute-start(bf16[144,256]{1,0:T(8,128)(2,1)S(1)} %collective-permute-done.6.refs_2_), channel_id=1, source_target_pairs={{0,4},{4,0},{1,5},{5,1},{2,6},{6,2},{3,7},{7,3},{8,12},{12,8},{9,1... | collective-permute-start | bytes 221192 | tf_op jit(solution)/shard_map/ppermute | solution.py:517
  48.3 1.3 %collective-permute-start.15 = (bf16[144,256]{1,0:T(8,128)(2,1)S(1)}, bf16[144,256]{1,0:T(8,128)(2,1)S(1)}, u32[]{:S(2)}, u32[]{:S(2)}) collective-permute-start(bf16[144,256]{1,0:T(8,128)(2,1)S(1)} %collective-permute-done.7.refs_3_), channel_id=1, source_target_pairs={{0,4},{4,0},{1,5},{5,1},{2,6},{6,2},{3,7},{7,3},{8,12},{12,8},{9,1... | collective-permute-start | bytes 221192 | tf_op jit(solution)/shard_map/ppermute | solution.py:517
  48.6 2.4 %collective-permute-start.9 = (f32[104,256]{1,0:T(8,128)S(1)}, f32[104,256]{1,0:T(8,128)S(1)}, u32[]{:S(2)}, u32[]{:S(2)}) collective-permute-start(f32[104,256]{1,0:T(8,128)S(1)} %get-tuple-element.49), channel_id=1, source_target_pairs={{0,4},{4,0},{1,5},{5,1},{2,6},{6,2},{3,7},{7,3},{8,12},{12,8},{9,1... | collective-permute-start | bytes 319496 | tf_op jit(solution)/shard_map/ppermute | solution.py:517
  51.0 5.7 %collective-permute-start.12 = (bf16[104,256]{1,0:T(8,128)(2,1)S(1)}, bf16[104,256]{1,0:T(8,128)(2,1)S(1)}, u32[]{:S(2)}, u32[]{:S(2)}) collective-permute-start(bf16[104,256]{1,0:T(8,128)(2,1)S(1)} %add_convert_fusion.1), channel_id=1, source_target_pairs={{0,192},{64,128},{128,64},{192,0},{1,193},{65,129},{129,65},{193,1... | collective-permute-start | bytes 159752 | tf_op jit(solution)/shard_map/ppermute | solution.py:522
  52.1 4.6 %collective-permute-start.11 = (bf16[104,256]{1,0:T(8,128)(2,1)S(1)}, bf16[104,256]{1,0:T(8,128)(2,1)S(1)}, u32[]{:S(2)}, u32[]{:S(2)}) collective-permute-start(bf16[104,256]{1,0:T(8,128)(2,1)S(1)} %add_convert_fusion.1), channel_id=1, source_target_pairs={{0,128},{64,192},{128,0},{192,64},{1,129},{65,193},{129,1},{193,65... | collective-permute-start | bytes 159752 | tf_op jit(solution)/shard_map/ppermute | solution.py:522
  52.9 3.8 %collective-permute-start.10 = (bf16[104,256]{1,0:T(8,128)(2,1)S(1)}, bf16[104,256]{1,0:T(8,128)(2,1)S(1)}, u32[]{:S(2)}, u32[]{:S(2)}) collective-permute-start(bf16[104,256]{1,0:T(8,128)(2,1)S(1)} %add_convert_fusion.1), channel_id=1, source_target_pairs={{0,64},{64,0},{128,192},{192,128},{1,65},{65,1},{129,193},{193,129... | collective-permute-start | bytes 159752 | tf_op jit(solution)/shard_map/ppermute | solution.py:522
  57.5 16.3 %all-to-all-start.1 = ((bf16[8,104,256]{2,1,0:T(8,128)(2,1)}), bf16[8,104,256]{2,1,0:T(8,128)(2,1)S(1)}, u32[]{:S(2)}, u32[]{:S(2)}) async-start(bf16[8,104,256]{2,1,0:T(8,128)(2,1)} %broadcast_in_dim.5), calls=%async_computation.1 | async-start | bytes 851968 | tf_op jit(solution)/shard_map/all_to_all | solution.py:529
  74.0 3.9 %collective-permute-start.16 = (f32[104,256]{1,0:T(8,128)S(1)}, f32[104,256]{1,0:T(8,128)S(1)}, u32[]{:S(2)}, u32[]{:S(2)}) collective-permute-start(f32[104,256]{1,0:T(8,128)S(1)} %fusion.half), channel_id=1, source_target_pairs={{0,4},{4,0},{1,5},{5,1},{2,6},{6,2},{3,7},{7,3},{8,12},{12,8},{9,1... | collective-permute-start | bytes 319496 | tf_op jit(solution)/shard_map/ppermute | solution.py:517

commit v5 on v4

--- a/solution.py
+++ b/solution.py
@@ -21,7 +21,7 @@
 HB = pl.BlockSpec(memory_space=pltpu.HBM)
 PARAMS = pltpu.CompilerParams(vmem_limit_bytes=24 * 1024 * 1024)
 PACK = (144, 256)
-EARLY = 1024
+EARLY = 512
 
 
 def bdot(left, right, dims=NN):
@@ -223,8 +223,7 @@
     rest[...] = grads[pl.ds(pl.multiple_of((1 - me[1]) * half, 8), half), :]
 
 
-def prepare_kernel(me, *refs):
-    mq, mxu, gn, wcr, packs, parts, wide, tall = refs[8:]
+def prepare_maps(me, refs, mq, mxu, gn, wcr, packs, parts, wide, tall):
     for g in range(4):
         packs[g, me[1]] = refs[g][...]
         packs[g, 1 - me[1]] = refs[4 + g][...]
@@ -272,7 +271,10 @@
     return project, derive, emit
 
 
-def early_kernel(sub, mq, mxu, gn, wcr, x, u, grad, out, logits, grad_w, pair, sem):
+def early_kernel(sub, me, *refs):
+    x, u, mq, mxu, gn, wcr, grad = refs[8:15]
+    packs, parts, wide, tall, out, logits, grad_w, pair, sem = refs[15:]
+    prepare_maps(me, refs[:8], mq, mxu, gn, wcr, packs, parts, wide, tall)
     points = out.shape[1]
     project, derive, emit = columns_stages(
         sub, mq, mxu, gn, wcr, x, u, out, logits, grad_w, pair
@@ -429,28 +431,6 @@
     )
 
 
-def prepare(me, packs, others):
-    return call(
-        prepare_kernel,
-        "prepare",
-        [SMEM] + [VM] * 8,
-        [
-            shape(512, 256, kind=BF16),
-            shape(512, 512, kind=BF16),
-            shape(512, 128),
-            shape(64, 1024, kind=BF16),
-        ],
-        [
-            pltpu.VMEM((4, 2) + PACK, BF16),
-            pltpu.VMEM((16, 512), BF16),
-            pltpu.VMEM((1024, 256), F32),
-            pltpu.VMEM((128, 1024), F32),
-        ],
-        (me, *packs, *others),
-        flops=1 << 31,
-    )
-
-
 def stage_scratch(points, sub):
     return [
         pltpu.VMEM((64, points), BF16),
@@ -460,18 +440,31 @@
     ]
 
 
-def early_pass(maps, x, u, points, sub=256):
+def early_pass(me, packs, others, x, u, points, sub=256):
     def kernel(*refs):
         early_kernel(sub, *refs)
 
     return call(
         kernel,
         "early_pass",
-        [VM] * 6,
-        shape(64, x.shape[0], kind=BF16),
-        stage_scratch(points, sub) + [pltpu.SemaphoreType.DMA],
-        (*maps, x, u),
-        out_specs=HB,
+        [SMEM] + [VM] * 10,
+        [
+            shape(512, 256, kind=BF16),
+            shape(512, 512, kind=BF16),
+            shape(512, 128),
+            shape(64, 1024, kind=BF16),
+            shape(64, x.shape[0], kind=BF16),
+        ],
+        [
+            pltpu.VMEM((4, 2) + PACK, BF16),
+            pltpu.VMEM((16, 512), BF16),
+            pltpu.VMEM((1024, 256), F32),
+            pltpu.VMEM((128, 1024), F32),
+        ]
+        + stage_scratch(points, sub)
+        + [pltpu.SemaphoreType.DMA],
+        (me, *packs, *others, x, u),
+        out_specs=[VM] * 4 + [HB],
         flops=1 << 32,
     )
 
@@ -560,8 +553,7 @@
     half = (mine + core_swap(rest)).astype(BF16)
     others = [core_swap(p) for p in packs]
     half = y_sum(half).astype(BF16)
-    maps = prepare(me, [pack] + packs, [other] + others)
-    grad = early_pass(maps, x, u, EARLY)
+    *maps, grad = early_pass(me, [pack] + packs, [other] + others, x, u, EARLY)
     half, maps, grad = lax.optimization_barrier((half, maps, grad))
     grad = late_pass(maps, held[1], held[2], grad, EARLY)
     half = z_sum(half, grad)

time: 79.4 us -> 79.4 us (level)
    ppermute x3, starting transfers between devices: 3.62 us -> 4.83 us  [shifted(): return lax.ppermute(value, 'head', [(i, (i + k) % 4) for i in range(4)])]
    ppermute x8, starting transfers between devices: 11.5 us -> 10.6 us  [core_swap(): return lax.ppermute(value, 'core', [(0, 1), (1, 0)])]
    pallas_call x7 -> x6, Pallas kernels: 30.9 us -> 31.3 us  [call(): pl.pallas_call(kernel, in_specs=in_specs, out_specs=out_specs if out_spec...]
  transfers between devices with their start and end apart: 18 -> 18, of which waited for: 7 -> 5; matrix products, arithmetic and copies ran while one was open for 0% -> 0% of each run, Pallas kernels for 28% -> 28%
where the time goes in v5:
time: 79.4 us; the launch traced here: 79.2 us
  Pallas kernels  31.3 us (39%)
  starting transfers between devices  25.1 us (32%)
  blocking collectives  16.1 us (20%)
  waiting for transfers between devices  4.73 us (6%)
  between operations  0.85 us (1%)
  local copies, waits for them, and re-layouts  0.84 us (1%)
    pallas_call x6, Pallas kernels, call(): pl.pallas_call(kernel, in_specs=in_specs, out_specs=out_specs if out_spec...  31.3 us
    all_to_all x1, blocking collectives, z_sum(): got = lax.all_to_all(sent, 'z', 0, 0)  16.1 us
    ppermute x8, starting transfers between devices, core_swap(): return lax.ppermute(value, 'core', [(0, 1), (1, 0)])  10.6 us
    ppermute x6, starting transfers between devices, y_sum(): lax.ppermute(value, 'y', [(i, i ^ k) for i in range(4)]).astype(F32)  5.99 us
    ppermute x3, starting transfers between devices, shifted(): return lax.ppermute(value, 'head', [(i, (i + k) % 4) for i in range(4)])  4.83 us
    all_to_all x1, starting transfers between devices, z_sum(): got = lax.all_to_all(sent, 'z', 0, 0)  3.68 us
    ppermute x6, waiting for transfers between devices, y_sum(): lax.ppermute(value, 'y', [(i, i ^ k) for i in range(4)]).astype(F32)  2.62 us
    ppermute x8, waiting for transfers between devices, core_swap(): return lax.ppermute(value, 'core', [(0, 1), (1, 0)])  2.1 us
  transfers between devices with their start and end apart: 18, of which 5 were waited for; matrix products, arithmetic and copies ran while one was open for 0% of the time, Pallas kernels for 28%

profile of v5, /device:TPU:1, one launch (start us, length us, event | category | flops | bytes accessed | tf_op | source)
XLA Modules:
  0.0 79.2 jit_solution(10948531759193612948)
XLA Ops:
  0.6 0.1 pad_add_fusion.refs_0_.me
  0.7 0.0 copy-start.4
  0.7 0.0 copy-start.5
  0.7 6.1 %pool_pass.1 = (f32[40,128]{1,0:T(8,128)S(1)}, f32[40,128]{1,0:T(8,128)S(1)}, f32[128,512]{1,0:T(8,128)S(1)}, bf16[256,256]{1,0:T(8,128)(2,1)S(1)}, bf16[8192,25...) custom-call(s32[2]{0:T(128)S(1)} %pad_add_fusion.refs_0_.me, f32[2]{0:T(128)} %sharp.1, bf16[8192,256]{1,0:T(8,128)(2,1)} %refs_4_.1, ...), custom_call_target="tpu_custom_call" | custom-call | flops 8589934592 | bytes 8388608 | tf_op jit(solution)/shard_map/pool_pass/pallas_call | solution.py:366
  6.9 3.3 %collective-permute-start = (f32[40,128]{1,0:T(8,128)S(1)}, f32[40,128]{1,0:T(8,128)S(1)}, u32[]{:S(2)}, u32[]{:S(2)}) collective-permute-start(f32[40,128]{1,0:T(8,128)S(1)} %get-tuple-element.40), channel_id=1, source_target_pairs={{0,4},{4,0},{1,5},{5,1},{2,6},{6,2},{3,7},{7,3},{8,12},{12,8},{9,1... | collective-permute-start | bytes 61448 | tf_op jit(solution)/shard_map/ppermute | solution.py:510
  10.2 0.8 %collective-permute-done = f32[40,128]{1,0:T(8,128)S(1)} collective-permute-done((f32[40,128]{1,0:T(8,128)S(1)}, f32[40,128]{1,0:T(8,128)S(1)}, u32[]{:S(2)}, u32[]{:S(2)}) %collective-permute-start) | collective-permute-done | bytes 20512 | tf_op jit(solution)/shard_map/ppermute | solution.py:510
  11.1 1.2 %collective-permute-start.2 = (f32[40,128]{1,0:T(8,128)S(1)}, f32[40,128]{1,0:T(8,128)S(1)}, u32[]{:S(2)}, u32[]{:S(2)}) collective-permute-start(f32[40,128]{1,0:T(8,128)S(1)} %add.78), channel_id=1, source_target_pairs={{0,128},{64,192},{128,0},{192,64},{1,129},{65,193},{129,1},{193,65... | collective-permute-start | bytes 61448 | tf_op jit(solution)/shard_map/ppermute | solution.py:515
  12.2 0.8 collective-permute-start.3
  13.0 0.7 collective-permute-start.1
  13.7 1.5 %collective-permute-done.2 = f32[40,128]{1,0:T(8,128)S(1)} collective-permute-done((f32[40,128]{1,0:T(8,128)S(1)}, f32[40,128]{1,0:T(8,128)S(1)}, u32[]{:S(2)}, u32[]{:S(2)}) %collective-permute-start.2) | collective-permute-done | bytes 20512 | tf_op jit(solution)/shard_map/ppermute | solution.py:515
  15.2 1.1 %collective-permute-done.3 = f32[40,128]{1,0:T(8,128)S(1)} collective-permute-done((f32[40,128]{1,0:T(8,128)S(1)}, f32[40,128]{1,0:T(8,128)S(1)}, u32[]{:S(2)}, u32[]{:S(2)}) %collective-permute-start.3) | collective-permute-done | bytes 20512 | tf_op jit(solution)/shard_map/ppermute | solution.py:515
  16.3 0.0 collective-permute-done.1
  16.3 16.1 %all_to_all.10 = f32[8,40,128]{2,1,0:T(8,128)S(1)} all-to-all(f32[8,40,128]{2,1,0:T(8,128)S(1)} %broadcast_in_dim.4), channel_id=1, replica_groups=mesh['y'=4,'z'=8,'core'=2,'head'=4] {'z'}, dimensions={0} | all-to-all | bytes 327680 | tf_op jit(solution)/shard_map/all_to_all | solution.py:522
  32.5 1.5 %token_pass.1 = (bf16[144,256]{1,0:T(8,128)(2,1)S(1)}, f32[3,32,32]{2,1,0:T(8,128)S(1)}) custom-call(s32[2]{0:T(128)S(1)} %pad_add_fusion.refs_0_.me, f32[2]{0:T(128)S(1)} %copy-done.5, f32[40,128]{1,0:T(8,128)S(1)} %fusion.1.pay, f32[2,3,32,32]{3,2,1,0:T(8,128)S(1)} %copy-done, bf16[2,32,64]{2,1,0:T(8,128)(2,1)S(1)} %copy-done.4, ...), custom_call_target="tpu_custom_call" | custom-call | tf_op jit(solution)/shard_map/token_pass/pallas_call | solution.py:366
  34.0 3.2 %collective-permute-start.4 = (bf16[144,256]{1,0:T(8,128)(2,1)S(1)}, bf16[144,256]{1,0:T(8,128)(2,1)S(1)}, u32[]{:S(2)}, u32[]{:S(2)}) collective-permute-start(bf16[144,256]{1,0:T(8,128)(2,1)S(1)} %get-tuple-element.41.refs_1_), channel_id=1, source_target_pairs={{0,4},{4,0},{1,5},{5,1},{2,6},{6,2},{3,7},{7,3},{8,12},{12,8},{9,1... | collective-permute-start | bytes 221192 | tf_op jit(solution)/shard_map/ppermute | solution.py:510
  37.3 1.2 %collective-permute-start.5 = (bf16[144,256]{1,0:T(8,128)(2,1)S(1)}, bf16[144,256]{1,0:T(8,128)(2,1)S(1)}, u32[]{:S(2)}, u32[]{:S(2)}) collective-permute-start(bf16[144,256]{1,0:T(8,128)(2,1)S(1)} %get-tuple-element.41.refs_1_), channel_id=1, source_target_pairs={{0,1},{1,2},{2,3},{3,0},{4,5},{5,6},{6,7},{7,4},{8,9},{9,10},{10,1... | collective-permute-start | bytes 221192 | tf_op jit(solution)/shard_map/ppermute | solution.py:533
  38.5 2.5 %collective-permute-start.6 = (bf16[144,256]{1,0:T(8,128)(2,1)S(1)}, bf16[144,256]{1,0:T(8,128)(2,1)S(1)}, u32[]{:S(2)}, u32[]{:S(2)}) collective-permute-start(bf16[144,256]{1,0:T(8,128)(2,1)S(1)} %get-tuple-element.41.refs_1_), channel_id=1, source_target_pairs={{0,2},{1,3},{2,0},{3,1},{4,6},{5,7},{6,4},{7,5},{8,10},{9,11},{10,... | collective-permute-start | bytes 221192 | tf_op jit(solution)/shard_map/ppermute | solution.py:533
  40.9 1.2 %collective-permute-start.7 = (bf16[144,256]{1,0:T(8,128)(2,1)S(1)}, bf16[144,256]{1,0:T(8,128)(2,1)S(1)}, u32[]{:S(2)}, u32[]{:S(2)}) collective-permute-start(bf16[144,256]{1,0:T(8,128)(2,1)S(1)} %get-tuple-element.41.refs_1_), channel_id=1, source_target_pairs={{0,3},{1,0},{2,1},{3,2},{4,7},{5,4},{6,5},{7,6},{8,11},{9,8},{10,9... | collective-permute-start | bytes 221192 | tf_op jit(solution)/shard_map/ppermute | solution.py:533
  42.1 0.9 %collective-permute-start.8 = (f32[3,32,32]{2,1,0:T(8,128)S(1)}, f32[3,32,32]{2,1,0:T(8,128)S(1)}, u32[]{:S(2)}, u32[]{:S(2)}) collective-permute-start(f32[3,32,32]{2,1,0:T(8,128)S(1)} %get-tuple-element.48.attn_own), channel_id=1, source_target_pairs={{0,4},{4,0},{1,5},{5,1},{2,6},{6,2},{3,7},{7,3},{8,12},{12,8},{9,1... | collective-permute-start | bytes 36872 | tf_op jit(solution)/shard_map/ppermute | solution.py:510
  43.0 0.0 collective-permute-done.4.refs_2_.refs_5_
  43.0 5.9 %weight_pass.1 = (f32[104,256]{1,0:T(8,128)S(1)}, f32[104,256]{1,0:T(8,128)S(1)}) custom-call(s32[2]{0:T(128)S(1)} %pad_add_fusion.refs_0_.me, bf16[144,256]{1,0:T(8,128)(2,1)S(1)} %get-tuple-element.41.refs_1_, bf16[144,256]{1,0:T(8,128)(2,1)S(1)} %collective-permute-done.4.refs_2_.refs_5_, bf16[2,32,64]{2,1,0:T(8,128)(2,1)S(1)} %copy-done.4, ...), custom_call_target="tpu_custom_call" | custom-call | flops 8589934592 | bytes 8388608 | tf_op jit(solution)/shard_map/weight_pass/pallas_call | solution.py:366
  48.9 0.0 collective-permute-done.8.attn_other
  48.9 0.0 collective-permute-done.5.refs_2_
  48.9 0.0 collective-permute-done.6.refs_3_
  48.9 0.0 collective-permute-done.7.refs_4_
  48.9 0.1 collective-permute-start.9
  49.0 0.5 collective-permute-start.13
  49.5 0.3 collective-permute-start.14
  49.8 0.2 collective-permute-start.15
  50.0 0.3 collective-permute-done.9
  50.3 1.8 %collective-permute-start.12 = (bf16[104,256]{1,0:T(8,128)(2,1)S(1)}, bf16[104,256]{1,0:T(8,128)(2,1)S(1)}, u32[]{:S(2)}, u32[]{:S(2)}) collective-permute-start(bf16[104,256]{1,0:T(8,128)(2,1)S(1)} %add_convert_fusion.1), channel_id=1, source_target_pairs={{0,192},{64,128},{128,64},{192,0},{1,193},{65,129},{129,65},{193,1... | collective-permute-start | bytes 159752 | tf_op jit(solution)/shard_map/ppermute | solution.py:515
  52.2 0.0 collective-permute-start.11
  52.2 0.0 collective-permute-done.13.refs_6_
  52.2 1.5 %collective-permute-start.10 = (bf16[104,256]{1,0:T(8,128)(2,1)S(1)}, bf16[104,256]{1,0:T(8,128)(2,1)S(1)}, u32[]{:S(2)}, u32[]{:S(2)}) collective-permute-start(bf16[104,256]{1,0:T(8,128)(2,1)S(1)} %add_convert_fusion.1), channel_id=1, source_target_pairs={{0,64},{64,0},{128,192},{192,128},{1,65},{65,1},{129,193},{193,129... | collective-permute-start | bytes 159752 | tf_op jit(solution)/shard_map/ppermute | solution.py:515
  53.7 0.0 collective-permute-done.14.refs_7_
  53.7 0.0 collective-permute-done.15.refs_8_
  53.7 2.9 %early_pass.1 = (bf16[512,256]{1,0:T(8,128)(2,1)S(1)}, bf16[512,512]{1,0:T(8,128)(2,1)S(1)}, f32[512,128]{1,0:T(8,128)S(1)}, bf16[64,1024]{1,0:T(8,128)(2,1)S(1)}, bf16[64,8192]{1,0:T(8,128)(2,1)}) custom-call(s32[2]{0:T(128)S(1)} %pad_add_fusion.refs_0_.me, bf16[144,256]{1,0:T(8,128)(2,1)S(1)} %get-tuple-element.41.refs_1_, ...), custom_call_target="tpu_custom_call" | custom-call | flops 4294967296 | bytes 8388608 | tf_op jit(solution)/shard_map/early_pass/pallas_call | solution.py:366
  56.6 0.0 collective-permute-done.12
  56.6 0.0 collective-permute-done.11
  56.7 0.0 collective-permute-done.10
  56.7 0.8 %broadcast_in_dim.5 = bf16[8,104,256]{2,1,0:T(8,128)(2,1)} broadcast(bf16[104,256]{1,0:T(8,128)(2,1)S(1)} %add_convert_fusion), dimensions={1,2} | broadcast | bytes 479232 | tf_op jit(solution)/shard_map/broadcast_in_dim | solution.py:521
  57.5 3.7 %all-to-all-start.1 = ((bf16[8,104,256]{2,1,0:T(8,128)(2,1)}), bf16[8,104,256]{2,1,0:T(8,128)(2,1)S(1)}, u32[]{:S(2)}, u32[]{:S(2)}) async-start(bf16[8,104,256]{2,1,0:T(8,128)(2,1)} %broadcast_in_dim.5), calls=%async_computation.1 | async-start | bytes 851968 | tf_op jit(solution)/shard_map/all_to_all | solution.py:522
  61.2 13.6 %late_pass.1 = bf16[64,8192]{1,0:T(8,128)(2,1)} custom-call(bf16[512,256]{1,0:T(8,128)(2,1)S(1)} %get-tuple-element.59.refs_0_, bf16[512,512]{1,0:T(8,128)(2,1)S(1)} %get-tuple-element.60.refs_1_, f32[512,128]{1,0:T(8,128)S(1)} %get-tuple-element.61.refs_2_, bf16[64,1024]{1,0:T(8,128)(2,1)S(1)} %get-tuple-element.62.refs_3_, ...), custom_call_target="tpu_custom_call", output_to_operand_aliasing={{}: (6, {})} | custom-call | flops 8589934592 | bytes 8388608 | tf_op jit(solution)/shard_map/late_pass/pallas_call | solution.py:366
  74.8 0.1 convert_element_type.27
  74.8 0.1 fusion.half
  74.9 2.1 %collective-permute-start.16 = (f32[104,256]{1,0:T(8,128)S(1)}, f32[104,256]{1,0:T(8,128)S(1)}, u32[]{:S(2)}, u32[]{:S(2)}) collective-permute-start(f32[104,256]{1,0:T(8,128)S(1)} %fusion.half), channel_id=1, source_target_pairs={{0,4},{4,0},{1,5},{5,1},{2,6},{6,2},{3,7},{7,3},{8,12},{12,8},{9,1... | collective-permute-start | bytes 319496 | tf_op jit(solution)/shard_map/ppermute | solution.py:510
  77.0 1.0 %collective-permute-done.16.other = f32[104,256]{1,0:T(8,128)S(1)} collective-permute-done((f32[104,256]{1,0:T(8,128)S(1)}, f32[104,256]{1,0:T(8,128)S(1)}, u32[]{:S(2)}, u32[]{:S(2)}) %collective-permute-start.16) | collective-permute-done | bytes 106528 | tf_op jit(solution)/shard_map/ppermute | solution.py:510
  77.9 1.3 %final_pass.1 = (f32[64,256]{1,0:T(8,128)}, f32[64,256]{1,0:T(8,128)}, f32[64,256]{1,0:T(8,128)}, f32[2,32,64]{2,1,0:T(8,128)}, f32[2,3,32,32]{3,2,1,0:T(8,128)}) custom-call(s32[2]{0:T(128)S(1)} %pad_add_fusion.refs_0_.me, f32[104,256]{1,0:T(8,128)S(1)} %fusion.half, f32[104,256]{1,0:T(8,128)S(1)} %collective-permute-done.16.other, ...), custom_call_target="tpu_custom_call" | custom-call | tf_op jit(solution)/shard_map/final_pass/pallas_call | solution.py:366
  (17 shorter events, 0.1 us)
Async XLA Ops:
  0.7 31.8 %copy-start = (f32[2,3,32,32]{3,2,1,0:T(8,128)S(1)}, f32[2,3,32,32]{3,2,1,0:T(8,128)}, u32[]{:S(2)}) copy-start(f32[2,3,32,32]{3,2,1,0:T(8,128)} %qkv.1) | copy-start | bytes 73732
  0.7 31.8 %copy-start.1 = (bf16[256,64]{0,1:T(8,128)(2,1)S(1)}, bf16[256,64]{0,1:T(8,128)(2,1)}, u32[]{:S(2)}) copy-start(bf16[256,64]{0,1:T(8,128)(2,1)} %param.10) | copy-start | bytes 98308
  0.7 31.8 %copy-start.2 = (bf16[64,256]{1,0:T(8,128)(2,1)S(1)}, bf16[64,256]{1,0:T(8,128)(2,1)}, u32[]{:S(2)}) copy-start(bf16[64,256]{1,0:T(8,128)(2,1)} %wout.1) | copy-start | bytes 98308
  0.7 31.8 %copy-start.3 = (bf16[256,64]{0,1:T(8,128)(2,1)S(1)}, bf16[256,64]{0,1:T(8,128)(2,1)}, u32[]{:S(2)}) copy-start(bf16[256,64]{0,1:T(8,128)(2,1)} %param.11) | copy-start | bytes 98308
  0.7 31.8 %copy-start.4 = (bf16[2,32,64]{2,1,0:T(8,128)(2,1)S(1)}, bf16[2,32,64]{2,1,0:T(8,128)(2,1)}, u32[]{:S(2)}) copy-start(bf16[2,32,64]{2,1,0:T(8,128)(2,1)} %refs_3_.3) | copy-start | bytes 24580
  0.7 31.8 %copy-start.5 = (f32[2]{0:T(128)S(1)}, f32[2]{0:T(128)}, u32[]{:S(2)}) copy-start(f32[2]{0:T(128)} %sharp.1) | copy-start | bytes 28
  6.9 4.2 %collective-permute-start = (f32[40,128]{1,0:T(8,128)S(1)}, f32[40,128]{1,0:T(8,128)S(1)}, u32[]{:S(2)}, u32[]{:S(2)}) collective-permute-start(f32[40,128]{1,0:T(8,128)S(1)} %get-tuple-element.40), channel_id=1, source_target_pairs={{0,4},{4,0},{1,5},{5,1},{2,6},{6,2},{3,7},{7,3},{8,12},{12,8},{9,1... | collective-permute-start | bytes 61448 | tf_op jit(solution)/shard_map/ppermute | solution.py:510
  11.1 4.1 %collective-permute-start.2 = (f32[40,128]{1,0:T(8,128)S(1)}, f32[40,128]{1,0:T(8,128)S(1)}, u32[]{:S(2)}, u32[]{:S(2)}) collective-permute-start(f32[40,128]{1,0:T(8,128)S(1)} %add.78), channel_id=1, source_target_pairs={{0,128},{64,192},{128,0},{192,64},{1,129},{65,193},{129,1},{193,65... | collective-permute-start | bytes 61448 | tf_op jit(solution)/shard_map/ppermute | solution.py:515
  12.2 4.1 %collective-permute-start.3 = (f32[40,128]{1,0:T(8,128)S(1)}, f32[40,128]{1,0:T(8,128)S(1)}, u32[]{:S(2)}, u32[]{:S(2)}) collective-permute-start(f32[40,128]{1,0:T(8,128)S(1)} %add.78), channel_id=1, source_target_pairs={{0,192},{64,128},{128,64},{192,0},{1,193},{65,129},{129,65},{193,1... | collective-permute-start | bytes 61448 | tf_op jit(solution)/shard_map/ppermute | solution.py:515
  13.0 3.3 %collective-permute-start.1 = (f32[40,128]{1,0:T(8,128)S(1)}, f32[40,128]{1,0:T(8,128)S(1)}, u32[]{:S(2)}, u32[]{:S(2)}) collective-permute-start(f32[40,128]{1,0:T(8,128)S(1)} %add.78), channel_id=1, source_target_pairs={{0,64},{64,0},{128,192},{192,128},{1,65},{65,1},{129,193},{193,129... | collective-permute-start | bytes 61448 | tf_op jit(solution)/shard_map/ppermute | solution.py:515
  34.0 9.0 %collective-permute-start.4 = (bf16[144,256]{1,0:T(8,128)(2,1)S(1)}, bf16[144,256]{1,0:T(8,128)(2,1)S(1)}, u32[]{:S(2)}, u32[]{:S(2)}) collective-permute-start(bf16[144,256]{1,0:T(8,128)(2,1)S(1)} %get-tuple-element.41.refs_1_), channel_id=1, source_target_pairs={{0,4},{4,0},{1,5},{5,1},{2,6},{6,2},{3,7},{7,3},{8,12},{12,8},{9,1... | collective-permute-start | bytes 221192 | tf_op jit(solution)/shard_map/ppermute | solution.py:510
  37.3 11.6 %collective-permute-start.5 = (bf16[144,256]{1,0:T(8,128)(2,1)S(1)}, bf16[144,256]{1,0:T(8,128)(2,1)S(1)}, u32[]{:S(2)}, u32[]{:S(2)}) collective-permute-start(bf16[144,256]{1,0:T(8,128)(2,1)S(1)} %get-tuple-element.41.refs_1_), channel_id=1, source_target_pairs={{0,1},{1,2},{2,3},{3,0},{4,5},{5,6},{6,7},{7,4},{8,9},{9,10},{10,1... | collective-permute-start | bytes 221192 | tf_op jit(solution)/shard_map/ppermute | solution.py:533
  38.5 10.4 %collective-permute-start.6 = (bf16[144,256]{1,0:T(8,128)(2,1)S(1)}, bf16[144,256]{1,0:T(8,128)(2,1)S(1)}, u32[]{:S(2)}, u32[]{:S(2)}) collective-permute-start(bf16[144,256]{1,0:T(8,128)(2,1)S(1)} %get-tuple-element.41.refs_1_), channel_id=1, source_target_pairs={{0,2},{1,3},{2,0},{3,1},{4,6},{5,7},{6,4},{7,5},{8,10},{9,11},{10,... | collective-permute-start | bytes 221192 | tf_op jit(solution)/shard_map/ppermute | solution.py:533
  40.9 8.0 %collective-permute-start.7 = (bf16[144,256]{1,0:T(8,128)(2,1)S(1)}, bf16[144,256]{1,0:T(8,128)(2,1)S(1)}, u32[]{:S(2)}, u32[]{:S(2)}) collective-permute-start(bf16[144,256]{1,0:T(8,128)(2,1)S(1)} %get-tuple-element.41.refs_1_), channel_id=1, source_target_pairs={{0,3},{1,0},{2,1},{3,2},{4,7},{5,4},{6,5},{7,6},{8,11},{9,8},{10,9... | collective-permute-start | bytes 221192 | tf_op jit(solution)/shard_map/ppermute | solution.py:533
  42.1 6.8 %collective-permute-start.8 = (f32[3,32,32]{2,1,0:T(8,128)S(1)}, f32[3,32,32]{2,1,0:T(8,128)S(1)}, u32[]{:S(2)}, u32[]{:S(2)}) collective-permute-start(f32[3,32,32]{2,1,0:T(8,128)S(1)} %get-tuple-element.48.attn_own), channel_id=1, source_target_pairs={{0,4},{4,0},{1,5},{5,1},{2,6},{6,2},{3,7},{7,3},{8,12},{12,8},{9,1... | collective-permute-start | bytes 36872 | tf_op jit(solution)/shard_map/ppermute | solution.py:510
  48.9 1.4 %collective-permute-start.9 = (f32[104,256]{1,0:T(8,128)S(1)}, f32[104,256]{1,0:T(8,128)S(1)}, u32[]{:S(2)}, u32[]{:S(2)}) collective-permute-start(f32[104,256]{1,0:T(8,128)S(1)} %get-tuple-element.50), channel_id=1, source_target_pairs={{0,4},{4,0},{1,5},{5,1},{2,6},{6,2},{3,7},{7,3},{8,12},{12,8},{9,1... | collective-permute-start | bytes 319496 | tf_op jit(solution)/shard_map/ppermute | solution.py:510
  49.0 3.1 %collective-permute-start.13 = (bf16[144,256]{1,0:T(8,128)(2,1)S(1)}, bf16[144,256]{1,0:T(8,128)(2,1)S(1)}, u32[]{:S(2)}, u32[]{:S(2)}) collective-permute-start(bf16[144,256]{1,0:T(8,128)(2,1)S(1)} %collective-permute-done.5.refs_2_), channel_id=1, source_target_pairs={{0,4},{4,0},{1,5},{5,1},{2,6},{6,2},{3,7},{7,3},{8,12},{12,8},{9,1... | collective-permute-start | bytes 221192 | tf_op jit(solution)/shard_map/ppermute | solution.py:510
  49.5 4.2 %collective-permute-start.14 = (bf16[144,256]{1,0:T(8,128)(2,1)S(1)}, bf16[144,256]{1,0:T(8,128)(2,1)S(1)}, u32[]{:S(2)}, u32[]{:S(2)}) collective-permute-start(bf16[144,256]{1,0:T(8,128)(2,1)S(1)} %collective-permute-done.6.refs_3_), channel_id=1, source_target_pairs={{0,4},{4,0},{1,5},{5,1},{2,6},{6,2},{3,7},{7,3},{8,12},{12,8},{9,1... | collective-permute-start | bytes 221192 | tf_op jit(solution)/shard_map/ppermute | solution.py:510
  49.8 3.9 %collective-permute-start.15 = (bf16[144,256]{1,0:T(8,128)(2,1)S(1)}, bf16[144,256]{1,0:T(8,128)(2,1)S(1)}, u32[]{:S(2)}, u32[]{:S(2)}) collective-permute-start(bf16[144,256]{1,0:T(8,128)(2,1)S(1)} %collective-permute-done.7.refs_4_), channel_id=1, source_target_pairs={{0,4},{4,0},{1,5},{5,1},{2,6},{6,2},{3,7},{7,3},{8,12},{12,8},{9,1... | collective-permute-start | bytes 221192 | tf_op jit(solution)/shard_map/ppermute | solution.py:510
  50.3 6.3 %collective-permute-start.12 = (bf16[104,256]{1,0:T(8,128)(2,1)S(1)}, bf16[104,256]{1,0:T(8,128)(2,1)S(1)}, u32[]{:S(2)}, u32[]{:S(2)}) collective-permute-start(bf16[104,256]{1,0:T(8,128)(2,1)S(1)} %add_convert_fusion.1), channel_id=1, source_target_pairs={{0,192},{64,128},{128,64},{192,0},{1,193},{65,129},{129,65},{193,1... | collective-permute-start | bytes 159752 | tf_op jit(solution)/shard_map/ppermute | solution.py:515
  52.2 4.5 %collective-permute-start.11 = (bf16[104,256]{1,0:T(8,128)(2,1)S(1)}, bf16[104,256]{1,0:T(8,128)(2,1)S(1)}, u32[]{:S(2)}, u32[]{:S(2)}) collective-permute-start(bf16[104,256]{1,0:T(8,128)(2,1)S(1)} %add_convert_fusion.1), channel_id=1, source_target_pairs={{0,128},{64,192},{128,0},{192,64},{1,129},{65,193},{129,1},{193,65... | collective-permute-start | bytes 159752 | tf_op jit(solution)/shard_map/ppermute | solution.py:515
  52.2 4.5 %collective-permute-start.10 = (bf16[104,256]{1,0:T(8,128)(2,1)S(1)}, bf16[104,256]{1,0:T(8,128)(2,1)S(1)}, u32[]{:S(2)}, u32[]{:S(2)}) collective-permute-start(bf16[104,256]{1,0:T(8,128)(2,1)S(1)} %add_convert_fusion.1), channel_id=1, source_target_pairs={{0,64},{64,0},{128,192},{192,128},{1,65},{65,1},{129,193},{193,129... | collective-permute-start | bytes 159752 | tf_op jit(solution)/shard_map/ppermute | solution.py:515
  57.5 17.3 %all-to-all-start.1 = ((bf16[8,104,256]{2,1,0:T(8,128)(2,1)}), bf16[8,104,256]{2,1,0:T(8,128)(2,1)S(1)}, u32[]{:S(2)}, u32[]{:S(2)}) async-start(bf16[8,104,256]{2,1,0:T(8,128)(2,1)} %broadcast_in_dim.5), calls=%async_computation.1 | async-start | bytes 851968 | tf_op jit(solution)/shard_map/all_to_all | solution.py:522
  74.9 3.0 %collective-permute-start.16 = (f32[104,256]{1,0:T(8,128)S(1)}, f32[104,256]{1,0:T(8,128)S(1)}, u32[]{:S(2)}, u32[]{:S(2)}) collective-permute-start(f32[104,256]{1,0:T(8,128)S(1)} %fusion.half), channel_id=1, source_target_pairs={{0,4},{4,0},{1,5},{5,1},{2,6},{6,2},{3,7},{7,3},{8,12},{12,8},{9,1... | collective-permute-start | bytes 319496 | tf_op jit(solution)/shard_map/ppermute | solution.py:510
